TPU v7x, 32 devices: a whole 2x2x4 slice. The times are simulated.
32 devices in a mesh: req: 4 (over x, core), mlp: 8 (over z, y).
Axes of the slice: x: 2, y: 2, z: 4, core: 2. Of those that a mesh axis runs over, the one named last changes fastest.
Arguments:
- residual_in: bfloat16 [4096, 1792], P(('req', 'mlp')), may hold values from -6 to 6
- query_in: bfloat16 [4096, 256], P(('req', 'mlp')), may hold values from -4 to 4
- key_in: bfloat16 [4096, 256], P(('req', 'mlp')), may hold values from -4 to 4
- values_in: bfloat16 [4096, 1792], P(('req', 'mlp')), may hold values from -6 to 6
- conv_weight: float32 [3, 1792], replicated, may hold values from -0.8 to 0.8
- prefix_state: float32 [4, 16, 273, 112], P('req', 'mlp'), may hold values from -896 to 896
- prefix_norm: float32 [4, 16, 273], P('req', 'mlp'), as said below
- prefix_owner: int32 [4], replicated, may hold values from 0 to 3, each once
- lengths: int32 [4, 4], P('req'), may hold values from 1 to 512, 1024 in all within a row
- old_flags: int32 [4, 4], P('req'), may hold values 0 or 1
- out_weight: bfloat16 [1792, 1792], replicated, may hold values from -0.125 to 0.125
- mlp_gain: float32 [1792], replicated, may hold values from 0.5 to 1.5
- gate_weight: bfloat16 [1792, 4864], P(None, 'mlp'), may hold values from -0.125 to 0.125
- up_weight: bfloat16 [1792, 4864], P(None, 'mlp'), may hold values from -0.125 to 0.125
- down_weight: bfloat16 [4864, 1792], P('mlp'), may hold values from -0.078125 to 0.078125
- next_gain: float32 [1792], replicated, may hold values from 0.5 to 1.5
- qkv_weight: bfloat16 [1792, 2304], replicated, may hold values from -0.125 to 0.125
Outputs:
- hidden_out: bfloat16 [4096, 1792], P(('req', 'mlp'))
- next_qkv: bfloat16 [4096, 2304], P(('req', 'mlp'))
Inputs may be any that keep to these rules, and one draw needn't show every extreme that they name: `prefix_owner`: each slot holds exactly one group's cached state. `lengths`: a group's requests follow one another in order and fill its 1024 tokens; the longest of a group has exactly half of 1024. `prefix_norm`: a head's cached normalizer is a sum of feature maps of earlier keys.
All inputs are finite; a program needn't handle non-finite values. No bound on the sum of `old_flags` on one device may be relied on, other than what follows from the above.
Results may differ from a plain program's by a relative error of at most 0.024.
Values may be sent and summed in bfloat16 or wider, within the bound.
No kernel may reach another device: no remote copies, remote signals or barrier semaphores. Data moves between devices by JAX's collectives and lax.ppermute only.
A program may use at most 192 MiB of HBM per device.

v0:
```python
import math

import jax
import jax.numpy as jnp
from jax import lax
from jax.sharding import PartitionSpec as P

EPSILON = 1e-05
HIGHEST = lax.Precision.HIGHEST


def shifted(block, axis, distance):
    devices = range(lax.axis_size(axis))
    route = [(i - distance, i) for i in devices if i - distance in devices]
    return lax.ppermute(block, axis, route)


def prefix(value, axis, combine, identity):
    count, position = (lax.axis_size(axis), lax.axis_index(axis))
    everything = jax.tree.map(
        lambda part, kind: lax.all_gather(part.astype(kind), axis),
        value,
        (jnp.bfloat16, jnp.bfloat16, jnp.bfloat16),
    )
    start = jax.tree.map(
        lambda part, zero: jnp.broadcast_to(jnp.asarray(zero, part.dtype), part.shape),
        value,
        identity,
    )

    def step(k, before):
        reached = k < position
        new = combine(
            before, jax.tree.map(lambda part, own: part[k].astype(own.dtype), everything, value)
        )
        return jax.tree.map(lambda a, b: jnp.where(reached, a, b), new, before)

    return lax.fori_loop(0, count, step, start)


def feature_map(entries):
    feat_dim = entries.shape[-1]
    leading = entries.shape[:-1]
    squares = (entries[..., :, None] * entries[..., None, :]).reshape(
        leading + (feat_dim * feat_dim,)
    )
    constant = jnp.ones(leading + (1,), jnp.float32)
    return jnp.concatenate(
        [constant, entries * feat_dim ** (-0.25), squares / (math.sqrt(2.0) * math.sqrt(feat_dim))],
        axis=-1,
    )


def request_of(lengths, positions):
    boundary = jnp.cumsum(lengths)[:-1]
    which = jnp.sum((positions[:, None] >= boundary[None, :]).astype(jnp.int32), axis=1)
    return jnp.where(positions < 0, jnp.int32(-1), which)


def convolve(entries, weights, requests, earlier_rows, earlier_requests):
    tap_count = weights.shape[0]
    row_count = entries.shape[0]
    extended = jnp.concatenate([earlier_rows, entries], axis=0).astype(jnp.float32)
    request_rows = jnp.concatenate([earlier_requests, requests], axis=0)
    summed = jnp.zeros(entries.shape, jnp.float32)
    for shift_by in range(tap_count):
        first_row = tap_count - 1 - shift_by
        earlier = extended[first_row : first_row + row_count]
        matching = (request_rows[first_row : first_row + row_count] == requests)[:, None]
        summed = summed + weights[shift_by][None, :] * jnp.where(matching, earlier, 0.0)
    return summed.astype(jnp.bfloat16)


def block_output(
    feat_query,
    feat_key,
    entries,
    requests,
    before,
    token_flags,
    carry_state,
    carry_norm,
    prefix_state,
    prefix_norm,
):
    row_count = requests.shape[0]
    scores = jnp.einsum("bhf,chf->hbc", feat_query, feat_key, preferred_element_type=jnp.float32)
    row_index = jnp.arange(row_count)
    visible = (row_index[:, None] >= row_index[None, :]) & (requests[:, None] == requests[None, :])
    scores = jnp.where(visible[None], scores, 0.0)
    normalizer = jnp.transpose(jnp.sum(scores, axis=2))
    numerator = jnp.einsum(
        "hbc,che->bhe", scores.astype(jnp.bfloat16), entries, preferred_element_type=jnp.float32
    )
    continues = (requests == before).astype(jnp.float32)
    query_wide = feat_query.astype(jnp.float32)
    numerator = numerator + token_flags[:, None, None] * jnp.einsum(
        "bhf,hfe->bhe", query_wide, prefix_state, precision=HIGHEST
    )
    numerator = numerator + continues[:, None, None] * jnp.einsum(
        "bhf,hfe->bhe", query_wide, carry_state, precision=HIGHEST
    )
    normalizer = normalizer + token_flags[:, None] * jnp.einsum(
        "bhf,hf->bh", query_wide, prefix_norm, precision=HIGHEST
    )
    normalizer = normalizer + continues[:, None] * jnp.einsum(
        "bhf,hf->bh", query_wide, carry_norm, precision=HIGHEST
    )
    return (numerator / normalizer[:, :, None]).astype(jnp.bfloat16)


def block_state(feat_key, entries, requests, before):
    in_last = (requests == requests[-1]).astype(jnp.bfloat16)
    keys_last = feat_key * in_last[:, None, None]
    state = jnp.einsum("bhf,bhe->hfe", keys_last, entries, preferred_element_type=jnp.float32)
    norm_sum = jnp.sum(keys_last.astype(jnp.float32), axis=0)
    started = (requests[-1] != before).astype(jnp.float32)
    return (state, norm_sum, started)


def link_blocks(earlier, later):
    keeping = 1.0 - later[2]
    return (
        later[0] + keeping * earlier[0],
        later[1] + keeping * earlier[1],
        jnp.maximum(earlier[2], later[2]),
    )


def flag_lookup(requests, request_ids, flag_row):
    matches = requests[:, None] == request_ids[None, :]
    return jnp.sum(jnp.where(matches, flag_row[None, :], 0.0), axis=1)


def rms_scale(entries, gain):
    return entries * lax.rsqrt(jnp.mean(entries * entries, axis=-1, keepdims=True) + EPSILON) * gain


def shards(
    residual_in,
    query_in,
    key_in,
    values_in,
    conv_weight,
    prefix_state,
    prefix_norm,
    prefix_owner,
    lengths,
    old_flags,
    out_weight,
    mlp_gain,
    gate_weight,
    up_weight,
    down_weight,
    next_gain,
    qkv_weight,
):
    local_rows = residual_in.shape[0]
    mlp_count = lax.axis_size("mlp")
    group_id = lax.axis_index("req")
    column_id = lax.axis_index("mlp")
    heads_local = prefix_state.shape[1]
    head_count = heads_local * mlp_count
    head_width = values_in.shape[1] // head_count
    feat_dim = query_in.shape[1] // head_count
    taps_count = conv_weight.shape[0]
    slot_state, slot_norm = (
        lax.all_gather(prefix_state.astype(jnp.bfloat16), "req", axis=0, tiled=True).astype(
            prefix_state.dtype
        ),
        lax.all_gather(prefix_norm.astype(jnp.bfloat16), "req", axis=0, tiled=True).astype(
            prefix_norm.dtype
        ),
    )
    owner_slot = prefix_owner[group_id]
    own_state = lax.dynamic_index_in_dim(slot_state, owner_slot, 0, keepdims=False)
    own_norm = lax.dynamic_index_in_dim(slot_norm, owner_slot, 0, keepdims=False)
    flag_row = old_flags[0].astype(jnp.float32)
    request_ids = jnp.arange(flag_row.shape[0], dtype=jnp.int32)
    all_state, all_norm = (
        lax.all_gather(own_state.astype(jnp.bfloat16), "mlp", axis=0, tiled=True).astype(
            own_state.dtype
        ),
        lax.all_gather(own_norm.astype(jnp.bfloat16), "mlp", axis=0, tiled=True).astype(
            own_norm.dtype
        ),
    )
    positions = column_id * local_rows + jnp.arange(local_rows, dtype=jnp.int32)
    requests = request_of(lengths[0], positions)
    rim_rows = shifted(values_in[local_rows - (taps_count - 1) :], "mlp", 1)
    earlier_positions = (
        column_id * local_rows - (taps_count - 1) + jnp.arange(taps_count - 1, dtype=jnp.int32)
    )
    conv_values = convolve(
        values_in, conv_weight, requests, rim_rows, request_of(lengths[0], earlier_positions)
    )
    before = request_of(lengths[0], jnp.reshape(column_id * local_rows - 1, (1,)))[0]
    token_flags = flag_lookup(requests, request_ids, flag_row)
    feat_query = feature_map(
        query_in.reshape(local_rows, head_count, feat_dim).astype(jnp.float32)
    ).astype(jnp.bfloat16)
    feat_key = feature_map(
        key_in.reshape(local_rows, head_count, feat_dim).astype(jnp.float32)
    ).astype(jnp.bfloat16)
    value_heads = conv_values.reshape(local_rows, head_count, head_width)
    state, norm_sum, started = block_state(feat_key, value_heads, requests, before)
    carry_state, carry_norm, _ = prefix(
        (state, norm_sum, started),
        "mlp",
        link_blocks,
        (jnp.zeros_like(state), jnp.zeros_like(norm_sum), jnp.zeros((), jnp.float32)),
    )
    attended = block_output(
        feat_query,
        feat_key,
        value_heads,
        requests,
        before,
        token_flags,
        carry_state,
        carry_norm,
        all_state,
        all_norm,
    ).reshape(local_rows, head_count * head_width)
    projected = jnp.dot(attended, out_weight, preferred_element_type=jnp.float32)
    first_sum = (residual_in.astype(jnp.float32) + projected).astype(jnp.bfloat16)
    normed = rms_scale(first_sum.astype(jnp.float32), mlp_gain).astype(jnp.bfloat16)
    row_piece = lax.all_gather(normed, "mlp", axis=0, tiled=True)
    gate_rows = jnp.dot(row_piece, gate_weight, preferred_element_type=jnp.float32)
    up_rows = jnp.dot(row_piece, up_weight, preferred_element_type=jnp.float32)
    hidden = (jax.nn.silu(gate_rows) * up_rows).astype(jnp.bfloat16)
    mlp_output = lax.psum_scatter(
        jnp.dot(hidden, down_weight, preferred_element_type=jnp.float32).astype(jnp.bfloat16),
        "mlp",
        scatter_dimension=0,
        tiled=True,
    ).astype(jnp.float32)
    second_sum = (first_sum.astype(jnp.float32) + mlp_output).astype(jnp.bfloat16)
    normed_next = rms_scale(second_sum.astype(jnp.float32), next_gain).astype(jnp.bfloat16)
    projections = jnp.dot(normed_next, qkv_weight, preferred_element_type=jnp.float32).astype(
        jnp.bfloat16
    )
    return (second_sum, projections)


def solution(mesh):
    placed = (
        P(("req", "mlp"), None),
        P(("req", "mlp"), None),
        P(("req", "mlp"), None),
        P(("req", "mlp"), None),
        P(),
        P("req", "mlp", None, None),
        P("req", "mlp", None),
        P(),
        P("req", None),
        P("req", None),
        P(),
        P(),
        P(None, "mlp"),
        P(None, "mlp"),
        P("mlp", None),
        P(),
        P(),
    )
    return jax.shard_map(
        shards,
        mesh=mesh,
        in_specs=placed,
        out_specs=(P(("req", "mlp"), None), P(("req", "mlp"), None)),
        check_vma=False,
    )
```

profile of v0, /device:TPU:0, one launch (start us, length us, event | category | flops | bytes accessed | tf_op | source)
XLA Modules:
  0.0 418.0 jit_solution(5588682013483522918)
XLA Ops:
  7.2 0.9 slice.38
  8.1 1.0 copy.49
  9.1 5.6 %collective-permute-start = (bf16[2,1792]{0,1:T(8,128)(2,1)}, bf16[2,1792]{0,1:T(8,128)(2,1)}, u32[]{:S(2)}, u32[]{:S(2)}) collective-permute-start(bf16[2,1792]{0,1:T(8,128)(2,1)} %copy.49), channel_id=1, source_target_pairs={{0,1},{1,2},{2,3},{3,4},{4,5},{5,6},{6,7},{8,9},{9,10},{10,11},{11... | collective-permute-start | bytes 21512 | tf_op jit(solution)/shard_map/ppermute | solution.py:15
  14.8 0.9 copy.52
  16.1 0.8 reduce-window.4
  16.9 0.6 slice_bitcast_fusion
  18.5 0.6 compare_convert_fusion.1
  19.1 0.6 slice.47
  19.7 0.7 slice_compare_fusion.1
  20.4 0.9 slice_reduce_fusion.2
  21.3 2.0 copy.50
  23.3 0.8 collective-permute-done
  24.1 1.5 maximum_convert_fusion
  25.6 1.4 fusion.16
  27.0 0.8 copy-done.3
  27.8 0.8 convolution_convert_fusion.2
  28.7 1.1 copy.55
  30.5 0.6 dynamic-slice
  31.1 0.7 dynamic-update-slice
  31.9 23.6 %all-reduce = bf16[8]{0:T(256)(128)(2,1)} all-reduce(bf16[8]{0:T(256)(128)(2,1)S(1)} %dynamic-update-slice), channel_id=1, replica_groups=mesh['req'=4,'mlp'=8] {'mlp'}, use_global_device_ids=true, to_apply=%add | all-reduce | flops 8 | bytes 32
  58.1 5.2 %all_gather.41 = bf16[4,2,273]{2,1,0:T(2,128)(2,1)S(1)} all-gather(bf16[1,2,273]{2,1,0:T(2,128)(2,1)S(1)} %convert_element_type.203), channel_id=1, replica_groups=mesh['req'=4,'mlp'=8] {'req'}, dimensions={0}, use_global_device_ids=true | all-gather | bytes 5460 | tf_op jit(solution)/shard_map/all_gather | solution.py:171
  63.3 1.1 convert_element_type.193
  64.3 7.4 %all_gather.33 = bf16[4,2,273,112]{3,1,2,0:T(2,128)(2,1)S(1)} all-gather(bf16[1,2,273,112]{3,1,2,0:T(2,128)(2,1)S(1)} %convert_element_type.193), channel_id=1, replica_groups=mesh['req'=4,'mlp'=8] {'req'}, dimensions={0}, use_global_device_ids=true | all-gather | bytes 611520 | tf_op jit(solution)/shard_map/all_gather | solution.py:168
  71.9 30.7 %all-gather.3 = bf16[1,16,273]{2,0,1:T(2,128)(2,1)S(1)} all-gather(bf16[1,2,273]{2,0,1:T(2,128)(2,1)S(1)} %copy.57), channel_id=5, replica_groups=mesh['req'=4,'mlp'=8] {'mlp'}, dimensions={1}, use_global_device_ids=true | all-gather | bytes 9828 | tf_op jit(solution)/shard_map/all_gather | solution.py:184
  102.6 1.0 multiply_reduce_fusion
  103.6 32.7 %all-gather.2 = bf16[128,273]{1,0:T(8,128)(2,1)S(1)} all-gather(bf16[16,273]{1,0:T(8,128)(2,1)S(1)} %multiply_reduce_fusion), channel_id=4, replica_groups=mesh['req'=4,'mlp'=8] {'mlp'}, dimensions={0}, use_global_device_ids=true | all-gather | bytes 78624 | tf_op jit(solution)/shard_map/all_gather | solution.py:21
  136.3 0.7 convert_bitcast_fusion
  138.0 1.3 fusion.33
  139.3 42.0 %all-gather = bf16[1,16,273,112]{3,2,0,1:T(8,128)(2,1)S(1)} all-gather(bf16[1,2,273,112]{3,2,0,1:T(8,128)(2,1)S(1)} %copy.54), channel_id=2, replica_groups=mesh['req'=4,'mlp'=8] {'mlp'}, dimensions={1}, use_global_device_ids=true | all-gather | bytes 1100736 | tf_op jit(solution)/shard_map/all_gather | solution.py:181
  181.7 1.9 fusion.7
  183.6 47.9 %while.16 = (s32[]{:T(128)}, f32[16,273,112]{2,1,0:T(8,128)}, f32[16,273]{1,0:T(8,128)S(1)}, s32[]{:T(128)}, bf16[8,16,273,112]{3,1,0,2:T(8,128)(2,1)}, /*index=...) while((s32[]{:T(128)}, f32[16,273,112]{2,1,0:T(8,128)}, ...), condition=%wide.region_7.8_spmd.clone, body=%wide.region_6.7_spmd.clone.sunk | while | flops 2467925 | bytes 6892861 | solution.py:38
  184.8 1.5 constant_dynamic-slice_fusion.2
  186.3 1.8 fusion.49
  188.2 0.6 dynamic_slice.49
  189.4 1.5 constant_dynamic-slice_fusion.2
  190.9 3.4 fusion.49
  194.4 0.6 dynamic_slice.49
  195.6 1.5 constant_dynamic-slice_fusion.2
  197.1 3.4 fusion.49
  200.6 0.6 dynamic_slice.49
  201.8 1.5 constant_dynamic-slice_fusion.2
  203.3 3.4 fusion.49
  206.8 0.6 dynamic_slice.49
  208.0 1.5 constant_dynamic-slice_fusion.2
  209.5 3.4 fusion.49
  213.0 0.6 dynamic_slice.49
  214.2 1.5 constant_dynamic-slice_fusion.2
  215.7 3.4 fusion.49
  219.2 0.6 dynamic_slice.49
  220.4 1.5 constant_dynamic-slice_fusion.2
  221.9 3.4 fusion.49
  225.3 0.6 dynamic_slice.49
  226.6 1.5 constant_dynamic-slice_fusion.2
  228.1 3.4 fusion.49
  231.6 2.2 fusion.28
  233.9 4.2 %fusion.8 = bf16[128,16,112]{0,2,1:T(8,128)(2,1)S(1)} fusion(f32[16,112,128]{2,1,0:T(8,128)} %fusion.7, f32[16,273,112]{2,1,0:T(8,128)S(1)} %copy-done.1, f32[128,16]{0,1:T(8,128)S(1)} %add_bitcast_fusion, f32[128]{0:T(128)S(1)} %copy-done.13, bf16[128,16,256]{0,2,1:T(8,128)(2,1)} %bitcast.79, bf16[128,16,16]{0,2,1:T(8,128)(2,1)S(1)} %copy-done.10, ...), kind=kOutput, calls=%fused_computation.22 | convolution fusion | flops 755707904 | bytes 4456482 | tf_op jit(solution)/shard_map/bhf,hfe->bhe/dot_general | solution.py:100
  238.2 4.0 multiply_reduce_fusion.1
  242.2 0.9 multiply_convert_fusion.3
  243.4 63.9 %all-gather.7.cloned.1.call-done = bf16[1024,1792]{1,0:T(8,128)(2,1)} async-done(((bf16[128,1792]{1,0:T(8,128)(2,1)}), bf16[1024,1792]{1,0:T(8,128)(2,1)}) %all-gather.7.cloned.1.call-update) | async-done | bytes 3670032 | tf_op jit(solution)/shard_map/all_gather | solution.py:228
  307.3 6.7 %fusion.34 = f32[1024,608]{0,1:T(8,128)} fusion(bf16[1024,1792]{1,0:T(8,128)(2,1)} %all-gather.7.cloned.1.call-done, bf16[1792,608]{0,1:T(8,128)(2,1)} %param.31), kind=kOutput, calls=%fused_computation.86 | convolution fusion | flops 2231369728 | bytes 8339456 | tf_op jit(solution)/shard_map/dot_general | solution.py:229
  314.0 10.7 %convolution_convert_fusion = bf16[1024,1792]{1,0:T(8,128)(2,1)} fusion(bf16[608,1792]{1,0:T(8,128)(2,1)S(1)} %copy-done, f32[1024,608]{0,1:T(8,128)} %fusion.34, bf16[1024,1792]{1,0:T(8,128)(2,1)} %all-gather.7.cloned.1.call-done, bf16[1792,608]{0,1:T(8,128)(2,1)} %param.32), kind=kOutput, calls=%fused_computation.6 | convolution fusion | flops 4468310016 | bytes 14188544 | tf_op jit(solution)/shard_map/dot_general | solution.py:233
  324.7 79.8 %reduce-scatter.2.cloned.1.call-done = bf16[128,1792]{1,0:T(8,128)(2,1)} async-done(((bf16[1024,1792]{1,0:T(8,128)(2,1)}), bf16[128,1792]{1,0:T(8,128)(2,1)}) %reduce-scatter.2.cloned.1.call-update) | async-done | bytes 458768 | tf_op jit(solution)/shard_map/reduce_scatter | solution.py:232
  404.5 1.2 fusion.11
  405.8 5.6 %convolution_convert_fusion.1 = bf16[128,2304]{1,0:T(8,128)(2,1)} fusion(bf16[1792,2304]{1,0:T(8,128)(2,1)} %param.35, bf16[128,1792]{1,0:T(8,128)(2,1)S(1)} %get-tuple-element.192, f32[1792]{0:T(1024)S(1)} %copy-done.7, f32[128]{0:T(128)S(1)} %add_rsqrt_fusion), kind=kOutput, calls=%fused_computation.7 | convolution fusion | flops 1058177024 | bytes 9313792 | tf_op jit(solution)/shard_map/dot_general | solution.py:240
  (81 shorter events, 4.1 us)
Async XLA Ops:
  7.2 306.9 %copy-start = (bf16[608,1792]{1,0:T(8,128)(2,1)S(1)}, bf16[608,1792]{1,0:T(8,128)(2,1)}, u32[]{:S(2)}) copy-start(bf16[608,1792]{1,0:T(8,128)(2,1)} %param.33) | copy-start | bytes 6537220
  7.2 176.4 %all-gather.9.cloned.1.call-start = ((), (), s32[]{:S(2)}) async-start(), calls=%async_computation.3 | async-start | bytes 10063872 | tf_op jit(solution)/shard_map/all_gather | solution.py:21
  9.1 14.9 %collective-permute-start = (bf16[2,1792]{0,1:T(8,128)(2,1)}, bf16[2,1792]{0,1:T(8,128)(2,1)}, u32[]{:S(2)}, u32[]{:S(2)}) collective-permute-start(bf16[2,1792]{0,1:T(8,128)(2,1)} %copy.49), channel_id=1, source_target_pairs={{0,1},{1,2},{2,3},{3,4},{4,5},{5,6},{6,7},{8,9},{9,10},{10,11},{11... | collective-permute-start | bytes 21512 | tf_op jit(solution)/shard_map/ppermute | solution.py:15
  27.0 0.8 copy-start.3
  28.6 1.9 copy-start.18
  28.6 26.8 %copy-start.16 = (s32[4]{0:T(128)S(1)}, s32[4]{0:T(128)}, u32[]{:S(2)}) copy-start(s32[4]{0:T(128)} %param.26) | copy-start | bytes 52
  28.7 28.7 %copy-start.8 = (bf16[128,256]{1,0:T(8,128)(2,1)S(1)}, bf16[128,256]{1,0:T(8,128)(2,1)}, u32[]{:S(2)}) copy-start(bf16[128,256]{1,0:T(8,128)(2,1)} %param.20) | copy-start | bytes 196612
  28.7 28.8 %copy-start.12 = (f32[1,2,273]{2,1,0:T(2,128)S(1)}, f32[1,2,273]{2,1,0:T(2,128)}, u32[]{:S(2)}) copy-start(f32[1,2,273]{2,1,0:T(2,128)} %param.25) | copy-start | bytes 6556
  29.8 277.5 %all-gather.7.cloned.1.call-start = ((), (), s32[]{:S(2)}) async-start(), calls=%async_computation.1 | async-start | bytes 4128768 | tf_op jit(solution)/shard_map/all_gather | solution.py:228
  137.1 44.6 %copy-start.14 = (f32[128]{0:T(128)}, f32[128]{0:T(128)S(1)}, u32[]{:S(2)}) copy-start(f32[128]{0:T(128)S(1)} %select_reduce_fusion) | copy-start | bytes 1540
  137.2 44.5 %copy-start.9 = (bf16[128,16,16]{0,2,1:T(8,128)(2,1)}, bf16[128,16,16]{0,2,1:T(8,128)(2,1)S(1)}, u32[]{:S(2)}) copy-start(bf16[128,16,16]{0,2,1:T(8,128)(2,1)S(1)} %multiply_convert_fusion.5) | copy-start | bytes 196612
  137.5 44.2 %copy-start.5 = (bf16[128,16,16,16]{0,3,2,1:T(8,128)(2,1)}, bf16[128,16,16,16]{0,3,2,1:T(8,128)(2,1)S(1)}, u32[]{:S(2)}) copy-start(bf16[128,16,16,16]{0,3,2,1:T(8,128)(2,1)S(1)} %multiply_convert_fusion.2) | copy-start | bytes 3145732
  138.0 43.2 %copy-start.4 = (bf16[128,1792]{0,1:T(8,128)(2,1)S(1)}, bf16[128,1792]{0,1:T(8,128)(2,1)}, u32[]{:S(2)}) copy-start(bf16[128,1792]{0,1:T(8,128)(2,1)} %copy-done.3) | copy-start | bytes 1376260
  181.7 1.9 copy-start.17
  183.6 48.0 %copy-start.10 = (bf16[128,16,16]{0,2,1:T(8,128)(2,1)S(1)}, bf16[128,16,16]{0,2,1:T(8,128)(2,1)}, u32[]{:S(2)}) copy-start(bf16[128,16,16]{0,2,1:T(8,128)(2,1)} %copy-done.9) | copy-start | bytes 196612
  231.5 2.3 copy-start.13
  231.6 2.3 copy-start.15
  231.6 2.3 copy-start.1
  233.9 4.3 %copy-start.6 = (bf16[128,1792]{1,0:T(8,128)(2,1)S(1)}, bf16[128,1792]{1,0:T(8,128)(2,1)}, u32[]{:S(2)}) copy-start(bf16[128,1792]{1,0:T(8,128)(2,1)} %param.19) | copy-start | bytes 1376260
  238.1 4.0 copy-start.11
  243.1 161.4 %reduce-scatter.2.cloned.1.call-start = ((), (), s32[]{:S(2)}) async-start(), calls=%async_computation.2 | async-start | bytes 4128768 | tf_op jit(solution)/shard_map/reduce_scatter | solution.py:232
  324.7 81.1 %copy-start.7 = (f32[1792]{0:T(1024)S(1)}, f32[1792]{0:T(1024)}, u32[]{:S(2)}) copy-start(f32[1792]{0:T(1024)} %param.34) | copy-start | bytes 21508
  405.8 5.6 %copy-start.2 = (bf16[128,1792]{1,0:T(8,128)(2,1)}, bf16[128,1792]{1,0:T(8,128)(2,1)S(1)}, u32[]{:S(2)}) copy-start(bf16[128,1792]{1,0:T(8,128)(2,1)S(1)} %get-tuple-element.192) | copy-start | bytes 1376260
Sparse Core Ops, SparseCore 0:
  30.0 147.1 all-gather.8
  243.2 64.0 all-gather.6
  324.8 79.6 reduce-scatter.1
where the time goes:
time: 419 us; the launch traced here: 418 us
  waiting for transfers between devices  145 us (35%)
  blocking collectives  141 us (34%)
  matrix products  38.4 us (9%)
  other arithmetic  37.7 us (9%)
  local copies, waits for them, and re-layouts  26.9 us (6%)
  between operations  17.4 us (4%)
  starting transfers between devices  5.98 us (1%)
  loops' own time  5.5 us (1%)
    reduce_scatter x1, waiting for transfers between devices, shards(): lax.psum_scatter(jnp.dot(hidden, down_weight, preferred_element_type=jnp....  79.8 us
    all_gather x1, waiting for transfers between devices, shards(): row_piece = lax.all_gather(normed, 'mlp', axis=0, tiled=True)  63.9 us
    all_gather x1, blocking collectives, shards(): lax.all_gather(own_state.astype(jnp.bfloat16), 'mlp', axis=0, tiled=True)  42 us
    all_gather x1, blocking collectives, prefix(): lax.all_gather(part.astype(kind), axis)  32.7 us
    all_gather x1, blocking collectives, shards(): lax.all_gather(own_norm.astype(jnp.bfloat16), 'mlp', axis=0, tiled=True)  30.7 us
    select_n x16, other arithmetic, step(): return jax.tree.map(lambda a, b: jnp.where(reached, a, b), new, before)  25.9 us
    unnamed x1, blocking collectives  23.6 us
    dynamic_slice x16, local copies, waits for them, and re-layouts, step(): part[k].astype(own.dtype)  16.6 us
  transfers between devices with their start and end apart: 4, of which 3 were waited for; matrix products, arithmetic and copies ran while one was open for 4% of the time, Pallas kernels for 0%

commit v1 on v0

v1 whole, which is shorter than its diff:
```python
import functools
import math

import jax
import jax.numpy as jnp
from jax import lax
from jax.experimental import pallas as pl
from jax.experimental.pallas import tpu as pltpu
from jax.sharding import PartitionSpec as P

EPSILON = 1e-05
DEPTH = 4
MIB = 1 << 20
ACROSS = (((0,), (0,)), ((), ()))
PLAIN = (((1,), (0,)), ((), ()))
F32 = jnp.float32
BF16 = jnp.bfloat16
VMEM = pltpu.VMEM


def vmem():
    return pl.BlockSpec(memory_space=VMEM)


def dot(a, b, dims=PLAIN):
    return lax.dot_general(a, b, dims, preferred_element_type=F32)


def pack_kernel(q_ref, k_ref, v_ref, out_ref):
    count = out_ref.shape[0]
    at = 0
    for ref in (q_ref, k_ref, v_ref):
        turned = ref[...].T
        part = turned.shape[0] // count
        for m in range(count):
            out_ref[m, at : at + part, :] = turned[m * part : (m + 1) * part, :]
        at += part


def pack(q, k, v, count):
    rows = (q.shape[1] + k.shape[1] + v.shape[1]) // count
    return pl.pallas_call(
        pack_kernel,
        out_shape=jax.ShapeDtypeStruct((count, rows, q.shape[0]), BF16),
        in_specs=[vmem()] * 3,
        out_specs=vmem(),
        compiler_params=pltpu.CompilerParams(vmem_limit_bytes=24 * MIB),
        name="pack_heads",
    )(q, k, v)


def attention_kernel(heads, fd, hd, meta_ref, x_ref, conv_ref, state_ref, out_ref, turned, vconv, feats):
    blocks, rows, local = x_ref.shape
    tokens = blocks * local
    requests = meta_ref.shape[1]
    values_at = 2 * heads * fd
    tile = 256 if tokens % 256 == 0 else local
    for m in range(blocks):
        turned[:, m * local : (m + 1) * local] = x_ref[m]

    position = lax.broadcasted_iota(jnp.int32, (1, tokens), 1)
    start = jnp.zeros((1, tokens), jnp.int32)
    flag = jnp.zeros((1, tokens), F32) + meta_ref[1, 0].astype(F32)
    boundary = jnp.int32(0)
    for r in range(1, requests):
        boundary = boundary + meta_ref[0, r - 1]
        reached = position >= boundary
        start = jnp.where(reached, boundary, start)
        flag = jnp.where(reached, meta_ref[1, r].astype(F32), flag)

    values = turned[values_at:, :].astype(F32)
    total = conv_ref[:, 0:1] * values
    for tap in range(1, conv_ref.shape[1]):
        earlier = pltpu.roll(values, tap, 1)
        total = total + conv_ref[:, tap : tap + 1] * jnp.where(position - tap >= start, earlier, 0.0)
    vconv[...] = total.astype(BF16)

    for h in range(heads):
        query = turned[h * fd : (h + 1) * fd, :]
        wide = query.astype(F32)
        scaled = wide * (1.0 / math.sqrt(2.0 * fd))
        for a in range(fd):
            feats[a * fd : (a + 1) * fd, :] = (wide[a : a + 1, :] * scaled).astype(BF16)
        feats[fd * fd : fd * fd + fd, :] = (wide * fd ** (-0.25)).astype(BF16)
        ones = lax.broadcasted_iota(jnp.int32, (16, tokens), 0) == 0
        feats[fd * fd + fd :, :] = ones.astype(F32).astype(BF16)
        key = turned[(heads + h) * fd : (heads + h + 1) * fd, :]
        for first in range(0, tokens, tile):
            last = first + tile
            old = dot(state_ref[h], feats[:, first:last], ACROSS)
            score = dot(key[:, :last], query[:, first:last], ACROSS) * (fd**-0.5) + 1.0
            score = score * score * 0.5 + 0.5
            key_at = lax.broadcasted_iota(jnp.int32, (last, tile), 0)
            visible = (key_at >= start[:, first:last]) & (key_at <= position[:, first:last])
            score = jnp.where(visible, score, 0.0)
            den = jnp.sum(score, axis=0, keepdims=True) + flag[:, first:last] * old[hd : hd + 1, :]
            num = dot(vconv[h * hd : (h + 1) * hd, :last], score.astype(BF16))
            num = num + flag[:, first:last] * old[:hd, :]
            result = (num / den).astype(BF16)
            for at in range(first, last, local):
                out_ref[at // local, h * hd : (h + 1) * hd, :] = result[:, at - first : at - first + local]


def attention(meta, x, conv, state, heads, fd, hd):
    blocks, rows, local = x.shape
    tokens = blocks * local
    return pl.pallas_call(
        functools.partial(attention_kernel, heads, fd, hd),
        out_shape=jax.ShapeDtypeStruct((blocks, heads * hd, local), BF16),
        in_specs=[pl.BlockSpec(memory_space=pltpu.SMEM)] + [vmem()] * 3,
        out_specs=vmem(),
        scratch_shapes=[
            VMEM((rows, tokens), BF16),
            VMEM((heads * hd, tokens), BF16),
            VMEM((state.shape[1], tokens), BF16),
        ],
        compiler_params=pltpu.CompilerParams(vmem_limit_bytes=40 * MIB),
        name="attention",
    )(meta, x, conv, state)


def rms(rows, gain):
    return rows * lax.rsqrt(jnp.mean(rows * rows, axis=-1, keepdims=True) + EPSILON) * gain


def project_kernel(tile, att_ref, w_ref, res_ref, gain_ref, sum_ref, normed_ref, rows):
    step = pl.program_id(0)

    @pl.when(step == 0)
    def _():
        rows[...] = att_ref[...].T

    at = pl.ds(pl.multiple_of(step * tile, tile), tile)
    projected = dot(rows[...], w_ref[...])
    sum_ref[:, at] = (res_ref[:, at].astype(F32) + projected).astype(BF16)

    @pl.when(step == pl.num_programs(0) - 1)
    def _():
        normed_ref[...] = rms(sum_ref[...].astype(F32), gain_ref[...]).astype(BF16)


def project(att, w, residual, gain):
    depth, rows = att.shape
    width = w.shape[1]
    tile = 256
    whole = lambda shape: pl.BlockSpec(shape, lambda i: (0, 0))
    return pl.pallas_call(
        functools.partial(project_kernel, tile),
        grid=(width // tile,),
        out_shape=[jax.ShapeDtypeStruct((rows, width), BF16)] * 2,
        in_specs=[
            whole((depth, rows)),
            pl.BlockSpec((depth, tile), lambda i: (0, i)),
            whole((rows, width)),
            whole((1, width)),
        ],
        out_specs=[whole((rows, width))] * 2,
        scratch_shapes=[VMEM((rows, depth), BF16)],
        compiler_params=pltpu.CompilerParams(vmem_limit_bytes=24 * MIB),
        name="out_projection",
    )(att, w, residual, gain)


def mlp_kernel(inputs, sides, flips, *refs):
    it = iter(refs)
    take = lambda n: [next(it) for _ in range(n)]
    xs = take(inputs)
    own = take(3)
    pieces = [[take(2) for _ in flips] for _ in range(sides)]
    outs = take(inputs)
    gates, ups, downs, sems = take(4)
    me = lax.axis_index("req")
    copies = [
        pltpu.make_async_copy(own[0], gates.at[0], sems.at[0]),
        pltpu.make_async_copy(own[1], ups.at[0], sems.at[1]),
        pltpu.make_async_copy(own[2], downs.at[0, pl.ds(0, own[2].shape[0])], sems.at[2]),
    ]
    index = 3
    for side in range(sides):
        for flip, (gate_up, down) in zip(flips, pieces[side]):
            slot = me ^ flip
            deep, tall = gate_up.shape[1], down.shape[0]
            at = pl.ds(pl.multiple_of(slot * deep, 16), deep)
            low = pl.ds(pl.multiple_of(slot * tall, 16), tall)
            copies.append(pltpu.make_async_copy(gate_up.at[0], gates.at[1 + side, at], sems.at[index]))
            copies.append(pltpu.make_async_copy(gate_up.at[1], ups.at[1 + side, at], sems.at[index + 1]))
            copies.append(pltpu.make_async_copy(down, downs.at[1 + side, low], sems.at[index + 2]))
            index += 3
    for copy in copies:
        copy.start()
    x = xs[0][...] if inputs == 1 else jnp.concatenate([ref[...] for ref in xs], axis=0)
    hidden_units = own[0].shape[1]
    per_side = 3 * len(flips)
    total = None
    for side in range(1 + sides):
        for copy in copies[:3] if side == 0 else copies[3 + (side - 1) * per_side : 3 + side * per_side]:
            copy.wait()
        gate = dot(x, gates[side])
        up = dot(x, ups[side])
        hidden = (gate * jax.nn.sigmoid(gate) * up).astype(BF16)
        part = dot(hidden, downs[side, :hidden_units, :])
        total = part if total is None else total + part
    local = xs[0].shape[0]
    for i, out in enumerate(outs):
        out[...] = total[i * local : (i + 1) * local].astype(BF16)


def mlp(xs, own, pieces, flips):
    deep, units = own[0].shape
    sides = len(pieces)
    tall = pieces[0][0][1].shape[0] * len(flips) if sides else units
    flat = [ref for side in pieces for piece in side for ref in piece]
    rows = xs[0].shape[0]
    weight_bytes = 2 * (1 + sides) * 3 * deep * units
    return pl.pallas_call(
        functools.partial(mlp_kernel, len(xs), sides, flips),
        out_shape=[jax.ShapeDtypeStruct((rows, deep), BF16)] * len(xs),
        in_specs=[vmem()] * len(xs) + [pl.BlockSpec(memory_space=pl.ANY)] * (3 + len(flat)),
        out_specs=[vmem()] * len(xs),
        scratch_shapes=[
            VMEM((1 + sides, deep, units), BF16),
            VMEM((1 + sides, deep, units), BF16),
            VMEM((1 + sides, max(tall, units), deep), BF16),
            pltpu.SemaphoreType.DMA((3 + 3 * sides * len(flips),)),
        ],
        compiler_params=pltpu.CompilerParams(vmem_limit_bytes=40 * MIB),
        cost_estimate=pl.CostEstimate(
            flops=6 * len(xs) * rows * (1 + sides) * deep * units,
            bytes_accessed=weight_bytes,
            transcendentals=0,
        ),
        name="feed_forward",
    )(*xs, *own, *flat)


def next_kernel(tile, first_ref, own_ref, left_ref, right_ref, gain_ref, w_ref, sum_ref, out_ref, normed):
    step = pl.program_id(0)

    @pl.when(step == 0)
    def _():
        extra = own_ref[...].astype(F32) + left_ref[...].astype(F32) + right_ref[...].astype(F32)
        second = (first_ref[...].astype(F32) + extra).astype(BF16)
        sum_ref[...] = second
        normed[...] = rms(second.astype(F32), gain_ref[...]).astype(BF16)

    out_ref[...] = dot(normed[...], w_ref[...]).astype(BF16)


def next_projection(first, own, left, right, gain, w):
    rows, deep = first.shape
    width = w.shape[1]
    tile = 256
    whole = lambda shape: pl.BlockSpec(shape, lambda i: (0, 0))
    return pl.pallas_call(
        functools.partial(next_kernel, tile),
        grid=(width // tile,),
        out_shape=[
            jax.ShapeDtypeStruct((rows, deep), BF16),
            jax.ShapeDtypeStruct((rows, width), BF16),
        ],
        in_specs=[whole((rows, deep))] * 4
        + [whole((1, deep)), pl.BlockSpec((deep, tile), lambda i: (0, i))],
        out_specs=[whole((rows, deep)), pl.BlockSpec((rows, tile), lambda i: (0, i))],
        scratch_shapes=[VMEM((rows, deep), BF16)],
        compiler_params=pltpu.CompilerParams(vmem_limit_bytes=24 * MIB),
        name="next_projection",
    )(first, own, left, right, gain, w)


def side_weights(gate, up, down, width):
    sharers = lax.axis_size("req")
    me = lax.axis_index("req")
    depth = lax.axis_size("mlp") // width
    deep = gate.shape[0] // sharers
    tall = -(-down.shape[0] // (16 * sharers)) * 16
    padded = jnp.pad(down, ((0, tall * sharers - down.shape[0]), (0, 0)))
    mine = (
        jnp.stack([lax.dynamic_slice_in_dim(w, me * deep, deep, 0) for w in (gate, up)]),
        lax.dynamic_slice_in_dim(padded, me * tall, tall, 0),
    )
    sides, flips = [], []
    for turn in range(1, width):
        route = [
            (z * width + y, z * width + (y + turn) % width) for z in range(depth) for y in range(width)
        ]
        held = [(0, tuple(lax.ppermute(part, "mlp", route) for part in mine))]
        bit = sharers // 2
        while bit:
            swap = [(i, i ^ bit) for i in range(sharers)]
            held += [
                (flip ^ bit, tuple(lax.ppermute(part, "req", swap) for part in piece))
                for flip, piece in held
            ]
            bit //= 2
        flips = [flip for flip, _ in held]
        sides.append([piece for _, piece in held])
    return sides, flips


def cached_state(prefix_state, prefix_norm, prefix_owner, fd):
    heads, feats, hd = prefix_state.shape[1:]
    both = jnp.concatenate([prefix_state[0], prefix_norm[0][:, :, None]], axis=2).astype(BF16)
    ordered = jnp.concatenate([both[:, 1 + fd :], both[:, 1 : 1 + fd], both[:, :1]], axis=1)
    packed = jnp.pad(ordered, ((0, 0), (0, 15), (0, 128 - hd - 1)))
    slots = lax.axis_size("req")
    me = lax.axis_index("req")
    owner = prefix_owner[me]
    chosen = packed
    for turn in range(1, slots):
        other = lax.ppermute(packed, "req", [(i, i ^ turn) for i in range(slots)])
        chosen = jnp.where((me ^ turn) == owner, other, chosen)
    return chosen


def shards(
    residual_in,
    query_in,
    key_in,
    values_in,
    conv_weight,
    prefix_state,
    prefix_norm,
    prefix_owner,
    lengths,
    old_flags,
    out_weight,
    mlp_gain,
    gate_weight,
    up_weight,
    down_weight,
    next_gain,
    qkv_weight,
):
    mlp_count = lax.axis_size("mlp")
    column = lax.axis_index("mlp")
    width = mlp_count // DEPTH
    level = column // width
    heads = prefix_state.shape[1]
    hd = values_in.shape[1] // (heads * mlp_count)
    fd = query_in.shape[1] // (heads * mlp_count)

    state = cached_state(prefix_state, prefix_norm, prefix_owner, fd)
    pieces, flips = side_weights(gate_weight, up_weight, down_weight, width)

    taps = lax.dynamic_slice_in_dim(conv_weight, column * heads * hd, heads * hd, 1).T
    meta = jnp.concatenate([lengths, old_flags], axis=0)
    by_head = lax.all_to_all(pack(query_in, key_in, values_in, mlp_count), "mlp", 0, 0, tiled=True)
    attended = attention(meta, by_head, taps, state, heads, fd, hd)
    by_row = lax.all_to_all(attended, "mlp", 0, 0, tiled=True)
    by_row = by_row.reshape(mlp_count * heads * hd, by_row.shape[2])
    first_sum, normed = project(by_row, out_weight, residual_in, mlp_gain[None])

    def along(data, hops):
        return lax.ppermute(
            data, "mlp", [(a * width + y, b * width + y) for a, b in hops for y in range(width)]
        )

    own = (gate_weight, up_weight, down_weight)
    feed = lambda *xs: mlp(xs, own, pieces, flips)
    from_left = along(normed, [(0, 1), (1, 2), (2, 3)])
    from_right = along(normed, [(3, 2), (2, 1), (1, 0)])
    left_two = along(from_left, [(1, 2), (2, 3)])
    right_two = along(from_right, [(2, 1), (1, 0)])
    two = jnp.where(level >= 2, left_two, right_two)
    three = along(two, [(2, 3), (1, 0)])
    (part_own,) = feed(normed)
    part_left, part_right = feed(from_left, from_right)
    (part_two,) = feed(two)
    (part_three,) = feed(three)

    far = along(part_three, [(0, 1), (3, 2)])
    middle = part_two + far
    to_right = along(middle, [(0, 1), (1, 2)])
    to_left = along(middle, [(3, 2), (2, 1)])
    last_right = along(part_right + to_right, [(0, 1), (1, 2), (2, 3)])
    last_left = along(part_left + to_left, [(3, 2), (2, 1), (1, 0)])
    return next_projection(first_sum, part_own, last_right, last_left, next_gain[None], qkv_weight)


def solution(mesh):
    rows = P(("req", "mlp"), None)
    placed = (
        rows,
        rows,
        rows,
        rows,
        P(),
        P("req", "mlp", None, None),
        P("req", "mlp", None),
        P(),
        P("req", None),
        P("req", None),
        P(),
        P(),
        P(None, "mlp"),
        P(None, "mlp"),
        P("mlp", None),
        P(),
        P(),
    )
    return jax.shard_map(
        shards, mesh=mesh, in_specs=placed, out_specs=(rows, rows), check_vma=False
    )
```

time: 419 us -> 166 us (0.40)
  blocking collectives: 141 us -> 0 us
  waiting for transfers between devices: 145 us -> 44.8 us
  Pallas kernels: 0 us -> 41.3 us
  matrix products: 38.4 us -> 0 us
  starting transfers between devices: 5.98 us -> 42.8 us
  other arithmetic: 37.7 us -> 4.37 us
  between operations: 17.4 us -> 2.77 us
  loops' own time: 5.5 us -> 0 us
    all_gather x5 -> x0, blocking collectives: 118 us -> none  [the longest x1 42 us: shards(): lax.all_gather(own_state.astype(jnp.bfloat16), 'mlp', axis=0, tiled=True)]
    reduce_scatter x1 -> x0, waiting for transfers between devices: 79.8 us -> none  [shards(): lax.psum_scatter(jnp.dot(hidden, down_weight, preferred_element_type=jnp....]
    all_gather x2 -> x0, waiting for transfers between devices: 64 us -> none  [the longest x1 63.9 us: shards(): row_piece = lax.all_gather(normed, 'mlp', axis=0, tiled=True)]
    ppermute x1 -> x21, waiting for transfers between devices: 0.75 us -> 44.2 us  [the longest x10 23 us: along(): lax.ppermute(data, 'mlp', [(a * width + y, b * width + y) for a, b in hop...]
    pallas_call x0 -> x8, Pallas kernels: none -> 41.3 us  [the longest x4 26.9 us: mlp(): pl.pallas_call(functools.partial(mlp_kernel, len(xs), sides, flips), out_...]
    dot_general x11 -> x0, matrix products: 38.4 us -> none  [the longest x1 10.7 us: shards(): jnp.dot(hidden, down_weight, preferred_element_type=jnp.float32)]
    ppermute x1 -> x21, starting transfers between devices: 5.64 us -> 31 us  [the longest x10 22.8 us: along(): lax.ppermute(data, 'mlp', [(a * width + y, b * width + y) for a, b in hop...]
    select_n x17 -> x2, other arithmetic: 25.9 us -> 1.85 us  [the longest x1 1.02 us: cached_state(): chosen = jnp.where(me ^ turn == owner, other, chosen)]
  transfers between devices with their start and end apart: 4 -> 23, of which waited for: 3 -> 12; matrix products, arithmetic and copies ran while one was open for 4% -> 10% of each run, Pallas kernels for 0% -> 17%
where the time goes in v1:
time: 166 us; the launch traced here: 165 us
  waiting for transfers between devices  44.8 us (27%)
  starting transfers between devices  42.8 us (26%)
  Pallas kernels  41.3 us (25%)
  local copies, waits for them, and re-layouts  29 us (17%)
  other arithmetic  4.37 us (3%)
  between operations  2.77 us (2%)
    pallas_call x4, Pallas kernels, mlp(): pl.pallas_call(functools.partial(mlp_kernel, len(xs), sides, flips), out_...  26.9 us
    unnamed x64, local copies, waits for them, and re-layouts  24.8 us
    ppermute x10, waiting for transfers between devices, along(): lax.ppermute(data, 'mlp', [(a * width + y, b * width + y) for a, b in hop...  23 us
    ppermute x10, starting transfers between devices, along(): lax.ppermute(data, 'mlp', [(a * width + y, b * width + y) for a, b in hop...  22.8 us
    ppermute x2, waiting for transfers between devices, side_weights(): held = [(0, tuple((lax.ppermute(part, 'mlp', route) for part in mine)))]  8.9 us
    ppermute x6, waiting for transfers between devices, side_weights(): lax.ppermute(part, 'req', swap)  7.67 us
    all_to_all x1, starting transfers between devices, shards(): lax.all_to_all(pack(query_in, key_in, values_in, mlp_count), 'mlp', 0, 0,...  7.28 us
    pallas_call x1, Pallas kernels, next_projection(): pl.pallas_call(functools.partial(next_kernel, tile), grid=(width // tile,...  5.35 us
  transfers between devices with their start and end apart: 23, of which 12 were waited for; matrix products, arithmetic and copies ran while one was open for 10% of the time, Pallas kernels for 17%

profile of v1, /device:TPU:0, one launch (start us, length us, event | category | flops | bytes accessed | tf_op | source)
XLA Modules:
  0.0 165.0 jit_solution(15200780841226145546)
XLA Ops:
  0.7 1.0 copy-done.10
  1.7 0.8 copy-done.20
  2.5 0.8 copy-done.21
  3.4 1.0 pack_heads.1
  4.4 7.3 %all-to-all-start = ((bf16[8,288,128]{2,1,0:T(8,128)(2,1)}), bf16[8,288,128]{2,1,0:T(8,128)(2,1)}, u32[]{:S(2)}, u32[]{:S(2)}) async-start(bf16[8,288,128]{2,1,0:T(8,128)(2,1)} %pack_heads.1), calls=%async_computation | async-start | bytes 1179648 | tf_op jit(solution)/shard_map/all_to_all | solution.py:347
  11.7 1.9 %constant_dynamic-slice_fusion = (bf16[448,608]{0,1:T(8,128)(2,1)S(1)}, bf16[448,608]{0,1:T(8,128)(2,1)S(1)}) fusion(bf16[1792,608]{0,1:T(8,128)(2,1)} %param.30, s32[]{:T(128)S(6)} %select_n.54, bf16[1792,608]{0,1:T(8,128)(2,1)} %param.29), kind=kLoop, calls=%fused_computation.26 | loop fusion | bytes 2179076 | tf_op jit(solution)/shard_map/dynamic_slice | solution.py:278
  13.6 0.3 copy.35
  13.9 0.3 copy.34
  14.3 1.2 pad_maximum_fusion
  15.5 2.0 %collective-permute-start.3 = (bf16[2,448,608]{2,1,0:T(8,128)(2,1)}, bf16[2,448,608]{2,1,0:T(8,128)(2,1)S(1)}, u32[]{:S(2)}, u32[]{:S(2)}) collective-permute-start(bf16[2,448,608]{2,1,0:T(8,128)(2,1)} %pad_maximum_fusion), channel_id=1, source_target_pairs={{0,1},{1,0},{2,3},{3,2},{4,5},{5,4},{6,7},{7,6},{8,9},{9,8},{10,11... | collective-permute-start | bytes 3268616 | tf_op jit(solution)/shard_map/ppermute | solution.py:286
  18.0 0.7 fusion.7
  18.7 1.5 collective-permute-start.1
  20.2 0.3 collective-permute-start.2
  20.7 0.8 copy.44
  21.5 0.6 dynamic_slice.16
  23.7 1.4 collective-permute-done
  25.0 3.3 %collective-permute-done.1 = bf16[2,288,128]{2,1,0:T(8,128)(2,1)} collective-permute-done((bf16[2,288,128]{2,1,0:T(8,128)(2,1)}, bf16[2,288,128]{2,1,0:T(8,128)(2,1)}, u32[]{:S(2)}, u32[]{:S(2)}) %collective-permute-start.1) | collective-permute-done | bytes 147488 | tf_op jit(solution)/shard_map/ppermute | solution.py:310
  28.4 1.0 select_select_fusion.state_ref
  29.4 0.9 copy-done.9
  30.3 4.1 %attention.1 = bf16[8,224,128]{2,1,0:T(8,128)(2,1)S(1)} custom-call(s32[2,4]{1,0:T(2,128)S(1)} %pad_add_fusion.meta_ref, bf16[8,288,128]{2,1,0:T(8,128)(2,1)} %all-to-all-done.x_ref, f32[224,3]{1,0:T(8,128)S(1)} %bitcast.10, bf16[2,288,128]{2,1,0:T(8,128)(2,1)S(1)} %select_select_fusion.state_ref), custom_call_target="tpu_custom_call" | custom-call | tf_op jit(solution)/shard_map/attention/pallas_call | solution.py:107
  34.4 0.8 copy-done.8
  35.2 4.5 %all-to-all-start.1 = ((bf16[8,224,128]{2,1,0:T(8,128)(2,1)}), bf16[8,224,128]{2,1,0:T(8,128)(2,1)}, u32[]{:S(2)}, u32[]{:S(2)}) async-start(bf16[8,224,128]{2,1,0:T(8,128)(2,1)} %copy-done.8), calls=%async_computation.1 | async-start | bytes 917504 | tf_op jit(solution)/shard_map/all_to_all | solution.py:349
  39.7 8.9 %collective-permute-done.3.refs_4_.refs_5_ = bf16[2,448,608]{2,1,0:T(8,128)(2,1)S(1)} collective-permute-done((bf16[2,448,608]{2,1,0:T(8,128)(2,1)}, bf16[2,448,608]{2,1,0:T(8,128)(2,1)S(1)}, u32[]{:S(2)}, u32[]{:S(2)}) %collective-permute-start.3) | collective-permute-done | bytes 1089568 | tf_op jit(solution)/shard_map/ppermute | solution.py:286
  48.6 1.5 collective-permute-start.5
  50.1 0.9 pad_dynamic-slice_fusion
  51.0 1.5 collective-permute-start.4
  52.5 0.6 all-to-all-done.1
  53.1 2.8 %copy-done.7 = bf16[1792,1792]{1,0:T(8,128)(2,1)S(1)} copy-done((bf16[1792,1792]{1,0:T(8,128)(2,1)S(1)}, bf16[1792,1792]{1,0:T(8,128)(2,1)}, u32[]{:S(2)}) %copy-start.7) | copy-done | bytes 6422552
  55.9 1.0 copy-done.11
  56.9 4.0 %out_projection.1 = (bf16[128,1792]{1,0:T(8,128)(2,1)S(1)}, bf16[128,1792]{1,0:T(8,128)(2,1)S(1)}) custom-call(bf16[1792,128]{1,0:T(8,128)(2,1)} %bitcast.4.att_ref, bf16[1792,1792]{1,0:T(8,128)(2,1)S(1)} %copy-done.7, bf16[128,1792]{1,0:T(8,128)(2,1)S(1)} %copy-done.11, f32[1,1792]{1,0:T(1,128)S(1)} %broadcast_in_dim.6.gain_ref), custom_call_target="tpu_custom_call" | custom-call | tf_op jit(solution)/shard_map/out_projection/pallas_call | solution.py:147
  60.9 0.8 copy-done.18
  61.6 3.0 %collective-permute-start.11 = (bf16[128,1792]{1,0:T(8,128)(2,1)S(1)}, bf16[128,1792]{1,0:T(8,128)(2,1)S(1)}, u32[]{:S(2)}, u32[]{:S(2)}) collective-permute-start(bf16[128,1792]{1,0:T(8,128)(2,1)S(1)} %get-tuple-element.7.refs_0_), channel_id=1, source_target_pairs={{0,2},{1,3},{2,4},{3,5},{4,6},{5,7},{8,10},{9,11},{10,12},{11,13},... | collective-permute-start | bytes 1376264 | tf_op jit(solution)/shard_map/ppermute | solution.py:354
  64.6 1.3 collective-permute-start.12
  65.9 0.8 copy-done.12
  66.7 0.2 collective-permute-start.6
  67.0 6.1 %collective-permute-done.11.refs_0_ = bf16[128,1792]{1,0:T(8,128)(2,1)S(1)} collective-permute-done((bf16[128,1792]{1,0:T(8,128)(2,1)S(1)}, bf16[128,1792]{1,0:T(8,128)(2,1)S(1)}, u32[]{:S(2)}, u32[]{:S(2)}) %collective-permute-start.11) | collective-permute-done | bytes 458784 | tf_op jit(solution)/shard_map/ppermute | solution.py:354
  73.1 0.7 collective-permute-start.13
  73.8 3.5 %collective-permute-done.12.refs_1_ = bf16[128,1792]{1,0:T(8,128)(2,1)S(1)} collective-permute-done((bf16[128,1792]{1,0:T(8,128)(2,1)S(1)}, bf16[128,1792]{1,0:T(8,128)(2,1)S(1)}, u32[]{:S(2)}, u32[]{:S(2)}) %collective-permute-start.12) | collective-permute-done | bytes 458784 | tf_op jit(solution)/shard_map/ppermute | solution.py:354
  77.2 1.3 collective-permute-start.14
  78.6 0.5 collective-permute-start.9
  79.1 7.7 %collective-permute-done.6.refs_7_.refs_8_ = bf16[160,1792]{1,0:T(8,128)(2,1)} collective-permute-done((bf16[160,1792]{1,0:T(8,128)(2,1)}, bf16[160,1792]{1,0:T(8,128)(2,1)}, u32[]{:S(2)}, u32[]{:S(2)}) %collective-permute-start.6) | collective-permute-done | bytes 573472 | tf_op jit(solution)/shard_map/ppermute | solution.py:291
  86.8 0.5 collective-permute-start.10
  87.3 1.7 %collective-permute-done.14 = bf16[128,1792]{1,0:T(8,128)(2,1)S(1)} collective-permute-done((bf16[128,1792]{1,0:T(8,128)(2,1)S(1)}, bf16[128,1792]{1,0:T(8,128)(2,1)S(1)}, u32[]{:S(2)}, u32[]{:S(2)}) %collective-permute-start.14) | collective-permute-done | bytes 458784 | tf_op jit(solution)/shard_map/ppermute | solution.py:354
  89.0 0.8 broadcast_select_fusion.refs_0_
  89.8 1.3 collective-permute-start.15
  91.1 3.3 %copy.36.refs_1_.refs_2_ = bf16[1792,608]{1,0:T(8,128)(2,1)S(1)} copy(bf16[1792,608]{0,1:T(8,128)(2,1)} %param.29) | data formatting | bytes 4358144 | tf_op args[12]
  94.4 4.2 %copy.37.refs_2_.refs_3_ = bf16[1792,608]{1,0:T(8,128)(2,1)} copy(bf16[1792,608]{0,1:T(8,128)(2,1)} %param.30) | data formatting | bytes 4358144 | tf_op args[13]
  98.6 4.9 %collective-permute-done.15.refs_0_ = bf16[128,1792]{1,0:T(8,128)(2,1)} collective-permute-done((bf16[128,1792]{1,0:T(8,128)(2,1)}, bf16[128,1792]{1,0:T(8,128)(2,1)}, u32[]{:S(2)}, u32[]{:S(2)}) %collective-permute-start.15) | collective-permute-done | bytes 458784 | tf_op jit(solution)/shard_map/ppermute | solution.py:354
  103.5 1.6 copy-done.1
  105.2 1.6 copy-done.4
  106.8 6.8 %feed_forward.7 = bf16[128,1792]{1,0:T(8,128)(2,1)S(1)} custom-call(bf16[128,1792]{1,0:T(8,128)(2,1)} %collective-permute-done.15.refs_0_, bf16[1792,608]{1,0:T(8,128)(2,1)S(1)} %copy.36.refs_1_.refs_2_, bf16[1792,608]{1,0:T(8,128)(2,1)S(1)} %copy-done.1, bf16[608,1792]{1,0:T(8,128)(2,1)S(1)} %copy-done.4, ...), custom_call_target="tpu_custom_call" | custom-call | flops 1673527296 | bytes 13074432 | tf_op jit(solution)/shard_map/feed_forward/pallas_call | solution.py:215
  113.6 1.8 %collective-permute-start.16 = (bf16[128,1792]{1,0:T(8,128)(2,1)S(1)}, bf16[128,1792]{1,0:T(8,128)(2,1)S(1)}, u32[]{:S(2)}, u32[]{:S(2)}) collective-permute-start(bf16[128,1792]{1,0:T(8,128)(2,1)S(1)} %feed_forward.7), channel_id=1, source_target_pairs={{0,2},{1,3},{6,4},{7,5},{8,10},{9,11},{14,12},{15,13},{16,18},{17,... | collective-permute-start | bytes 1376264 | tf_op jit(solution)/shard_map/ppermute | solution.py:354
  115.4 6.8 %feed_forward.6 = bf16[128,1792]{1,0:T(8,128)(2,1)S(1)} custom-call(bf16[128,1792]{1,0:T(8,128)(2,1)} %broadcast_select_fusion.refs_0_, bf16[1792,608]{1,0:T(8,128)(2,1)S(1)} %copy.36.refs_1_.refs_2_, bf16[1792,608]{1,0:T(8,128)(2,1)S(1)} %copy-done.1, bf16[608,1792]{1,0:T(8,128)(2,1)S(1)} %copy-done.4, ...), custom_call_target="tpu_custom_call" | custom-call | flops 1673527296 | bytes 13074432 | tf_op jit(solution)/shard_map/feed_forward/pallas_call | solution.py:215
  122.1 1.2 collective-permute-done.16
  123.4 4.4 %collective-permute-start.17 = (bf16[128,1792]{1,0:T(8,128)(2,1)S(1)}, bf16[128,1792]{1,0:T(8,128)(2,1)S(1)}, u32[]{:S(2)}, u32[]{:S(2)}) collective-permute-start(bf16[128,1792]{1,0:T(8,128)(2,1)S(1)} %add.31), channel_id=1, source_target_pairs={{0,2},{1,3},{2,4},{3,5},{8,10},{9,11},{10,12},{11,13},{16,18},{17,... | collective-permute-start | bytes 1376264 | tf_op jit(solution)/shard_map/ppermute | solution.py:354
  127.9 0.7 collective-permute-start.19
  128.6 7.6 %feed_forward.5 = (bf16[128,1792]{1,0:T(8,128)(2,1)S(1)}, bf16[128,1792]{1,0:T(8,128)(2,1)S(1)}) custom-call(bf16[128,1792]{1,0:T(8,128)(2,1)S(1)} %copy-done.15, bf16[128,1792]{1,0:T(8,128)(2,1)S(1)} %copy-done.17, bf16[1792,608]{1,0:T(8,128)(2,1)S(1)} %copy.36.refs_1_.refs_2_, bf16[1792,608]{1,0:T(8,128)(2,1)} %copy.37.refs_2_.refs_3_, ...), custom_call_target="tpu_custom_call" | custom-call | flops 3347054592 | bytes 13074432 | tf_op jit(solution)/shard_map/feed_forward/pallas_call | solution.py:215
  136.3 7.1 %collective-permute-start.18 = (bf16[128,1792]{1,0:T(8,128)(2,1)S(1)}, bf16[128,1792]{1,0:T(8,128)(2,1)S(1)}, u32[]{:S(2)}, u32[]{:S(2)}) collective-permute-start(bf16[128,1792]{1,0:T(8,128)(2,1)S(1)} %add.32), channel_id=1, source_target_pairs={{0,2},{1,3},{2,4},{3,5},{4,6},{5,7},{8,10},{9,11},{10,12},{11,13},... | collective-permute-start | bytes 1376264 | tf_op jit(solution)/shard_map/ppermute | solution.py:354
  143.6 1.3 collective-permute-start.20
  145.0 5.8 %feed_forward.4.own_ref = bf16[128,1792]{1,0:T(8,128)(2,1)S(1)} custom-call(bf16[128,1792]{1,0:T(8,128)(2,1)S(1)} %copy-done.13, bf16[1792,608]{1,0:T(8,128)(2,1)S(1)} %copy.36.refs_1_.refs_2_, bf16[1792,608]{1,0:T(8,128)(2,1)S(1)} %copy-done.2, bf16[608,1792]{1,0:T(8,128)(2,1)S(1)} %copy-done.5, ...), custom_call_target="tpu_custom_call" | custom-call | flops 1673527296 | bytes 13074432 | tf_op jit(solution)/shard_map/feed_forward/pallas_call | solution.py:215
  150.7 0.7 collective-permute-done.18.left_ref
  151.5 4.9 %collective-permute-done.20.right_ref = bf16[128,1792]{1,0:T(8,128)(2,1)S(1)} collective-permute-done((bf16[128,1792]{1,0:T(8,128)(2,1)S(1)}, bf16[128,1792]{1,0:T(8,128)(2,1)S(1)}, u32[]{:S(2)}, u32[]{:S(2)}) %collective-permute-start.20) | collective-permute-done | bytes 458784 | tf_op jit(solution)/shard_map/ppermute | solution.py:354
  156.3 3.3 %copy-done.6 = bf16[1792,2304]{1,0:T(8,128)(2,1)S(1)} copy-done((bf16[1792,2304]{1,0:T(8,128)(2,1)S(1)}, bf16[1792,2304]{1,0:T(8,128)(2,1)}, u32[]{:S(2)}) %copy-start.6) | copy-done | bytes 8257560
  159.7 5.4 %next_projection.1 = (bf16[128,1792]{1,0:T(8,128)(2,1)}, bf16[128,2304]{1,0:T(8,128)(2,1)}) custom-call(bf16[128,1792]{1,0:T(8,128)(2,1)S(1)} %copy-done.19, bf16[128,1792]{1,0:T(8,128)(2,1)S(1)} %feed_forward.4.own_ref, bf16[128,1792]{1,0:T(8,128)(2,1)S(1)} %collective-permute-done.18.left_ref, bf16[128,1792]{1,0:T(8,128)(2,1)S(1)} %collective-permute-done.20.right_ref, ...), custom_call_target="tpu_custom_call" | custom-call | tf_op jit(solution)/shard_map/next_projection/pallas_call | solution.py:254
  (74 shorter events, 1.1 us)
Async XLA Ops:
  0.6 20.0 %copy-start = (f32[3,1792]{1,0:T(4,128)S(1)}, f32[3,1792]{1,0:T(4,128)}, u32[]{:S(2)}) copy-start(f32[3,1792]{1,0:T(4,128)} %param.21) | copy-start | bytes 64516
  0.6 1.0 copy-start.10
  1.7 0.8 copy-start.20
  2.5 0.8 copy-start.21
  4.4 25.0 %all-to-all-start = ((bf16[8,288,128]{2,1,0:T(8,128)(2,1)}), bf16[8,288,128]{2,1,0:T(8,128)(2,1)}, u32[]{:S(2)}, u32[]{:S(2)}) async-start(bf16[8,288,128]{2,1,0:T(8,128)(2,1)} %pack_heads.1), calls=%async_computation | async-start | bytes 1179648 | tf_op jit(solution)/shard_map/all_to_all | solution.py:347
  13.6 3.9 %copy-start.26 = (f32[1,2,273]{2,1,0:T(2,128)S(1)}, f32[1,2,273]{2,1,0:T(2,128)}, u32[]{:S(2)}) copy-start(f32[1,2,273]{2,1,0:T(2,128)} %param.23) | copy-start | bytes 6556
  13.6 4.1 %copy-start.22 = (f32[1,2,273,112]{3,1,2,0:T(2,128)S(1)}, f32[1,2,273,112]{3,1,2,0:T(2,128)}, u32[]{:S(2)}) copy-start(f32[1,2,273,112]{3,1,2,0:T(2,128)} %param.22) | copy-start | bytes 733828
  14.2 7.2 %copy-start.29 = (s32[4]{0:T(128)S(1)}, s32[4]{0:T(128)}, u32[]{:S(2)}) copy-start(s32[4]{0:T(128)} %param.24) | copy-start | bytes 52
  14.2 9.4 %copy-start.27 = (s32[1,4]{1,0:T(1,128)S(1)}, s32[1,4]{1,0:T(1,128)}, u32[]{:S(2)}) copy-start(s32[1,4]{1,0:T(1,128)} %param.26) | copy-start | bytes 52
  14.2 9.4 %copy-start.28 = (s32[1,4]{1,0:T(1,128)S(1)}, s32[1,4]{1,0:T(1,128)}, u32[]{:S(2)}) copy-start(s32[1,4]{1,0:T(1,128)} %param.25) | copy-start | bytes 52
  15.5 33.1 %collective-permute-start.3 = (bf16[2,448,608]{2,1,0:T(8,128)(2,1)}, bf16[2,448,608]{2,1,0:T(8,128)(2,1)S(1)}, u32[]{:S(2)}, u32[]{:S(2)}) collective-permute-start(bf16[2,448,608]{2,1,0:T(8,128)(2,1)} %pad_maximum_fusion), channel_id=1, source_target_pairs={{0,1},{1,0},{2,3},{3,2},{4,5},{5,4},{6,7},{7,6},{8,9},{9,8},{10,11... | collective-permute-start | bytes 3268616 | tf_op jit(solution)/shard_map/ppermute | solution.py:286
  17.8 32.4 %copy-start.3 = (bf16[608,1792]{1,0:T(8,128)(2,1)S(1)}, bf16[608,1792]{1,0:T(8,128)(2,1)}, u32[]{:S(2)}) copy-start(bf16[608,1792]{1,0:T(8,128)(2,1)} %refs_3_.6) | copy-start | bytes 6537220
  18.7 6.3 %collective-permute-start = (bf16[2,288,128]{2,1,0:T(8,128)(2,1)}, bf16[2,288,128]{2,1,0:T(8,128)(2,1)S(1)}, u32[]{:S(2)}, u32[]{:S(2)}) collective-permute-start(bf16[2,288,128]{2,1,0:T(8,128)(2,1)} %fusion.7), channel_id=1, source_target_pairs={{0,24},{8,16},{16,8},{24,0},{1,25},{9,17},{17,9},{25,1},{2,26},{10... | collective-permute-start | bytes 442376 | tf_op jit(solution)/shard_map/ppermute | solution.py:310
  18.7 9.6 %collective-permute-start.1 = (bf16[2,288,128]{2,1,0:T(8,128)(2,1)}, bf16[2,288,128]{2,1,0:T(8,128)(2,1)}, u32[]{:S(2)}, u32[]{:S(2)}) collective-permute-start(bf16[2,288,128]{2,1,0:T(8,128)(2,1)} %fusion.7), channel_id=1, source_target_pairs={{0,16},{8,24},{16,0},{24,8},{1,17},{9,25},{17,1},{25,9},{2,18},{10... | collective-permute-start | bytes 442376 | tf_op jit(solution)/shard_map/ppermute | solution.py:310
  20.2 8.1 %collective-permute-start.2 = (bf16[2,288,128]{2,1,0:T(8,128)(2,1)}, bf16[2,288,128]{2,1,0:T(8,128)(2,1)}, u32[]{:S(2)}, u32[]{:S(2)}) collective-permute-start(bf16[2,288,128]{2,1,0:T(8,128)(2,1)} %fusion.7), channel_id=1, source_target_pairs={{0,8},{8,0},{16,24},{24,16},{1,9},{9,1},{17,25},{25,17},{2,10},{10... | collective-permute-start | bytes 442376 | tf_op jit(solution)/shard_map/ppermute | solution.py:310
  25.0 3.3 %copy-start.23 = (bf16[2,288,128]{2,1,0:T(8,128)(2,1)}, bf16[2,288,128]{2,1,0:T(8,128)(2,1)S(1)}, u32[]{:S(2)}) copy-start(bf16[2,288,128]{2,1,0:T(8,128)(2,1)S(1)} %collective-permute-done) | copy-start | bytes 442372
  29.4 0.9 copy-start.9
  30.3 22.2 %copy-start.24 = (f32[1792]{0:T(1024)S(1)}, f32[1792]{0:T(1024)}, u32[]{:S(2)}) copy-start(f32[1792]{0:T(1024)} %param.28) | copy-start | bytes 21508
  34.4 0.8 copy-start.8
  35.2 17.9 %all-to-all-start.1 = ((bf16[8,224,128]{2,1,0:T(8,128)(2,1)}), bf16[8,224,128]{2,1,0:T(8,128)(2,1)}, u32[]{:S(2)}, u32[]{:S(2)}) async-start(bf16[8,224,128]{2,1,0:T(8,128)(2,1)} %copy-done.8), calls=%async_computation.1 | async-start | bytes 917504 | tf_op jit(solution)/shard_map/all_to_all | solution.py:349
  48.6 30.0 %collective-permute-start.5 = (bf16[2,448,608]{2,1,0:T(8,128)(2,1)S(1)}, bf16[2,448,608]{2,1,0:T(8,128)(2,1)}, u32[]{:S(2)}, u32[]{:S(2)}) collective-permute-start(bf16[2,448,608]{2,1,0:T(8,128)(2,1)S(1)} %collective-permute-done.3.refs_4_.refs_5_), channel_id=1, source_target_pairs={{0,16},{8,24},{16,0},{24,8},{1,17},{9,25},{17,1},{25,9},{2,18},{10... | collective-permute-start | bytes 3268616 | tf_op jit(solution)/shard_map/ppermute | solution.py:291
  51.0 15.8 %collective-permute-start.4 = (bf16[160,1792]{1,0:T(8,128)(2,1)}, bf16[160,1792]{1,0:T(8,128)(2,1)}, u32[]{:S(2)}, u32[]{:S(2)}) collective-permute-start(bf16[160,1792]{1,0:T(8,128)(2,1)} %pad_dynamic-slice_fusion), channel_id=1, source_target_pairs={{0,1},{1,0},{2,3},{3,2},{4,5},{5,4},{6,7},{7,6},{8,9},{9,8},{10,11... | collective-permute-start | bytes 1720328 | tf_op jit(solution)/shard_map/ppermute | solution.py:286
  53.1 2.8 %copy-start.7 = (bf16[1792,1792]{1,0:T(8,128)(2,1)S(1)}, bf16[1792,1792]{1,0:T(8,128)(2,1)}, u32[]{:S(2)}) copy-start(bf16[1792,1792]{1,0:T(8,128)(2,1)} %w_ref.2) | copy-start | bytes 19267588
  55.9 1.0 copy-start.11
  60.9 0.8 copy-start.18
  61.6 11.4 %collective-permute-start.11 = (bf16[128,1792]{1,0:T(8,128)(2,1)S(1)}, bf16[128,1792]{1,0:T(8,128)(2,1)S(1)}, u32[]{:S(2)}, u32[]{:S(2)}) collective-permute-start(bf16[128,1792]{1,0:T(8,128)(2,1)S(1)} %get-tuple-element.7.refs_0_), channel_id=1, source_target_pairs={{0,2},{1,3},{2,4},{3,5},{4,6},{5,7},{8,10},{9,11},{10,12},{11,13},... | collective-permute-start | bytes 1376264 | tf_op jit(solution)/shard_map/ppermute | solution.py:354
  64.6 12.6 %collective-permute-start.12 = (bf16[128,1792]{1,0:T(8,128)(2,1)S(1)}, bf16[128,1792]{1,0:T(8,128)(2,1)S(1)}, u32[]{:S(2)}, u32[]{:S(2)}) collective-permute-start(bf16[128,1792]{1,0:T(8,128)(2,1)S(1)} %get-tuple-element.7.refs_0_), channel_id=1, source_target_pairs={{6,4},{7,5},{4,2},{5,3},{2,0},{3,1},{14,12},{15,13},{12,10},{13,11... | collective-permute-start | bytes 1376264 | tf_op jit(solution)/shard_map/ppermute | solution.py:354
  65.9 0.8 copy-start.12
  66.7 20.0 %collective-permute-start.6 = (bf16[160,1792]{1,0:T(8,128)(2,1)}, bf16[160,1792]{1,0:T(8,128)(2,1)}, u32[]{:S(2)}, u32[]{:S(2)}) collective-permute-start(bf16[160,1792]{1,0:T(8,128)(2,1)} %collective-permute-done.4.refs_5_.refs_6_), channel_id=1, source_target_pairs={{0,16},{8,24},{16,0},{24,8},{1,17},{9,25},{17,1},{25,9},{2,18},{10... | collective-permute-start | bytes 1720328 | tf_op jit(solution)/shard_map/ppermute | solution.py:291
  73.1 16.8 %copy-start.14 = (bf16[128,1792]{1,0:T(8,128)(2,1)}, bf16[128,1792]{1,0:T(8,128)(2,1)S(1)}, u32[]{:S(2)}) copy-start(bf16[128,1792]{1,0:T(8,128)(2,1)S(1)} %collective-permute-done.11.refs_0_) | copy-start | bytes 1376260
  73.1 13.7 %collective-permute-start.13 = (bf16[128,1792]{1,0:T(8,128)(2,1)S(1)}, bf16[128,1792]{1,0:T(8,128)(2,1)S(1)}, u32[]{:S(2)}, u32[]{:S(2)}) collective-permute-start(bf16[128,1792]{1,0:T(8,128)(2,1)S(1)} %collective-permute-done.11.refs_0_), channel_id=1, source_target_pairs={{2,4},{3,5},{4,6},{5,7},{10,12},{11,13},{12,14},{13,15},{18,20},{1... | collective-permute-start | bytes 1376264 | tf_op jit(solution)/shard_map/ppermute | solution.py:354
  77.2 12.6 %copy-start.16 = (bf16[128,1792]{1,0:T(8,128)(2,1)}, bf16[128,1792]{1,0:T(8,128)(2,1)S(1)}, u32[]{:S(2)}) copy-start(bf16[128,1792]{1,0:T(8,128)(2,1)S(1)} %collective-permute-done.12.refs_1_) | copy-start | bytes 1376260
  77.2 11.8 %collective-permute-start.14 = (bf16[128,1792]{1,0:T(8,128)(2,1)S(1)}, bf16[128,1792]{1,0:T(8,128)(2,1)S(1)}, u32[]{:S(2)}, u32[]{:S(2)}) collective-permute-start(bf16[128,1792]{1,0:T(8,128)(2,1)S(1)} %collective-permute-done.12.refs_1_), channel_id=1, source_target_pairs={{4,2},{5,3},{2,0},{3,1},{12,10},{13,11},{10,8},{11,9},{20,18},{21,... | collective-permute-start | bytes 1376264 | tf_op jit(solution)/shard_map/ppermute | solution.py:354
  78.5 20.1 %collective-permute-start.7 = (bf16[2,448,608]{2,1,0:T(8,128)(2,1)S(1)}, bf16[2,448,608]{2,1,0:T(8,128)(2,1)}, u32[]{:S(2)}, u32[]{:S(2)}) collective-permute-start(bf16[2,448,608]{2,1,0:T(8,128)(2,1)S(1)} %collective-permute-done.3.refs_4_.refs_5_), channel_id=1, source_target_pairs={{0,8},{8,0},{16,24},{24,16},{1,9},{9,1},{17,25},{25,17},{2,10},{10... | collective-permute-start | bytes 3268616 | tf_op jit(solution)/shard_map/ppermute | solution.py:291
  78.6 24.9 %collective-permute-start.9 = (bf16[2,448,608]{2,1,0:T(8,128)(2,1)}, bf16[2,448,608]{2,1,0:T(8,128)(2,1)}, u32[]{:S(2)}, u32[]{:S(2)}) collective-permute-start(bf16[2,448,608]{2,1,0:T(8,128)(2,1)} %collective-permute-done.5.refs_6_.refs_7_), channel_id=1, source_target_pairs={{0,8},{8,0},{16,24},{24,16},{1,9},{9,1},{17,25},{25,17},{2,10},{10... | collective-permute-start | bytes 3268616 | tf_op jit(solution)/shard_map/ppermute | solution.py:291
  86.7 11.9 %collective-permute-start.8 = (bf16[160,1792]{1,0:T(8,128)(2,1)}, bf16[160,1792]{1,0:T(8,128)(2,1)}, u32[]{:S(2)}, u32[]{:S(2)}) collective-permute-start(bf16[160,1792]{1,0:T(8,128)(2,1)} %collective-permute-done.4.refs_5_.refs_6_), channel_id=1, source_target_pairs={{0,8},{8,0},{16,24},{24,16},{1,9},{9,1},{17,25},{25,17},{2,10},{10... | collective-permute-start | bytes 1720328 | tf_op jit(solution)/shard_map/ppermute | solution.py:291
  86.8 11.9 %collective-permute-start.10 = (bf16[160,1792]{1,0:T(8,128)(2,1)}, bf16[160,1792]{1,0:T(8,128)(2,1)}, u32[]{:S(2)}, u32[]{:S(2)}) collective-permute-start(bf16[160,1792]{1,0:T(8,128)(2,1)} %collective-permute-done.6.refs_7_.refs_8_), channel_id=1, source_target_pairs={{0,8},{8,0},{16,24},{24,16},{1,9},{9,1},{17,25},{25,17},{2,10},{10... | collective-permute-start | bytes 1720328 | tf_op jit(solution)/shard_map/ppermute | solution.py:291
  89.8 13.7 %collective-permute-start.15 = (bf16[128,1792]{1,0:T(8,128)(2,1)}, bf16[128,1792]{1,0:T(8,128)(2,1)}, u32[]{:S(2)}, u32[]{:S(2)}) collective-permute-start(bf16[128,1792]{1,0:T(8,128)(2,1)} %broadcast_select_fusion.refs_0_), channel_id=1, source_target_pairs={{4,6},{5,7},{2,0},{3,1},{12,14},{13,15},{10,8},{11,9},{20,22},{21,... | collective-permute-start | bytes 1376264 | tf_op jit(solution)/shard_map/ppermute | solution.py:354
  103.5 1.6 copy-start.1
  105.2 1.6 copy-start.4
  113.6 15.0 %copy-start.15 = (bf16[128,1792]{1,0:T(8,128)(2,1)S(1)}, bf16[128,1792]{1,0:T(8,128)(2,1)}, u32[]{:S(2)}) copy-start(bf16[128,1792]{1,0:T(8,128)(2,1)} %copy-done.14) | copy-start | bytes 1376260
  113.6 15.0 %copy-start.17 = (bf16[128,1792]{1,0:T(8,128)(2,1)S(1)}, bf16[128,1792]{1,0:T(8,128)(2,1)}, u32[]{:S(2)}) copy-start(bf16[128,1792]{1,0:T(8,128)(2,1)} %copy-done.16) | copy-start | bytes 1376260
  113.6 9.8 %collective-permute-start.16 = (bf16[128,1792]{1,0:T(8,128)(2,1)S(1)}, bf16[128,1792]{1,0:T(8,128)(2,1)S(1)}, u32[]{:S(2)}, u32[]{:S(2)}) collective-permute-start(bf16[128,1792]{1,0:T(8,128)(2,1)S(1)} %feed_forward.7), channel_id=1, source_target_pairs={{0,2},{1,3},{6,4},{7,5},{8,10},{9,11},{14,12},{15,13},{16,18},{17,... | collective-permute-start | bytes 1376264 | tf_op jit(solution)/shard_map/ppermute | solution.py:354
  123.4 12.8 %collective-permute-start.17 = (bf16[128,1792]{1,0:T(8,128)(2,1)S(1)}, bf16[128,1792]{1,0:T(8,128)(2,1)S(1)}, u32[]{:S(2)}, u32[]{:S(2)}) collective-permute-start(bf16[128,1792]{1,0:T(8,128)(2,1)S(1)} %add.31), channel_id=1, source_target_pairs={{0,2},{1,3},{2,4},{3,5},{8,10},{9,11},{10,12},{11,13},{16,18},{17,... | collective-permute-start | bytes 1376264 | tf_op jit(solution)/shard_map/ppermute | solution.py:354
  127.9 15.6 %collective-permute-start.19 = (bf16[128,1792]{1,0:T(8,128)(2,1)S(1)}, bf16[128,1792]{1,0:T(8,128)(2,1)S(1)}, u32[]{:S(2)}, u32[]{:S(2)}) collective-permute-start(bf16[128,1792]{1,0:T(8,128)(2,1)S(1)} %add.31), channel_id=1, source_target_pairs={{6,4},{7,5},{4,2},{5,3},{14,12},{15,13},{12,10},{13,11},{22,20},{2... | collective-permute-start | bytes 1376264 | tf_op jit(solution)/shard_map/ppermute | solution.py:354
  128.6 16.3 %copy-start.25 = (f32[1792]{0:T(1024)S(1)}, f32[1792]{0:T(1024)}, u32[]{:S(2)}) copy-start(f32[1792]{0:T(1024)} %param.32) | copy-start | bytes 21508
  128.6 16.3 %copy-start.5 = (bf16[608,1792]{1,0:T(8,128)(2,1)S(1)}, bf16[608,1792]{1,0:T(8,128)(2,1)}, u32[]{:S(2)}) copy-start(bf16[608,1792]{1,0:T(8,128)(2,1)} %refs_3_.6) | copy-start | bytes 6537220
  136.2 8.7 %copy-start.2 = (bf16[1792,608]{1,0:T(8,128)(2,1)S(1)}, bf16[1792,608]{1,0:T(8,128)(2,1)}, u32[]{:S(2)}) copy-start(bf16[1792,608]{1,0:T(8,128)(2,1)} %copy.37.refs_2_.refs_3_) | copy-start | bytes 6537220
  136.2 8.7 %copy-start.13 = (bf16[128,1792]{1,0:T(8,128)(2,1)S(1)}, bf16[128,1792]{1,0:T(8,128)(2,1)}, u32[]{:S(2)}) copy-start(bf16[128,1792]{1,0:T(8,128)(2,1)} %copy-done.12) | copy-start | bytes 1376260
  136.3 15.1 %collective-permute-start.18 = (bf16[128,1792]{1,0:T(8,128)(2,1)S(1)}, bf16[128,1792]{1,0:T(8,128)(2,1)S(1)}, u32[]{:S(2)}, u32[]{:S(2)}) collective-permute-start(bf16[128,1792]{1,0:T(8,128)(2,1)S(1)} %add.32), channel_id=1, source_target_pairs={{0,2},{1,3},{2,4},{3,5},{4,6},{5,7},{8,10},{9,11},{10,12},{11,13},... | collective-permute-start | bytes 1376264 | tf_op jit(solution)/shard_map/ppermute | solution.py:354
  143.6 12.7 %collective-permute-start.20 = (bf16[128,1792]{1,0:T(8,128)(2,1)S(1)}, bf16[128,1792]{1,0:T(8,128)(2,1)S(1)}, u32[]{:S(2)}, u32[]{:S(2)}) collective-permute-start(bf16[128,1792]{1,0:T(8,128)(2,1)S(1)} %add.33), channel_id=1, source_target_pairs={{6,4},{7,5},{4,2},{5,3},{2,0},{3,1},{14,12},{15,13},{12,10},{13,11... | collective-permute-start | bytes 1376264 | tf_op jit(solution)/shard_map/ppermute | solution.py:354
  145.0 11.4 %copy-start.19 = (bf16[128,1792]{1,0:T(8,128)(2,1)S(1)}, bf16[128,1792]{1,0:T(8,128)(2,1)}, u32[]{:S(2)}) copy-start(bf16[128,1792]{1,0:T(8,128)(2,1)} %copy-done.18) | copy-start | bytes 1376260
  156.3 3.3 %copy-start.6 = (bf16[1792,2304]{1,0:T(8,128)(2,1)S(1)}, bf16[1792,2304]{1,0:T(8,128)(2,1)}, u32[]{:S(2)}) copy-start(bf16[1792,2304]{1,0:T(8,128)(2,1)} %w_ref.3) | copy-start | bytes 24772612

commit v2 on v1

v2 whole, which is shorter than its diff:
```python
import functools
import math

import jax
import jax.numpy as jnp
from jax import lax
from jax.experimental import pallas as pl
from jax.experimental.pallas import tpu as pltpu
from jax.sharding import PartitionSpec as P

EPSILON = 1e-05
DEPTH = 4
TURNED = (((1,), (1,)), ((), ()))
MIB = 1 << 20
ACROSS = (((0,), (0,)), ((), ()))
PLAIN = (((1,), (0,)), ((), ()))
F32 = jnp.float32
BF16 = jnp.bfloat16
VMEM = pltpu.VMEM


def vmem():
    return pl.BlockSpec(memory_space=VMEM)


def dot(a, b, dims=PLAIN):
    return lax.dot_general(a, b, dims, preferred_element_type=F32)


def pack_kernel(q_ref, k_ref, v_ref, out_ref):
    count = out_ref.shape[0]
    at = 0
    for ref in (q_ref, k_ref, v_ref):
        turned = ref[...].T
        part = turned.shape[0] // count
        for m in range(count):
            out_ref[m, at : at + part, :] = turned[m * part : (m + 1) * part, :]
        at += part


def pack(q, k, v, count):
    rows = (q.shape[1] + k.shape[1] + v.shape[1]) // count
    return pl.pallas_call(
        pack_kernel,
        out_shape=jax.ShapeDtypeStruct((count, rows, q.shape[0]), BF16),
        in_specs=[vmem()] * 3,
        out_specs=vmem(),
        compiler_params=pltpu.CompilerParams(vmem_limit_bytes=24 * MIB),
        name="pack_heads",
    )(q, k, v)


def attention_kernel(heads, fd, hd, turns, *refs):
    lengths_ref, flags_ref, owner_ref, x_ref, conv_ref = refs[:5]
    states = refs[5 : 5 + len(turns)]
    out_ref, turned, vconv, feats, taps, cached = refs[5 + len(turns) :]
    blocks, rows, local = x_ref.shape
    tokens = blocks * local
    values_at = 2 * heads * fd
    tile = 256 if tokens % 256 == 0 else local
    slot = lax.axis_index("req")
    owner = owner_ref[slot]
    for turn, state in zip(turns, states):

        @pl.when((slot ^ turn) == owner)
        def _():
            cached[...] = state[...]

    for m in range(blocks):
        turned[:, m * local : (m + 1) * local] = x_ref[m]

    position = lax.broadcasted_iota(jnp.int32, (1, tokens), 1)
    start = jnp.zeros((1, tokens), jnp.int32)
    flag = jnp.zeros((1, tokens), F32) + flags_ref[0, 0].astype(F32)
    boundary = jnp.int32(0)
    for r in range(1, lengths_ref.shape[1]):
        boundary = boundary + lengths_ref[0, r - 1]
        reached = position >= boundary
        start = jnp.where(reached, boundary, start)
        flag = jnp.where(reached, flags_ref[0, r].astype(F32), flag)

    count = conv_ref.shape[0]
    spare = jnp.zeros((8 - count, conv_ref.shape[1]), F32)
    taps[...] = jnp.concatenate([conv_ref[...], spare], axis=0).T
    mine = pl.multiple_of(lax.axis_index("mlp") * heads * hd, 8)
    weights = taps[pl.ds(mine, heads * hd), :]
    values = turned[values_at:, :].astype(F32)
    total = weights[:, 0:1] * values
    for tap in range(1, count):
        earlier = pltpu.roll(values, tap, 1)
        total = total + weights[:, tap : tap + 1] * jnp.where(position - tap >= start, earlier, 0.0)
    vconv[...] = total.astype(BF16)

    for h in range(heads):
        query = turned[h * fd : (h + 1) * fd, :]
        wide = query.astype(F32)
        scaled = wide * (1.0 / math.sqrt(2.0 * fd))
        for a in range(fd):
            feats[a * fd : (a + 1) * fd, :] = (wide[a : a + 1, :] * scaled).astype(BF16)
        feats[fd * fd : fd * fd + fd, :] = (wide * fd ** (-0.25)).astype(BF16)
        ones = lax.broadcasted_iota(jnp.int32, (16, tokens), 0) == 0
        feats[fd * fd + fd :, :] = ones.astype(F32).astype(BF16)
        key = turned[(heads + h) * fd : (heads + h + 1) * fd, :]
        for first in range(0, tokens, tile):
            last = first + tile
            old = dot(cached[h], feats[:, first:last], ACROSS)
            score = dot(key[:, :last], query[:, first:last], ACROSS) * (fd**-0.5) + 1.0
            score = score * score * 0.5 + 0.5
            key_at = lax.broadcasted_iota(jnp.int32, (last, tile), 0)
            visible = (key_at >= start[:, first:last]) & (key_at <= position[:, first:last])
            score = jnp.where(visible, score, 0.0)
            den = jnp.sum(score, axis=0, keepdims=True) + flag[:, first:last] * old[hd : hd + 1, :]
            num = dot(vconv[h * hd : (h + 1) * hd, :last], score.astype(BF16))
            num = num + flag[:, first:last] * old[:hd, :]
            result = (num / den).astype(BF16)
            for at in range(first, last, local):
                out_ref[at // local, h * hd : (h + 1) * hd, :] = result[:, at - first : at - first + local]


def attention(lengths, flags, owner, x, conv, states, heads, fd, hd):
    blocks, rows, local = x.shape
    tokens = blocks * local
    turns = tuple(turn for turn, _ in states)
    arrays = [state for _, state in states]
    return pl.pallas_call(
        functools.partial(attention_kernel, heads, fd, hd, turns),
        out_shape=jax.ShapeDtypeStruct((blocks, heads * hd, local), BF16),
        in_specs=[pl.BlockSpec(memory_space=pltpu.SMEM)] * 3 + [vmem()] * (2 + len(arrays)),
        out_specs=vmem(),
        scratch_shapes=[
            VMEM((rows, tokens), BF16),
            VMEM((heads * hd, tokens), BF16),
            VMEM((arrays[0].shape[1], tokens), BF16),
            VMEM((conv.shape[1], 8), F32),
            VMEM(arrays[0].shape, BF16),
        ],
        compiler_params=pltpu.CompilerParams(vmem_limit_bytes=24 * MIB),
        name="attention",
    )(lengths, flags, owner, x, conv, *arrays)


def rms(rows, gain):
    return rows * lax.rsqrt(jnp.mean(rows * rows, axis=-1, keepdims=True) + EPSILON) * gain


def project_kernel(tile, att_ref, w_ref, res_ref, gain_ref, sum_ref, normed_ref, rows):
    step = pl.program_id(0)

    @pl.when(step == 0)
    def _():
        rows[...] = att_ref[...].T

    at = pl.ds(pl.multiple_of(step * tile, tile), tile)
    projected = dot(rows[...], w_ref[...])
    sum_ref[:, at] = (res_ref[:, at].astype(F32) + projected).astype(BF16)

    @pl.when(step == pl.num_programs(0) - 1)
    def _():
        normed_ref[...] = rms(sum_ref[...].astype(F32), gain_ref[...]).astype(BF16)


def project(att, w, residual, gain):
    depth, rows = att.shape
    width = w.shape[1]
    tile = 256
    whole = lambda shape: pl.BlockSpec(shape, lambda i: (0, 0))
    return pl.pallas_call(
        functools.partial(project_kernel, tile),
        grid=(width // tile,),
        out_shape=[jax.ShapeDtypeStruct((rows, width), BF16)] * 2,
        in_specs=[
            whole((depth, rows)),
            pl.BlockSpec((depth, tile), lambda i: (0, i)),
            whole((rows, width)),
            whole((1, width)),
        ],
        out_specs=[whole((rows, width))] * 2,
        scratch_shapes=[VMEM((rows, depth), BF16)],
        compiler_params=pltpu.CompilerParams(vmem_limit_bytes=24 * MIB),
        name="out_projection",
    )(att, w, residual, gain)


def mlp_kernel(inputs, *refs):
    xs, weights, outs = refs[:inputs], refs[inputs:-inputs], refs[-inputs:]
    x = xs[0][...] if inputs == 1 else jnp.concatenate([ref[...] for ref in xs], axis=0)
    total = None
    for at in range(0, len(weights), 3):
        gate_ref, up_ref, down_ref = weights[at : at + 3]
        gate = dot(x, gate_ref[...], TURNED)
        up = dot(x, up_ref[...], TURNED)
        hidden = (gate * jax.nn.sigmoid(gate) * up).astype(BF16)
        part = dot(hidden, down_ref[...])
        total = part if total is None else total + part
    local = xs[0].shape[0]
    for i, out in enumerate(outs):
        out[...] = total[i * local : (i + 1) * local].astype(BF16)


def mlp(xs, weights):
    rows, deep = xs[0].shape
    units = sum(w.shape[0] for w in weights) // 3
    return pl.pallas_call(
        functools.partial(mlp_kernel, len(xs)),
        out_shape=[jax.ShapeDtypeStruct((rows, deep), BF16)] * len(xs),
        in_specs=[vmem()] * (len(xs) + len(weights)),
        out_specs=[vmem()] * len(xs),
        compiler_params=pltpu.CompilerParams(vmem_limit_bytes=30 * MIB),
        cost_estimate=pl.CostEstimate(
            flops=6 * len(xs) * rows * deep * units,
            bytes_accessed=6 * deep * units,
            transcendentals=0,
        ),
        name="feed_forward",
    )(*xs, *weights)


def next_kernel(count, *refs):
    first_ref, parts = refs[0], refs[1 : 1 + count]
    gain_ref, w_ref, sum_ref, out_ref, normed = refs[1 + count :]
    step = pl.program_id(0)

    @pl.when(step == 0)
    def _():
        extra = sum(ref[...].astype(F32) for ref in parts)
        second = (first_ref[...].astype(F32) + extra).astype(BF16)
        sum_ref[...] = second
        normed[...] = rms(second.astype(F32), gain_ref[...]).astype(BF16)

    out_ref[...] = dot(normed[...], w_ref[...]).astype(BF16)


def next_projection(first, parts, gain, w):
    rows, deep = first.shape
    width = w.shape[1]
    tile = 256
    whole = lambda shape: pl.BlockSpec(shape, lambda i: (0, 0))
    return pl.pallas_call(
        functools.partial(next_kernel, len(parts)),
        grid=(width // tile,),
        out_shape=[
            jax.ShapeDtypeStruct((rows, deep), BF16),
            jax.ShapeDtypeStruct((rows, width), BF16),
        ],
        in_specs=[whole((rows, deep))] * (1 + len(parts))
        + [whole((1, deep)), pl.BlockSpec((deep, tile), lambda i: (0, i))],
        out_specs=[whole((rows, deep)), pl.BlockSpec((rows, tile), lambda i: (0, i))],
        scratch_shapes=[VMEM((rows, deep), BF16)],
        compiler_params=pltpu.CompilerParams(vmem_limit_bytes=24 * MIB),
        name="next_projection",
    )(first, *parts, gain, w)


def portion_kernel(gate, up, down, gate_out, up_out, down_out, sems):
    sharer = lax.axis_index("req")
    tall = gate_out.shape[0]
    wanted = sharer * tall
    first = jnp.minimum(wanted, gate.shape[0] - tall)
    rows = pl.ds(pl.multiple_of(first, 16), tall)
    copies = [
        pltpu.make_async_copy(ref.at[rows], out, sems.at[i])
        for i, (ref, out) in enumerate(((gate, gate_out), (up, up_out), (down, down_out)))
    ]
    for copy in copies:
        copy.start()
    for copy in copies:
        copy.wait()

    @pl.when(wanted > first)
    def _():
        spare = first + lax.broadcasted_iota(jnp.int32, (tall, 1), 0) < wanted
        for out in (gate_out, up_out, down_out):
            out[...] = jnp.where(spare, 0.0, out[...].astype(F32)).astype(BF16)


def portion(weights, sharers):
    units, deep = weights[0].shape
    tall = -(-units // (16 * sharers)) * 16
    return pl.pallas_call(
        portion_kernel,
        out_shape=[jax.ShapeDtypeStruct((tall, deep), BF16)] * 3,
        in_specs=[pl.BlockSpec(memory_space=pl.ANY)] * 3,
        out_specs=[vmem()] * 3,
        scratch_shapes=[pltpu.SemaphoreType.DMA((3,))],
        compiler_params=pltpu.CompilerParams(vmem_limit_bytes=16 * MIB),
        name="weight_share",
    )(*weights)


def partner_weights(mine, width):
    sharers = lax.axis_size("req")
    route = [(z * width + y, (z ^ 1) * width + y) for z in range(DEPTH) for y in range(width)]
    fetched = []
    for part in mine:
        if fetched:
            part, _ = lax.optimization_barrier((part, fetched[-1]))
        fetched.append(lax.ppermute(part, "mlp", route))
    whole = []
    for part in fetched:
        held = [part]
        bit = sharers // 2
        while bit:
            swap = [(i, i ^ bit) for i in range(sharers)]
            held += [lax.ppermute(piece, "req", swap) for piece in held]
            bit //= 2
        whole.append(jnp.concatenate(held, axis=0))
    return whole


def cached_state(prefix_state, prefix_norm, fd):
    heads, feats, hd = prefix_state.shape[1:]
    both = jnp.concatenate([prefix_state[0], prefix_norm[0][:, :, None]], axis=2).astype(BF16)
    ordered = jnp.concatenate([both[:, 1 + fd :], both[:, 1 : 1 + fd], both[:, :1]], axis=1)
    packed = jnp.pad(ordered, ((0, 0), (0, 15), (0, 128 - hd - 1)))
    return packed


def spread_state(packed):
    slots = lax.axis_size("req")
    states = [(0, packed)]
    for turn in range(1, slots):
        states.append((turn, lax.ppermute(packed, "req", [(i, i ^ turn) for i in range(slots)])))
    return states


def shards(
    residual_in,
    query_in,
    key_in,
    values_in,
    conv_weight,
    prefix_state,
    prefix_norm,
    prefix_owner,
    lengths,
    old_flags,
    out_weight,
    mlp_gain,
    gate_weight,
    up_weight,
    down_weight,
    next_gain,
    qkv_weight,
):
    mlp_count = lax.axis_size("mlp")
    width = mlp_count // DEPTH
    heads = prefix_state.shape[1]
    hd = values_in.shape[1] // (heads * mlp_count)
    fd = query_in.shape[1] // (heads * mlp_count)
    own = [gate_weight.T, up_weight.T, down_weight]

    packed = cached_state(prefix_state, prefix_norm, fd)
    share = portion(own, lax.axis_size("req"))
    query_in, packed, *share = lax.optimization_barrier((query_in, packed, *share))
    states = spread_state(packed)
    by_head = lax.all_to_all(pack(query_in, key_in, values_in, mlp_count), "mlp", 0, 0, tiled=True)
    weights = own + partner_weights(share, width)
    attended = attention(
        lengths, old_flags, prefix_owner, by_head, conv_weight, states, heads, fd, hd
    )
    by_row = lax.all_to_all(attended, "mlp", 0, 0, tiled=True)
    by_row = by_row.reshape(mlp_count * heads * hd, by_row.shape[2])
    first_sum, normed = project(by_row, out_weight, residual_in, mlp_gain[None])

    places = [(z, y) for z in range(DEPTH) for y in range(width)]

    def across(data):
        return lax.ppermute(data, "mlp", [(z * width + y, (z ^ 2) * width + y) for z, y in places])

    def beside(data, turn):
        return lax.ppermute(
            data, "mlp", [(z * width + y, z * width + (y + turn) % width) for z, y in places]
        )

    turns = range(1, width)
    far = across(normed)
    near = [beside(normed, turn) for turn in turns]
    part_own, *part_near = mlp([normed, *near], weights)
    far_near = [beside(far, turn) for turn in turns]
    (part_far,) = mlp([far], weights)
    part_far_near = mlp(far_near, weights)
    for turn, part in zip(turns, part_far_near):
        part_far = part_far.astype(F32) + beside(part, -turn).astype(F32)
    back = across(part_far.astype(BF16))
    near_back = [beside(part, -turn) for turn, part in zip(turns, part_near)]
    parts = [part_own, back, *near_back]
    return next_projection(first_sum, parts, next_gain[None], qkv_weight)


def solution(mesh):
    rows = P(("req", "mlp"), None)
    placed = (
        rows,
        rows,
        rows,
        rows,
        P(),
        P("req", "mlp", None, None),
        P("req", "mlp", None),
        P(),
        P("req", None),
        P("req", None),
        P(),
        P(),
        P(None, "mlp"),
        P(None, "mlp"),
        P("mlp", None),
        P(),
        P(),
    )
    return jax.shard_map(
        shards, mesh=mesh, in_specs=placed, out_specs=(rows, rows), check_vma=False
    )
```

time: 166 us -> 181 us (1.090)
  waiting for transfers between devices: 44.8 us -> 85.6 us
  Pallas kernels: 41.3 us -> 32.4 us
  starting transfers between devices: 42.8 us -> 34.8 us
  local copies, waits for them, and re-layouts: 29 us -> 25.5 us
  other arithmetic: 4.37 us -> 1.08 us
  between operations: 2.77 us -> 0.91 us
    ppermute x21, waiting for transfers between devices: 44.2 us -> 85.6 us  [the longest x2 29.3 us: across(): lax.ppermute(data, 'mlp', [(z * width + y, (z ^ 2) * width + y) for z, y...]
    ppermute x21, starting transfers between devices: 31 us -> 21.5 us  [the longest x9 6.87 us: partner_weights(): held += [lax.ppermute(piece, 'req', swap) for piece in held]]
    pallas_call x6, Pallas kernels: 36.3 us -> 28.4 us  [the longest x3 17.3 us: mlp(): pl.pallas_call(functools.partial(mlp_kernel, len(xs)), out_shape=[jax.Sha...]
    dynamic_slice x6 -> x0, local copies, waits for them, and re-layouts: 4.02 us -> none  [the longest x3 2.54 us: side_weights(): lax.dynamic_slice_in_dim(w, me * deep, deep, 0)]
    all_to_all x1, starting transfers between devices: 4.54 us -> 8.52 us  [shards(): by_row = lax.all_to_all(attended, 'mlp', 0, 0, tiled=True)]
    concatenate x0 -> x3, local copies, waits for them, and re-layouts: none -> 3.06 us  [partner_weights(): whole.append(jnp.concatenate(held, axis=0))]
    unnamed x64 -> x54, local copies, waits for them, and re-layouts: 24.8 us -> 22.3 us
    all_to_all x1, starting transfers between devices: 7.28 us -> 4.82 us  [shards(): lax.all_to_all(pack(query_in, key_in, values_in, mlp_count), 'mlp', 0, 0,...]
  transfers between devices with their start and end apart: 23 -> 23, of which waited for: 12 -> 8; matrix products, arithmetic and copies ran while one was open for 10% -> 8% of each run, Pallas kernels for 17% -> 14%
where the time goes in v2:
time: 181 us; the launch traced here: 180 us
  waiting for transfers between devices  85.6 us (47%)
  starting transfers between devices  34.8 us (19%)
  Pallas kernels  32.4 us (18%)
  local copies, waits for them, and re-layouts  25.5 us (14%)
    ppermute x2, waiting for transfers between devices, across(): lax.ppermute(data, 'mlp', [(z * width + y, (z ^ 2) * width + y) for z, y...  29.3 us
    ppermute x3, waiting for transfers between devices, partner_weights(): fetched.append(lax.ppermute(part, 'mlp', route))  24.9 us
    unnamed x54, local copies, waits for them, and re-layouts  22.3 us
    pallas_call x3, Pallas kernels, mlp(): pl.pallas_call(functools.partial(mlp_kernel, len(xs)), out_shape=[jax.Sha...  17.3 us
    ppermute x3, waiting for transfers between devices, spread_state(): lax.ppermute(packed, 'req', [(i, i ^ turn) for i in range(slots)])  16.7 us
    ppermute x4, waiting for transfers between devices, beside(): lax.ppermute(data, 'mlp', [(z * width + y, z * width + (y + turn) % width...  14.7 us
    all_to_all x1, starting transfers between devices, shards(): by_row = lax.all_to_all(attended, 'mlp', 0, 0, tiled=True)  8.52 us
    ppermute x9, starting transfers between devices, partner_weights(): held += [lax.ppermute(piece, 'req', swap) for piece in held]  6.87 us
  transfers between devices with their start and end apart: 23, of which 8 were waited for; matrix products, arithmetic and copies ran while one was open for 8% of the time, Pallas kernels for 14%

profile of v2, /device:TPU:0, one launch (start us, length us, event | category | flops | bytes accessed | tf_op | source)
XLA Modules:
  0.0 180.4 jit_solution(5850906559879441439)
XLA Ops:
  0.6 0.7 convert_bitcast_fusion
  1.3 0.2 copy.21
  1.5 1.0 copy.25
  2.5 0.1 slice_maximum_fusion
  2.6 0.1 fusion.13
  2.7 0.1 fusion.7.refs_5_
  2.8 1.6 copy-done
  4.4 1.6 copy-done.2
  6.0 1.6 copy-done.4
  7.6 1.1 weight_share.1
  8.8 0.8 copy-done.17
  9.6 0.0 copy-start.16
  9.6 3.1 %collective-permute-start.4 = (bf16[160,1792]{1,0:T(8,128)(2,1)S(1)}, bf16[160,1792]{1,0:T(8,128)(2,1)}, u32[]{:S(2)}, u32[]{:S(2)}) collective-permute-start(bf16[160,1792]{1,0:T(8,128)(2,1)S(1)} %get-tuple-element.23), channel_id=1, source_target_pairs={{0,2},{1,3},{2,0},{3,1},{4,6},{5,7},{6,4},{7,5},{8,10},{9,11},{10,... | collective-permute-start | bytes 1720328 | tf_op jit(solution)/shard_map/ppermute | solution.py:297
  12.7 1.0 pack_heads.1
  13.7 4.8 %all-to-all-start = ((bf16[8,288,128]{2,1,0:T(8,128)(2,1)}), bf16[8,288,128]{2,1,0:T(8,128)(2,1)S(1)}, u32[]{:S(2)}, u32[]{:S(2)}) async-start(bf16[8,288,128]{2,1,0:T(8,128)(2,1)} %pack_heads.1), calls=%async_computation | async-start | bytes 1179648 | tf_op jit(solution)/shard_map/all_to_all | solution.py:356
  18.6 12.0 %collective-permute-done.4 = bf16[160,1792]{1,0:T(8,128)(2,1)} collective-permute-done((bf16[160,1792]{1,0:T(8,128)(2,1)S(1)}, bf16[160,1792]{1,0:T(8,128)(2,1)}, u32[]{:S(2)}, u32[]{:S(2)}) %collective-permute-start.4) | collective-permute-done | bytes 573472 | tf_op jit(solution)/shard_map/ppermute | solution.py:297
  30.6 2.3 %collective-permute-start.5 = (bf16[160,1792]{1,0:T(8,128)(2,1)}, bf16[160,1792]{1,0:T(8,128)(2,1)}, u32[]{:S(2)}, u32[]{:S(2)}) collective-permute-start(bf16[160,1792]{1,0:T(8,128)(2,1)} %collective-permute-done.4), channel_id=1, source_target_pairs={{0,16},{8,24},{16,0},{24,8},{1,17},{9,25},{17,1},{25,9},{2,18},{10... | collective-permute-start | bytes 1720328 | tf_op jit(solution)/shard_map/ppermute | solution.py:304
  32.9 0.1 collective-permute-start.1
  32.9 1.5 collective-permute-start.2
  34.5 0.6 collective-permute-start.6
  35.1 1.1 constant_dynamic-update-slice_fusion.3
  36.2 13.9 %collective-permute-done.1.refs_7_ = bf16[2,288,128]{2,1,0:T(8,128)(2,1)S(1)} collective-permute-done((bf16[2,288,128]{2,1,0:T(8,128)(2,1)S(1)}, bf16[2,288,128]{2,1,0:T(8,128)(2,1)S(1)}, u32[]{:S(2)}, u32[]{:S(2)}) %collective-permute-start.1) | collective-permute-done | bytes 147488 | tf_op jit(solution)/shard_map/ppermute | solution.py:322
  50.0 2.8 %collective-permute-done.2.refs_8_ = bf16[2,288,128]{2,1,0:T(8,128)(2,1)S(1)} collective-permute-done((bf16[2,288,128]{2,1,0:T(8,128)(2,1)S(1)}, bf16[2,288,128]{2,1,0:T(8,128)(2,1)S(1)}, u32[]{:S(2)}, u32[]{:S(2)}) %collective-permute-start.2) | collective-permute-done | bytes 147488 | tf_op jit(solution)/shard_map/ppermute | solution.py:322
  52.9 4.6 %attention.1 = bf16[8,224,128]{2,1,0:T(8,128)(2,1)} custom-call(s32[1,4]{1,0:T(1,128)S(1)} %copy-done.14, s32[1,4]{1,0:T(1,128)S(1)} %copy-done.15, s32[4]{0:T(128)S(1)} %copy-done.16, bf16[8,288,128]{2,1,0:T(8,128)(2,1)S(1)} %all-to-all-done.refs_3_, f32[3,1792]{1,0:T(4,128)S(1)} %copy-done.13, bf16[2,288,128]{2,1,0:T(8,128)(2,1)S(1)} %fusion.7.refs_5_, ...), custom_call_target="tpu_custom_call" | custom-call | tf_op jit(solution)/shard_map/attention/pallas_call | solution.py:125
  57.5 8.5 %all-to-all-start.1 = ((bf16[8,224,128]{2,1,0:T(8,128)(2,1)}), bf16[8,224,128]{2,1,0:T(8,128)(2,1)S(1)}, u32[]{:S(2)}, u32[]{:S(2)}) async-start(bf16[8,224,128]{2,1,0:T(8,128)(2,1)} %attention.1), calls=%async_computation.1 | async-start | bytes 917504 | tf_op jit(solution)/shard_map/all_to_all | solution.py:361
  66.0 2.0 %collective-permute-start.12 = (bf16[160,1792]{1,0:T(8,128)(2,1)}, bf16[160,1792]{1,0:T(8,128)(2,1)}, u32[]{:S(2)}, u32[]{:S(2)}) collective-permute-start(bf16[160,1792]{1,0:T(8,128)(2,1)} %copy-done.17), channel_id=1, source_target_pairs={{0,2},{1,3},{2,0},{3,1},{4,6},{5,7},{6,4},{7,5},{8,10},{9,11},{10,... | collective-permute-start | bytes 1720328 | tf_op jit(solution)/shard_map/ppermute | solution.py:297
  68.0 1.5 collective-permute-start.9
  69.5 1.9 %constant_dynamic-update-slice_fusion.7 = bf16[640,1792]{1,0:T(8,128)(2,1)} fusion(bf16[160,1792]{1,0:T(8,128)(2,1)} %collective-permute-done.8), kind=kLoop, calls=%fused_computation.27 | loop fusion | bytes 1146880
  71.4 0.5 collective-permute-start.7
  71.9 1.1 constant_dynamic-update-slice_fusion.2
  73.0 0.0 copy-start.10
  73.0 1.1 constant_dynamic-update-slice_fusion.1
  74.2 1.4 copy-done.6
  75.6 12.9 %collective-permute-done.12 = bf16[160,1792]{1,0:T(8,128)(2,1)} collective-permute-done((bf16[160,1792]{1,0:T(8,128)(2,1)}, bf16[160,1792]{1,0:T(8,128)(2,1)}, u32[]{:S(2)}, u32[]{:S(2)}) %collective-permute-start.12) | collective-permute-done | bytes 573472 | tf_op jit(solution)/shard_map/ppermute | solution.py:297
  88.5 1.1 constant_dynamic-update-slice_fusion.11
  89.6 1.5 collective-permute-start.13
  91.1 0.5 collective-permute-start.11
  91.6 1.9 %constant_dynamic-update-slice_fusion.6 = bf16[640,1792]{1,0:T(8,128)(2,1)} fusion(bf16[640,1792]{1,0:T(8,128)(2,1)} %constant_dynamic-update-slice_fusion.7, bf16[160,1792]{1,0:T(8,128)(2,1)} %collective-permute-done.9), kind=kLoop, calls=%fused_computation.26 | loop fusion | bytes 1146880
  93.5 0.9 constant_dynamic-update-slice_fusion.5
  94.4 2.8 %copy-done.8 = bf16[1792,1792]{1,0:T(8,128)(2,1)S(1)} copy-done((bf16[1792,1792]{1,0:T(8,128)(2,1)S(1)}, bf16[1792,1792]{1,0:T(8,128)(2,1)}, u32[]{:S(2)}) %copy-start.8) | copy-done | bytes 6422552
  97.2 3.0 %out_projection.1 = (bf16[128,1792]{1,0:T(8,128)(2,1)S(1)}, bf16[128,1792]{1,0:T(8,128)(2,1)S(1)}) custom-call(bf16[1792,128]{1,0:T(8,128)(2,1)S(1)} %bitcast.18, bf16[1792,1792]{1,0:T(8,128)(2,1)S(1)} %copy-done.8, bf16[128,1792]{1,0:T(8,128)(2,1)S(1)} %copy-done.10, f32[1,1792]{1,0:T(1,128)S(1)} %broadcast_in_dim.6.gain_ref), custom_call_target="tpu_custom_call" | custom-call | tf_op jit(solution)/shard_map/out_projection/pallas_call | solution.py:167
  100.2 2.4 %collective-permute-start.16 = (bf16[128,1792]{1,0:T(8,128)(2,1)S(1)}, bf16[128,1792]{1,0:T(8,128)(2,1)S(1)}, u32[]{:S(2)}, u32[]{:S(2)}) collective-permute-start(bf16[128,1792]{1,0:T(8,128)(2,1)S(1)} %get-tuple-element.22.refs_0_), channel_id=1, source_target_pairs={{0,4},{1,5},{2,6},{3,7},{4,0},{5,1},{6,2},{7,3},{8,12},{9,13},{10,... | collective-permute-start | bytes 1376264 | tf_op jit(solution)/shard_map/ppermute | solution.py:368
  102.7 1.1 constant_dynamic-update-slice_fusion.refs_5_.refs_4_
  103.8 0.0 copy-start.1
  103.8 0.0 copy-start.3
  103.8 1.5 collective-permute-start.3
  105.3 1.1 constant_dynamic-update-slice_fusion.10
  106.4 16.7 %collective-permute-done.16.refs_0_ = bf16[128,1792]{1,0:T(8,128)(2,1)S(1)} collective-permute-done((bf16[128,1792]{1,0:T(8,128)(2,1)S(1)}, bf16[128,1792]{1,0:T(8,128)(2,1)S(1)}, u32[]{:S(2)}, u32[]{:S(2)}) %collective-permute-start.16) | collective-permute-done | bytes 458784 | tf_op jit(solution)/shard_map/ppermute | solution.py:368
  123.2 1.7 collective-permute-start.17
  124.9 1.1 constant_dynamic-update-slice_fusion.9
  126.0 1.9 %constant_dynamic-update-slice_fusion.4.refs_6_.refs_5_ = bf16[640,1792]{1,0:T(8,128)(2,1)} fusion(bf16[640,1792]{1,0:T(8,128)(2,1)} %constant_dynamic-update-slice_fusion.5, bf16[160,1792]{1,0:T(8,128)(2,1)} %collective-permute-done.11), kind=kLoop, calls=%fused_computation.24 | loop fusion | bytes 1146880 | tf_op jit(solution)/shard_map/concatenate | solution.py:306
  128.0 7.6 %collective-permute-done.17.refs_0_ = bf16[128,1792]{1,0:T(8,128)(2,1)S(1)} collective-permute-done((bf16[128,1792]{1,0:T(8,128)(2,1)S(1)}, bf16[128,1792]{1,0:T(8,128)(2,1)S(1)}, u32[]{:S(2)}, u32[]{:S(2)}) %collective-permute-start.17) | collective-permute-done | bytes 458784 | tf_op jit(solution)/shard_map/ppermute | solution.py:371
  135.6 5.3 %feed_forward.5 = bf16[128,1792]{1,0:T(8,128)(2,1)S(1)} custom-call(bf16[128,1792]{1,0:T(8,128)(2,1)S(1)} %collective-permute-done.17.refs_0_, bf16[608,1792]{1,0:T(8,128)(2,1)S(1)} %bitcast.9, bf16[608,1792]{1,0:T(8,128)(2,1)S(1)} %bitcast.13, bf16[608,1792]{1,0:T(8,128)(2,1)S(1)} %copy-done.5, ...), custom_call_target="tpu_custom_call" | custom-call | flops 1717567488 | bytes 13418496 | tf_op jit(solution)/shard_map/feed_forward/pallas_call | solution.py:203
  141.0 1.8 collective-permute-start.18
  142.8 6.4 %feed_forward.3 = (bf16[128,1792]{1,0:T(8,128)(2,1)S(1)}, bf16[128,1792]{1,0:T(8,128)(2,1)S(1)}) custom-call(bf16[128,1792]{1,0:T(8,128)(2,1)S(1)} %get-tuple-element.22.refs_0_, bf16[128,1792]{1,0:T(8,128)(2,1)S(1)} %collective-permute-done.3.refs_1_, bf16[608,1792]{1,0:T(8,128)(2,1)S(1)} %bitcast.10, bf16[608,1792]{1,0:T(8,128)(2,1)S(1)} %bitcast.14, ...), custom_call_target="tpu_custom_call" | custom-call | flops 3435134976 | bytes 13418496 | tf_op jit(solution)/shard_map/feed_forward/pallas_call | solution.py:203
  149.2 0.0 slice-start
  149.2 0.0 copy-start.19
  149.3 0.4 collective-permute-start.20
  149.6 5.5 %feed_forward.4 = bf16[128,1792]{1,0:T(8,128)(2,1)S(1)} custom-call(bf16[128,1792]{1,0:T(8,128)(2,1)S(1)} %collective-permute-done.16.refs_0_, bf16[608,1792]{1,0:T(8,128)(2,1)S(1)} %bitcast.11, bf16[608,1792]{1,0:T(8,128)(2,1)S(1)} %bitcast.15, bf16[608,1792]{1,0:T(8,128)(2,1)S(1)} %copy-done.5, ...), custom_call_target="tpu_custom_call" | custom-call | flops 1717567488 | bytes 13418496 | tf_op jit(solution)/shard_map/feed_forward/pallas_call | solution.py:203
  155.1 0.1 add_convert_fusion
  155.3 0.1 collective-permute-start.19
  155.4 7.1 %collective-permute-done.20.refs_3_ = bf16[128,1792]{1,0:T(8,128)(2,1)S(1)} collective-permute-done((bf16[128,1792]{1,0:T(8,128)(2,1)S(1)}, bf16[128,1792]{1,0:T(8,128)(2,1)S(1)}, u32[]{:S(2)}, u32[]{:S(2)}) %collective-permute-start.20) | collective-permute-done | bytes 458784 | tf_op jit(solution)/shard_map/ppermute | solution.py:371
  162.4 12.5 %collective-permute-done.19.refs_2_ = bf16[128,1792]{1,0:T(8,128)(2,1)S(1)} collective-permute-done((bf16[128,1792]{1,0:T(8,128)(2,1)S(1)}, bf16[128,1792]{1,0:T(8,128)(2,1)S(1)}, u32[]{:S(2)}, u32[]{:S(2)}) %collective-permute-start.19) | collective-permute-done | bytes 458784 | tf_op jit(solution)/shard_map/ppermute | solution.py:368
  175.0 5.4 %next_projection.1 = (bf16[128,1792]{1,0:T(8,128)(2,1)}, bf16[128,2304]{1,0:T(8,128)(2,1)}) custom-call(bf16[128,1792]{1,0:T(8,128)(2,1)S(1)} %get-tuple-element.21.refs_0_, bf16[128,1792]{1,0:T(8,128)(2,1)S(1)} %get-tuple-element.28.refs_1_, bf16[128,1792]{1,0:T(8,128)(2,1)S(1)} %collective-permute-done.19.refs_2_, ...), custom_call_target="tpu_custom_call" | custom-call | tf_op jit(solution)/shard_map/next_projection/pallas_call | solution.py:238
  (56 shorter events, 0.2 us)
Async XLA Ops:
  2.8 1.6 copy-start
  4.4 1.6 copy-start.2
  6.0 1.6 copy-start.4
  7.6 5.1 %copy-start.9 = (bf16[128,1792]{1,0:T(8,128)(2,1)S(1)}, bf16[128,1792]{1,0:T(8,128)(2,1)}, u32[]{:S(2)}) copy-start(bf16[128,1792]{1,0:T(8,128)(2,1)} %v_ref.1) | copy-start | bytes 1376260
  7.6 5.1 %copy-start.11 = (bf16[128,256]{1,0:T(8,128)(2,1)S(1)}, bf16[128,256]{1,0:T(8,128)(2,1)}, u32[]{:S(2)}) copy-start(bf16[128,256]{1,0:T(8,128)(2,1)} %q_ref) | copy-start | bytes 196612
  7.6 5.1 %copy-start.12 = (bf16[128,256]{1,0:T(8,128)(2,1)S(1)}, bf16[128,256]{1,0:T(8,128)(2,1)}, u32[]{:S(2)}) copy-start(bf16[128,256]{1,0:T(8,128)(2,1)} %k_ref.1) | copy-start | bytes 196612
  8.8 0.8 copy-start.17
  9.6 24.8 %copy-start.18 = (f32[1792]{0:T(1024)S(1)}, f32[1792]{0:T(1024)}, u32[]{:S(2)}) copy-start(f32[1792]{0:T(1024)} %param.28) | copy-start | bytes 21508
  9.6 43.2 %copy-start.13 = (f32[3,1792]{1,0:T(4,128)S(1)}, f32[3,1792]{1,0:T(4,128)}, u32[]{:S(2)}) copy-start(f32[3,1792]{1,0:T(4,128)} %refs_4_.2) | copy-start | bytes 64516
  9.6 43.2 %copy-start.14 = (s32[1,4]{1,0:T(1,128)S(1)}, s32[1,4]{1,0:T(1,128)}, u32[]{:S(2)}) copy-start(s32[1,4]{1,0:T(1,128)} %refs_0_.1) | copy-start | bytes 52
  9.6 43.2 %copy-start.15 = (s32[1,4]{1,0:T(1,128)S(1)}, s32[1,4]{1,0:T(1,128)}, u32[]{:S(2)}) copy-start(s32[1,4]{1,0:T(1,128)} %refs_1_.1) | copy-start | bytes 52
  9.6 43.3 %copy-start.16 = (s32[4]{0:T(128)S(1)}, s32[4]{0:T(128)}, u32[]{:S(2)}) copy-start(s32[4]{0:T(128)} %refs_2_.1) | copy-start | bytes 52
  9.6 21.0 %collective-permute-start.4 = (bf16[160,1792]{1,0:T(8,128)(2,1)S(1)}, bf16[160,1792]{1,0:T(8,128)(2,1)}, u32[]{:S(2)}, u32[]{:S(2)}) collective-permute-start(bf16[160,1792]{1,0:T(8,128)(2,1)S(1)} %get-tuple-element.23), channel_id=1, source_target_pairs={{0,2},{1,3},{2,0},{3,1},{4,6},{5,7},{6,4},{7,5},{8,10},{9,11},{10,... | collective-permute-start | bytes 1720328 | tf_op jit(solution)/shard_map/ppermute | solution.py:297
  13.7 39.1 %all-to-all-start = ((bf16[8,288,128]{2,1,0:T(8,128)(2,1)}), bf16[8,288,128]{2,1,0:T(8,128)(2,1)S(1)}, u32[]{:S(2)}, u32[]{:S(2)}) async-start(bf16[8,288,128]{2,1,0:T(8,128)(2,1)} %pack_heads.1), calls=%async_computation | async-start | bytes 1179648 | tf_op jit(solution)/shard_map/all_to_all | solution.py:356
  30.6 35.4 %collective-permute-start.8 = (bf16[160,1792]{1,0:T(8,128)(2,1)}, bf16[160,1792]{1,0:T(8,128)(2,1)}, u32[]{:S(2)}, u32[]{:S(2)}) collective-permute-start(bf16[160,1792]{1,0:T(8,128)(2,1)} %get-tuple-element.25), channel_id=1, source_target_pairs={{0,2},{1,3},{2,0},{3,1},{4,6},{5,7},{6,4},{7,5},{8,10},{9,11},{10,... | collective-permute-start | bytes 1720328 | tf_op jit(solution)/shard_map/ppermute | solution.py:297
  30.6 3.9 %collective-permute-start = (bf16[2,288,128]{2,1,0:T(8,128)(2,1)S(1)}, bf16[2,288,128]{2,1,0:T(8,128)(2,1)S(1)}, u32[]{:S(2)}, u32[]{:S(2)}) collective-permute-start(bf16[2,288,128]{2,1,0:T(8,128)(2,1)S(1)} %fusion.7.refs_5_), channel_id=1, source_target_pairs={{0,8},{8,0},{16,24},{24,16},{1,9},{9,1},{17,25},{25,17},{2,10},{10... | collective-permute-start | bytes 442376 | tf_op jit(solution)/shard_map/ppermute | solution.py:322
  30.6 40.8 %collective-permute-start.5 = (bf16[160,1792]{1,0:T(8,128)(2,1)}, bf16[160,1792]{1,0:T(8,128)(2,1)}, u32[]{:S(2)}, u32[]{:S(2)}) collective-permute-start(bf16[160,1792]{1,0:T(8,128)(2,1)} %collective-permute-done.4), channel_id=1, source_target_pairs={{0,16},{8,24},{16,0},{24,8},{1,17},{9,25},{17,1},{25,9},{2,18},{10... | collective-permute-start | bytes 1720328 | tf_op jit(solution)/shard_map/ppermute | solution.py:304
  32.9 17.2 %collective-permute-start.1 = (bf16[2,288,128]{2,1,0:T(8,128)(2,1)S(1)}, bf16[2,288,128]{2,1,0:T(8,128)(2,1)S(1)}, u32[]{:S(2)}, u32[]{:S(2)}) collective-permute-start(bf16[2,288,128]{2,1,0:T(8,128)(2,1)S(1)} %fusion.7.refs_5_), channel_id=1, source_target_pairs={{0,16},{8,24},{16,0},{24,8},{1,17},{9,25},{17,1},{25,9},{2,18},{10... | collective-permute-start | bytes 442376 | tf_op jit(solution)/shard_map/ppermute | solution.py:322
  32.9 19.9 %collective-permute-start.2 = (bf16[2,288,128]{2,1,0:T(8,128)(2,1)S(1)}, bf16[2,288,128]{2,1,0:T(8,128)(2,1)S(1)}, u32[]{:S(2)}, u32[]{:S(2)}) collective-permute-start(bf16[2,288,128]{2,1,0:T(8,128)(2,1)S(1)} %fusion.7.refs_5_), channel_id=1, source_target_pairs={{0,24},{8,16},{16,8},{24,0},{1,25},{9,17},{17,9},{25,1},{2,26},{10... | collective-permute-start | bytes 442376 | tf_op jit(solution)/shard_map/ppermute | solution.py:322
  34.5 38.6 %collective-permute-start.6 = (bf16[160,1792]{1,0:T(8,128)(2,1)}, bf16[160,1792]{1,0:T(8,128)(2,1)}, u32[]{:S(2)}, u32[]{:S(2)}) collective-permute-start(bf16[160,1792]{1,0:T(8,128)(2,1)} %collective-permute-done.4), channel_id=1, source_target_pairs={{0,8},{8,0},{16,24},{24,16},{1,9},{9,1},{17,25},{25,17},{2,10},{10... | collective-permute-start | bytes 1720328 | tf_op jit(solution)/shard_map/ppermute | solution.py:304
  57.5 36.9 %all-to-all-start.1 = ((bf16[8,224,128]{2,1,0:T(8,128)(2,1)}), bf16[8,224,128]{2,1,0:T(8,128)(2,1)S(1)}, u32[]{:S(2)}, u32[]{:S(2)}) async-start(bf16[8,224,128]{2,1,0:T(8,128)(2,1)} %attention.1), calls=%async_computation.1 | async-start | bytes 917504 | tf_op jit(solution)/shard_map/all_to_all | solution.py:361
  66.0 22.5 %collective-permute-start.12 = (bf16[160,1792]{1,0:T(8,128)(2,1)}, bf16[160,1792]{1,0:T(8,128)(2,1)}, u32[]{:S(2)}, u32[]{:S(2)}) collective-permute-start(bf16[160,1792]{1,0:T(8,128)(2,1)} %copy-done.17), channel_id=1, source_target_pairs={{0,2},{1,3},{2,0},{3,1},{4,6},{5,7},{6,4},{7,5},{8,10},{9,11},{10,... | collective-permute-start | bytes 1720328 | tf_op jit(solution)/shard_map/ppermute | solution.py:297
  68.0 23.1 %collective-permute-start.9 = (bf16[160,1792]{1,0:T(8,128)(2,1)}, bf16[160,1792]{1,0:T(8,128)(2,1)}, u32[]{:S(2)}, u32[]{:S(2)}) collective-permute-start(bf16[160,1792]{1,0:T(8,128)(2,1)} %collective-permute-done.8), channel_id=1, source_target_pairs={{0,16},{8,24},{16,0},{24,8},{1,17},{9,25},{17,1},{25,9},{2,18},{10... | collective-permute-start | bytes 1720328 | tf_op jit(solution)/shard_map/ppermute | solution.py:304
  71.4 22.1 %collective-permute-start.10 = (bf16[160,1792]{1,0:T(8,128)(2,1)}, bf16[160,1792]{1,0:T(8,128)(2,1)S(1)}, u32[]{:S(2)}, u32[]{:S(2)}) collective-permute-start(bf16[160,1792]{1,0:T(8,128)(2,1)} %collective-permute-done.8), channel_id=1, source_target_pairs={{0,8},{8,0},{16,24},{24,16},{1,9},{9,1},{17,25},{25,17},{2,10},{10... | collective-permute-start | bytes 1720328 | tf_op jit(solution)/shard_map/ppermute | solution.py:304
  71.4 31.3 %collective-permute-start.7 = (bf16[160,1792]{1,0:T(8,128)(2,1)}, bf16[160,1792]{1,0:T(8,128)(2,1)}, u32[]{:S(2)}, u32[]{:S(2)}) collective-permute-start(bf16[160,1792]{1,0:T(8,128)(2,1)} %collective-permute-done.5), channel_id=1, source_target_pairs={{0,8},{8,0},{16,24},{24,16},{1,9},{9,1},{17,25},{25,17},{2,10},{10... | collective-permute-start | bytes 1720328 | tf_op jit(solution)/shard_map/ppermute | solution.py:304
  73.0 21.4 %copy-start.10 = (bf16[128,1792]{1,0:T(8,128)(2,1)S(1)}, bf16[128,1792]{1,0:T(8,128)(2,1)}, u32[]{:S(2)}) copy-start(bf16[128,1792]{1,0:T(8,128)(2,1)} %res_ref.1) | copy-start | bytes 1376260
  74.2 1.4 copy-start.6
  89.6 15.7 %collective-permute-start.13 = (bf16[160,1792]{1,0:T(8,128)(2,1)}, bf16[160,1792]{1,0:T(8,128)(2,1)}, u32[]{:S(2)}, u32[]{:S(2)}) collective-permute-start(bf16[160,1792]{1,0:T(8,128)(2,1)} %collective-permute-done.12), channel_id=1, source_target_pairs={{0,16},{8,24},{16,0},{24,8},{1,17},{9,25},{17,1},{25,9},{2,18},{10... | collective-permute-start | bytes 1720328 | tf_op jit(solution)/shard_map/ppermute | solution.py:304
  91.1 33.8 %collective-permute-start.14 = (bf16[160,1792]{1,0:T(8,128)(2,1)}, bf16[160,1792]{1,0:T(8,128)(2,1)}, u32[]{:S(2)}, u32[]{:S(2)}) collective-permute-start(bf16[160,1792]{1,0:T(8,128)(2,1)} %collective-permute-done.12), channel_id=1, source_target_pairs={{0,8},{8,0},{16,24},{24,16},{1,9},{9,1},{17,25},{25,17},{2,10},{10... | collective-permute-start | bytes 1720328 | tf_op jit(solution)/shard_map/ppermute | solution.py:304
  91.1 34.9 %collective-permute-start.11 = (bf16[160,1792]{1,0:T(8,128)(2,1)}, bf16[160,1792]{1,0:T(8,128)(2,1)}, u32[]{:S(2)}, u32[]{:S(2)}) collective-permute-start(bf16[160,1792]{1,0:T(8,128)(2,1)} %collective-permute-done.9), channel_id=1, source_target_pairs={{0,8},{8,0},{16,24},{24,16},{1,9},{9,1},{17,25},{25,17},{2,10},{10... | collective-permute-start | bytes 1720328 | tf_op jit(solution)/shard_map/ppermute | solution.py:304
  94.4 2.8 %copy-start.8 = (bf16[1792,1792]{1,0:T(8,128)(2,1)S(1)}, bf16[1792,1792]{1,0:T(8,128)(2,1)}, u32[]{:S(2)}) copy-start(bf16[1792,1792]{1,0:T(8,128)(2,1)} %w_ref.1) | copy-start | bytes 19267588
  97.2 5.4 %copy-start.7 = (bf16[640,1792]{1,0:T(8,128)(2,1)S(1)}, bf16[640,1792]{1,0:T(8,128)(2,1)}, u32[]{:S(2)}) copy-start(bf16[640,1792]{1,0:T(8,128)(2,1)} %copy-done.6) | copy-start | bytes 6881284
  97.2 38.4 %copy-start.5 = (bf16[608,1792]{1,0:T(8,128)(2,1)S(1)}, bf16[608,1792]{1,0:T(8,128)(2,1)}, u32[]{:S(2)}) copy-start(bf16[608,1792]{1,0:T(8,128)(2,1)} %refs_3_.3) | copy-start | bytes 6537220
  100.2 22.9 %collective-permute-start.16 = (bf16[128,1792]{1,0:T(8,128)(2,1)S(1)}, bf16[128,1792]{1,0:T(8,128)(2,1)S(1)}, u32[]{:S(2)}, u32[]{:S(2)}) collective-permute-start(bf16[128,1792]{1,0:T(8,128)(2,1)S(1)} %get-tuple-element.22.refs_0_), channel_id=1, source_target_pairs={{0,4},{1,5},{2,6},{3,7},{4,0},{5,1},{6,2},{7,3},{8,12},{9,13},{10,... | collective-permute-start | bytes 1376264 | tf_op jit(solution)/shard_map/ppermute | solution.py:368
  103.8 31.9 %copy-start.1 = (bf16[1792,608]{0,1:T(8,128)(2,1)S(1)}, bf16[1792,608]{0,1:T(8,128)(2,1)}, u32[]{:S(2)}) copy-start(bf16[1792,608]{0,1:T(8,128)(2,1)} %param.29) | copy-start | bytes 6537220
  103.8 31.9 %copy-start.3 = (bf16[1792,608]{0,1:T(8,128)(2,1)S(1)}, bf16[1792,608]{0,1:T(8,128)(2,1)}, u32[]{:S(2)}) copy-start(bf16[1792,608]{0,1:T(8,128)(2,1)} %param.30) | copy-start | bytes 6537220
  103.8 39.0 %collective-permute-start.3 = (bf16[128,1792]{1,0:T(8,128)(2,1)S(1)}, bf16[128,1792]{1,0:T(8,128)(2,1)S(1)}, u32[]{:S(2)}, u32[]{:S(2)}) collective-permute-start(bf16[128,1792]{1,0:T(8,128)(2,1)S(1)} %get-tuple-element.22.refs_0_), channel_id=1, source_target_pairs={{0,1},{1,0},{2,3},{3,2},{4,5},{5,4},{6,7},{7,6},{8,9},{9,8},{10,11... | collective-permute-start | bytes 1376264 | tf_op jit(solution)/shard_map/ppermute | solution.py:371
  105.3 22.6 %collective-permute-start.15 = (bf16[160,1792]{1,0:T(8,128)(2,1)}, bf16[160,1792]{1,0:T(8,128)(2,1)S(1)}, u32[]{:S(2)}, u32[]{:S(2)}) collective-permute-start(bf16[160,1792]{1,0:T(8,128)(2,1)} %collective-permute-done.13), channel_id=1, source_target_pairs={{0,8},{8,0},{16,24},{24,16},{1,9},{9,1},{17,25},{25,17},{2,10},{10... | collective-permute-start | bytes 1720328 | tf_op jit(solution)/shard_map/ppermute | solution.py:304
  123.2 12.4 %collective-permute-start.17 = (bf16[128,1792]{1,0:T(8,128)(2,1)S(1)}, bf16[128,1792]{1,0:T(8,128)(2,1)S(1)}, u32[]{:S(2)}, u32[]{:S(2)}) collective-permute-start(bf16[128,1792]{1,0:T(8,128)(2,1)S(1)} %collective-permute-done.16.refs_0_), channel_id=1, source_target_pairs={{0,1},{1,0},{2,3},{3,2},{4,5},{5,4},{6,7},{7,6},{8,9},{9,8},{10,11... | collective-permute-start | bytes 1376264 | tf_op jit(solution)/shard_map/ppermute | solution.py:371
  141.0 14.2 %collective-permute-start.18 = (bf16[128,1792]{1,0:T(8,128)(2,1)S(1)}, bf16[128,1792]{1,0:T(8,128)(2,1)S(1)}, u32[]{:S(2)}, u32[]{:S(2)}) collective-permute-start(bf16[128,1792]{1,0:T(8,128)(2,1)S(1)} %feed_forward.5), channel_id=1, source_target_pairs={{0,1},{1,0},{2,3},{3,2},{4,5},{5,4},{6,7},{7,6},{8,9},{9,8},{10,11... | collective-permute-start | bytes 1376264 | tf_op jit(solution)/shard_map/ppermute | solution.py:371
  149.2 25.8 %slice-start = ((s8[8257536]{0:T(1024)(128)(4,1)}), s8[4194304]{0:T(1024)(128)(4,1)S(1)}, s32[]{:S(2)}) async-start(s8[8257536]{0:T(1024)(128)(4,1)} %bitcast.16), calls=%async_computation.2 | async-start | bytes 8388608
  149.2 6.1 %copy-start.19 = (f32[1792]{0:T(1024)S(1)}, f32[1792]{0:T(1024)}, u32[]{:S(2)}) copy-start(f32[1792]{0:T(1024)} %param.32) | copy-start | bytes 21508
  149.2 25.7 %slice-start.1 = ((s8[8257536]{0:T(1024)(128)(4,1)}), s8[4063232]{0:T(1024)(128)(4,1)S(1)}, s32[]{:S(2)}) async-start(s8[8257536]{0:T(1024)(128)(4,1)} %bitcast.16), calls=%async_computation.3 | async-start | bytes 8126464
  149.3 13.2 %collective-permute-start.20 = (bf16[128,1792]{1,0:T(8,128)(2,1)S(1)}, bf16[128,1792]{1,0:T(8,128)(2,1)S(1)}, u32[]{:S(2)}, u32[]{:S(2)}) collective-permute-start(bf16[128,1792]{1,0:T(8,128)(2,1)S(1)} %get-tuple-element.29), channel_id=1, source_target_pairs={{0,1},{1,0},{2,3},{3,2},{4,5},{5,4},{6,7},{7,6},{8,9},{9,8},{10,11... | collective-permute-start | bytes 1376264 | tf_op jit(solution)/shard_map/ppermute | solution.py:371
  155.3 19.7 %collective-permute-start.19 = (bf16[128,1792]{1,0:T(8,128)(2,1)S(1)}, bf16[128,1792]{1,0:T(8,128)(2,1)S(1)}, u32[]{:S(2)}, u32[]{:S(2)}) collective-permute-start(bf16[128,1792]{1,0:T(8,128)(2,1)S(1)} %add_convert_fusion), channel_id=1, source_target_pairs={{0,4},{1,5},{2,6},{3,7},{4,0},{5,1},{6,2},{7,3},{8,12},{9,13},{10,... | collective-permute-start | bytes 1376264 | tf_op jit(solution)/shard_map/ppermute | solution.py:368

commit v3 on v2

v3 whole, which is shorter than its diff:
```python
import functools
import math

import jax
import jax.numpy as jnp
from jax import lax
from jax.experimental import pallas as pl
from jax.experimental.pallas import tpu as pltpu
from jax.sharding import PartitionSpec as P

EPSILON = 1e-05
DEPTH = 4
TURNED = (((1,), (1,)), ((), ()))
MIB = 1 << 20
ACROSS = (((0,), (0,)), ((), ()))
PLAIN = (((1,), (0,)), ((), ()))
F32 = jnp.float32
BF16 = jnp.bfloat16
VMEM = pltpu.VMEM
GRANT = 60 * MIB
FRONT = 60
PARTS = 2
LIGHT = pl.CostEstimate(flops=1, bytes_accessed=1, transcendentals=0)


def vmem():
    return pl.BlockSpec(memory_space=VMEM)


def dot(a, b, dims=PLAIN):
    return lax.dot_general(a, b, dims, preferred_element_type=F32)


def hbm():
    return pl.BlockSpec(memory_space=pltpu.HBM)


def stay(x):
    return pltpu.with_memory_space_constraint(x, pltpu.HBM)


def pack_kernel(q_hbm, k_hbm, v_hbm, out_hbm, q, k, v, out, sems):
    count = out.shape[0]
    loads = [
        pltpu.make_async_copy(src, dst, sems.at[i])
        for i, (src, dst) in enumerate(((q_hbm, q), (k_hbm, k), (v_hbm, v)))
    ]
    for load in loads:
        load.start()
    at = 0
    for load, ref in zip(loads, (q, k, v)):
        load.wait()
        part = ref.shape[1] // count
        turned = ref[...].T
        for m in range(count):
            out[m, at : at + part, :] = turned[m * part : (m + 1) * part, :]
        at += part
    store = pltpu.make_async_copy(out, out_hbm, sems.at[3])
    store.start()
    store.wait()


def pack(q, k, v, count):
    rows = (q.shape[1] + k.shape[1] + v.shape[1]) // count
    shape = (count, rows, q.shape[0])
    return pl.pallas_call(
        pack_kernel,
        out_shape=jax.ShapeDtypeStruct(shape, BF16),
        in_specs=[hbm()] * 3,
        out_specs=hbm(),
        scratch_shapes=[
            VMEM(q.shape, BF16),
            VMEM(k.shape, BF16),
            VMEM(v.shape, BF16),
            VMEM(shape, BF16),
            pltpu.SemaphoreType.DMA((4,)),
        ],
        compiler_params=pltpu.CompilerParams(vmem_limit_bytes=24 * MIB),
        cost_estimate=LIGHT,
        name="pack_heads",
    )(stay(q), stay(k), stay(v))


def attention_kernel(heads, fd, hd, turns, *refs):
    lengths_ref, flags_ref, owner_ref, conv_ref = refs[:4]
    states, refs = refs[4 : 4 + len(turns)], refs[4 + len(turns) :]
    x_hbm, out_hbm, turned, vconv, feats, taps, cached, out_ref, in_sems, state_sem, out_sems = refs
    blocks, rows, local = x_hbm.shape
    tokens = blocks * local
    values_at = 2 * heads * fd
    tile = 256 if tokens % 256 == 0 else local
    me = lax.axis_index("mlp")
    loads = [
        pltpu.make_async_copy(x_hbm.at[m], turned.at[:, pl.ds(m * local, local)], in_sems.at[m])
        for m in range(blocks)
    ]
    for load in loads:
        load.start()
    slot = lax.axis_index("req")
    owner = owner_ref[slot]
    for turn, state in zip(turns, states):

        @pl.when((slot ^ turn) == owner)
        def _():
            pltpu.make_async_copy(state, cached, state_sem).start()

    position = lax.broadcasted_iota(jnp.int32, (1, tokens), 1)
    start = jnp.zeros((1, tokens), jnp.int32)
    flag = jnp.zeros((1, tokens), F32) + flags_ref[0, 0].astype(F32)
    boundary = jnp.int32(0)
    for r in range(1, lengths_ref.shape[1]):
        boundary = boundary + lengths_ref[0, r - 1]
        reached = position >= boundary
        start = jnp.where(reached, boundary, start)
        flag = jnp.where(reached, flags_ref[0, r].astype(F32), flag)

    count = conv_ref.shape[0]
    spare = jnp.zeros((8 - count, conv_ref.shape[1]), F32)
    taps[...] = jnp.concatenate([conv_ref[...], spare], axis=0).T
    mine = pl.multiple_of(me * heads * hd, 8)
    weights = taps[pl.ds(mine, heads * hd), :]
    for load in loads:
        load.wait()
    values = turned[values_at:, :].astype(F32)
    total = weights[:, 0:1] * values
    for tap in range(1, count):
        earlier = pltpu.roll(values, tap, 1)
        total = total + weights[:, tap : tap + 1] * jnp.where(position - tap >= start, earlier, 0.0)
    vconv[...] = total.astype(BF16)

    for h in range(heads):
        wide = turned[h * fd : (h + 1) * fd, :].astype(F32)
        scaled = wide * (1.0 / math.sqrt(2.0 * fd))
        for a in range(fd):
            feats[h, a * fd : (a + 1) * fd, :] = (wide[a : a + 1, :] * scaled).astype(BF16)
        feats[h, fd * fd : fd * fd + fd, :] = (wide * fd ** (-0.25)).astype(BF16)
        ones = lax.broadcasted_iota(jnp.int32, (16, tokens), 0) == 0
        feats[h, fd * fd + fd :, :] = ones.astype(F32).astype(BF16)
    pltpu.make_async_copy(states[0], cached, state_sem).wait()
    stores = []
    for first in range(0, tokens, tile):
        last = first + tile
        flags = flag[:, first:last]
        key_at = lax.broadcasted_iota(jnp.int32, (last, tile), 0)
        visible = (key_at >= start[:, first:last]) & (key_at <= position[:, first:last])
        for h in range(heads):
            key = turned[(heads + h) * fd : (heads + h + 1) * fd, :last]
            old = dot(cached[h], feats[h, :, first:last], ACROSS)
            score = dot(key, turned[h * fd : (h + 1) * fd, first:last], ACROSS) * (fd**-0.5) + 1.0
            score = jnp.where(visible, score * score * 0.5 + 0.5, 0.0)
            den = jnp.sum(score, axis=0, keepdims=True) + flags * old[hd : hd + 1, :]
            num = dot(vconv[h * hd : (h + 1) * hd, :last], score.astype(BF16))
            result = ((num + flags * old[:hd, :]) / den).astype(BF16)
            for at in range(first, last, local):
                out_ref[at // local, h * hd : (h + 1) * hd, :] = result[:, at - first : at - first + local]
        for m in range(first // local, last // local):
            stores.append(pltpu.make_async_copy(out_ref.at[m], out_hbm.at[m], out_sems.at[m]))
            stores[-1].start()
    for store in stores:
        store.wait()


def attention(lengths, flags, owner, x, conv, states, heads, fd, hd):
    blocks, rows, local = x.shape
    tokens = blocks * local
    turns = tuple(turn for turn, _ in states)
    arrays = [state for _, state in states]
    return pl.pallas_call(
        functools.partial(attention_kernel, heads, fd, hd, turns),
        out_shape=jax.ShapeDtypeStruct((blocks, heads * hd, local), BF16),
        in_specs=[pl.BlockSpec(memory_space=pltpu.SMEM)] * 3
        + [vmem()]
        + [hbm()] * (len(arrays) + 1),
        out_specs=hbm(),
        scratch_shapes=[
            VMEM((rows, tokens), BF16),
            VMEM((heads * hd, tokens), BF16),
            VMEM((heads, arrays[0].shape[1], tokens), BF16),
            VMEM((conv.shape[1], 8), F32),
            VMEM(arrays[0].shape, BF16),
            VMEM((blocks, heads * hd, local), BF16),
            pltpu.SemaphoreType.DMA((blocks,)),
            pltpu.SemaphoreType.DMA,
            pltpu.SemaphoreType.DMA((blocks,)),
        ],
        compiler_params=pltpu.CompilerParams(vmem_limit_bytes=GRANT),
        cost_estimate=LIGHT,
        name="attention",
    )(lengths, flags, owner, conv, *arrays, x)


def rms(rows, gain):
    return rows * lax.rsqrt(jnp.mean(rows * rows, axis=-1, keepdims=True) + EPSILON) * gain


def project_kernel(att_hbm, w_hbm, res_hbm, gain_ref, sum_ref, normed_ref, *refs):
    halves, (att, res, w, sems) = refs[:-4], refs[-4:]
    loads = [
        pltpu.make_async_copy(src, dst, sems.at[i])
        for i, (src, dst) in enumerate(((att_hbm, att), (w_hbm, w), (res_hbm, res)))
    ]
    for load in loads:
        load.start()
    for load in loads:
        load.wait()
    summed = (res[...].astype(F32) + dot(att[...].T, w[...])).astype(BF16)
    sum_ref[...] = summed
    normed = rms(summed.astype(F32), gain_ref[0:1, :]).astype(BF16)
    normed_ref[...] = normed
    step = halves[0].shape[0]
    for i, half in enumerate(halves):
        half[...] = normed[i * step : (i + 1) * step]


def project(att, w, residual, gains):
    rows = att.shape[1]
    width = w.shape[1]
    full = jax.ShapeDtypeStruct((rows, width), BF16)
    part = jax.ShapeDtypeStruct((rows // PARTS, width), BF16)
    first_sum, normed, *halves = pl.pallas_call(
        project_kernel,
        out_shape=[full] * 2 + [part] * PARTS,
        in_specs=[hbm()] * 3 + [vmem()],
        out_specs=[vmem()] * (2 + PARTS),
        scratch_shapes=[
            VMEM(att.shape, BF16),
            VMEM(residual.shape, BF16),
            VMEM(w.shape, BF16),
            pltpu.SemaphoreType.DMA((3,)),
        ],
        compiler_params=pltpu.CompilerParams(vmem_limit_bytes=40 * MIB),
        cost_estimate=LIGHT,
        name="out_projection",
    )(att, stay(w), stay(residual), gains)
    return first_sum, normed, halves


def mlp_kernel(inputs, flips, sharers, *refs):
    xs, own, refs = refs[:inputs], refs[inputs : inputs + 3], refs[inputs + 3 :]
    pieces, outs = refs[:-inputs], refs[-inputs:]
    x = xs[0][...] if inputs == 1 else jnp.concatenate([ref[...] for ref in xs], axis=0)
    units = own[0].shape[0]
    tall, sizes = share_of(units, sharers)
    column = lax.broadcasted_iota(jnp.int32, (1, sum(ref.shape[1] for ref in pieces)), 1)
    fresh, at = column * 0, 0
    for part, flip in flips:
        sharer = lax.axis_index("req") ^ flip
        repeated = sharer * tall - first_unit(sharer, tall, units) - sum(sizes[:part])
        fresh = jnp.where(column >= at, at + repeated, fresh)
        at += sizes[part]
    total = None
    for gates, ups, downs in ([[ref] for ref in own], [[ref.at[i] for ref in pieces] for i in range(3)]):
        gate, up = (
            dot(x, jnp.concatenate([ref[...] for ref in group], axis=0), TURNED)
            for group in (gates, ups)
        )
        hidden = gate * jax.nn.sigmoid(gate) * up
        if gates[0] is not own[0]:
            hidden = jnp.where(column >= fresh, hidden, 0.0)
        part = dot(hidden.astype(BF16), jnp.concatenate([ref[...] for ref in downs], axis=0))
        total = part if total is None else total + part
    local = xs[0].shape[0]
    for i, out in enumerate(outs):
        out[...] = total[i * local : (i + 1) * local].astype(BF16)


def mlp(xs, own, pieces):
    rows, deep = xs[0].shape
    flips = [flip for flip, _ in pieces]
    return pl.pallas_call(
        functools.partial(mlp_kernel, len(xs), flips, lax.axis_size("req")),
        out_shape=[jax.ShapeDtypeStruct((rows, deep), BF16)] * len(xs),
        in_specs=[vmem()] * (len(xs) + 3 + len(pieces)),
        out_specs=[vmem()] * len(xs),
        compiler_params=pltpu.CompilerParams(vmem_limit_bytes=30 * MIB),
        cost_estimate=LIGHT,
        name="feed_forward",
    )(*xs, *own, *(piece for _, piece in pieces))


def add_kernel(*refs):
    refs[-1][...] = sum(ref[...].astype(F32) for ref in refs[:-1]).astype(BF16)


def add(parts):
    return pl.pallas_call(
        add_kernel,
        out_shape=jax.ShapeDtypeStruct(parts[0].shape, BF16),
        in_specs=[vmem()] * len(parts),
        out_specs=vmem(),
        compiler_params=pltpu.CompilerParams(vmem_limit_bytes=16 * MIB),
        cost_estimate=LIGHT,
        name="add_parts",
    )(*parts)


def next_kernel(whole, *refs):
    first_ref, wholes, halves = refs[0], refs[1 : 1 + whole], refs[1 + whole : -6]
    gain_ref, w_hbm, sum_ref, out_ref, w, w_sem = refs[-6:]
    load = pltpu.make_async_copy(w_hbm, w, w_sem)
    load.start()
    extra = sum(ref[...].astype(F32) for ref in wholes)
    extra = extra + jnp.concatenate([ref[...].astype(F32) for ref in halves], axis=0)
    second = (first_ref[...].astype(F32) + extra).astype(BF16)
    sum_ref[...] = second
    normed = rms(second.astype(F32), gain_ref[1:2, :]).astype(BF16)
    load.wait()
    out_ref[...] = dot(normed, w[...]).astype(BF16)


def next_projection(first, wholes, halves, gains, w):
    rows, deep = first.shape
    width = w.shape[1]
    return pl.pallas_call(
        functools.partial(next_kernel, len(wholes)),
        out_shape=[
            jax.ShapeDtypeStruct((rows, deep), BF16),
            jax.ShapeDtypeStruct((rows, width), BF16),
        ],
        in_specs=[vmem()] * (2 + len(wholes) + len(halves)) + [hbm()],
        out_specs=[vmem()] * 2,
        scratch_shapes=[VMEM(w.shape, BF16), pltpu.SemaphoreType.DMA],
        compiler_params=pltpu.CompilerParams(vmem_limit_bytes=40 * MIB),
        cost_estimate=LIGHT,
        name="next_projection",
    )(first, *wholes, *halves, gains, w)


def share_of(units, sharers):
    tall = -(-units // (16 * sharers)) * 16
    if tall < 64:
        return tall, [tall]
    front = -(-tall * FRONT // 1600) * 16
    return tall, [front, tall - front]


def first_unit(sharer, tall, units):
    return jnp.minimum(sharer * tall, units - tall)


def portion_kernel(gate, up, down, *refs):
    outs, sems = refs[:-1], refs[-1]
    tall = sum(out.shape[1] for out in outs)
    at = first_unit(lax.axis_index("req"), tall, gate.shape[0])
    copies = []
    for out in outs:
        rows = pl.ds(pl.multiple_of(at, 16), out.shape[1])
        for i, ref in enumerate((gate, up, down)):
            copies.append(pltpu.make_async_copy(ref.at[rows], out.at[i], sems.at[len(copies)]))
        at = at + out.shape[1]
    for copy in copies:
        copy.start()
    for copy in copies:
        copy.wait()


def portion(weights, sharers):
    units, deep = weights[0].shape
    sizes = share_of(units, sharers)[1]
    return pl.pallas_call(
        portion_kernel,
        out_shape=[jax.ShapeDtypeStruct((3, size, deep), BF16) for size in sizes],
        in_specs=[hbm()] * 3,
        out_specs=[hbm()] * len(sizes),
        scratch_shapes=[pltpu.SemaphoreType.DMA((3 * len(sizes),))],
        compiler_params=pltpu.CompilerParams(vmem_limit_bytes=16 * MIB),
        cost_estimate=LIGHT,
        name="weight_share",
    )(*(stay(w) for w in weights))


def from_line(part, width):
    return [
        lax.ppermute(
            part,
            "mlp",
            [(z * width + y, z * width + (y + turn) % width) for z in range(DEPTH) for y in range(width)],
        )
        for turn in range(1, width)
    ]


def swapped(part, bit):
    return lax.ppermute(part, "req", [(i, i ^ bit) for i in range(lax.axis_size("req"))])


def by_xor(blocks, axis):
    count = lax.axis_size(axis)
    return [blocks[0]] + [
        lax.ppermute(blocks[turn], axis, [(i, i ^ turn) for i in range(count)])
        for turn in range(1, count)
    ]


def after(values, *earlier):
    values, _ = lax.optimization_barrier((values, earlier))
    return values


def cached_state(prefix_state, prefix_norm, fd):
    heads, feats, hd = prefix_state.shape[1:]
    both = jnp.concatenate([prefix_state[0], prefix_norm[0][:, :, None]], axis=2).astype(BF16)
    ordered = jnp.concatenate([both[:, 1 + fd :], both[:, 1 : 1 + fd], both[:, :1]], axis=1)
    packed = jnp.pad(ordered, ((0, 0), (0, 15), (0, 128 - hd - 1)))
    return packed


def shards(
    residual_in,
    query_in,
    key_in,
    values_in,
    conv_weight,
    prefix_state,
    prefix_norm,
    prefix_owner,
    lengths,
    old_flags,
    out_weight,
    mlp_gain,
    gate_weight,
    up_weight,
    down_weight,
    next_gain,
    qkv_weight,
):
    mlp_count = lax.axis_size("mlp")
    width = mlp_count // DEPTH
    heads = prefix_state.shape[1]
    hd = values_in.shape[1] // (heads * mlp_count)
    fd = query_in.shape[1] // (heads * mlp_count)
    own = [gate_weight.T, up_weight.T, down_weight]

    sharers = lax.axis_size("req")
    packed = cached_state(prefix_state, prefix_norm, fd)
    gains = jnp.stack([mlp_gain, next_gain])
    states = list(enumerate(by_xor([packed] * sharers, "req")))
    tokens = pack(*after((query_in, key_in, values_in), packed, gains), mlp_count)
    by_head = lax.all_to_all(tokens, "mlp", 0, 0, tiled=True)
    share = portion(after(own, tokens), sharers)
    count = len(share)
    lines = [from_line(share[0], width)]
    by_head = after(by_head, share)
    attended = attention(
        lengths, old_flags, prefix_owner, by_head, conv_weight, states, heads, fd, hd
    )
    by_row = lax.all_to_all(attended, "mlp", 0, 0, tiled=True)
    by_row = by_row.reshape(mlp_count * heads * hd, by_row.shape[2])

    bits = [1 << i for i in reversed(range(sharers.bit_length() - 1))]

    def pass_on(held, bit):
        return held + [((part, flip ^ bit), swapped(piece, bit)) for (part, flip), piece in held]

    held = [((0, 0), piece) for piece in after(lines[0], attended)]
    for bit in bits[:-1]:
        held = pass_on(held, bit)
    for part in range(1, count):
        lines.append(from_line(after(share[part], lines[-1], attended), width))
    first_sum, normed, parts = project(after(by_row, lines[0]), out_weight, residual_in, gains)

    def across(data):
        return lax.ppermute(data, "mlp", [(i, (i + mlp_count // 2) % mlp_count) for i in range(mlp_count)])

    def beside(data):
        return lax.ppermute(data, "mlp", [(i, i ^ width) for i in range(mlp_count)])

    near = beside(normed)
    far = [across(parts[0])]
    pieces, near = after(([piece for _, piece in held], near), far[0])
    held = list(zip([key for key, _ in held], pieces))
    far_near = []
    for part, piece in enumerate(lines[1:], 1):
        rest = [((part, 0), one) for one in piece]
        for bit in bits[:-1]:
            rest = pass_on(rest, bit)
        held = held + rest
    for part in parts[1:]:
        sent = after(far[-1], near, *far_near)
        far.append(across(after(part, near, far)))
        far_near.append(beside(sent))
    far_near.append(beside(after(far[-1], far_near)))
    pieces = [(key, after(piece, far_near[0], far[-1])) for key, piece in held]
    pieces = pass_on(pieces, bits[-1])
    back, sums = [], []
    fed = []
    for pair in zip(far, far_near):
        fed.append(mlp(after(list(pair), fed), own, pieces))
    for kept, sent in fed:
        total = add([kept, beside(sent)])
        back.append(across(after(total, back)))
        sums.append(total)
    part_own, part_near = mlp(after([normed, near], sums[0]), own, pieces)
    near_back = beside(part_near)
    return next_projection(first_sum, [part_own, near_back], back, gains, qkv_weight)


def solution(mesh):
    rows = P(("req", "mlp"), None)
    placed = (
        rows,
        rows,
        rows,
        rows,
        P(),
        P("req", "mlp", None, None),
        P("req", "mlp", None),
        P(),
        P("req", None),
        P("req", None),
        P(),
        P(),
        P(None, "mlp"),
        P(None, "mlp"),
        P("mlp", None),
        P(),
        P(),
    )
    return jax.shard_map(
        shards, mesh=mesh, in_specs=placed, out_specs=(rows, rows), check_vma=False
    )
```

time: 181 us -> 135 us (0.75)
  local copies, waits for them, and re-layouts: 25.5 us -> 4.97 us
  waiting for transfers between devices: 85.6 us -> 72.5 us
  starting transfers between devices: 34.8 us -> 25.1 us
  Pallas kernels: 32.4 us -> 29.8 us
    ppermute x21, waiting for transfers between devices: 85.6 us -> 56.7 us  [the longest x6 24.3 us: beside(): return lax.ppermute(data, 'mlp', [(i, i ^ width) for i in range(mlp_count)])]
    unnamed x54 -> x23, local copies, waits for them, and re-layouts: 22.3 us -> 3.38 us
    all_to_all x1, waiting for transfers between devices: 0.01 us -> 9.7 us  [shards(): by_head = lax.all_to_all(tokens, 'mlp', 0, 0, tiled=True)]
    ppermute x21, starting transfers between devices: 21.5 us -> 14.1 us  [the longest x6 4.82 us: beside(): return lax.ppermute(data, 'mlp', [(i, i ^ width) for i in range(mlp_count)])]
    all_to_all x1, waiting for transfers between devices: 0.01 us -> 6.08 us  [shards(): by_row = lax.all_to_all(attended, 'mlp', 0, 0, tiled=True)]
    all_to_all x1, starting transfers between devices: 8.52 us -> 3.69 us  [shards(): by_row = lax.all_to_all(attended, 'mlp', 0, 0, tiled=True)]
    pallas_call x7 -> x9, Pallas kernels: 27.8 us -> 23.5 us  [the longest x3 12.1 us: mlp(): pl.pallas_call(functools.partial(mlp_kernel, len(xs), flips, lax.axis_siz...]
    concatenate x3 -> x0, local copies, waits for them, and re-layouts: 3.06 us -> none  [partner_weights(): whole.append(jnp.concatenate(held, axis=0))]
  transfers between devices with their start and end apart: 23 -> 23, of which waited for: 8 -> 15; matrix products, arithmetic and copies ran while one was open for 8% -> 0% of each run, Pallas kernels for 14% -> 18%
where the time goes in v3:
time: 135 us; the launch traced here: 134 us
  waiting for transfers between devices  72.5 us (54%)
  Pallas kernels  29.8 us (22%)
  starting transfers between devices  25.1 us (19%)
  local copies, waits for them, and re-layouts  4.97 us (4%)
    ppermute x6, waiting for transfers between devices, beside(): return lax.ppermute(data, 'mlp', [(i, i ^ width) for i in range(mlp_count)])  24.3 us
    pallas_call x3, Pallas kernels, mlp(): pl.pallas_call(functools.partial(mlp_kernel, len(xs), flips, lax.axis_siz...  12.1 us
    ppermute x6, waiting for transfers between devices, swapped(): lax.ppermute(part, 'req', [(i, i ^ bit) for i in range(lax.axis_size('req...  11.3 us
    ppermute x4, waiting for transfers between devices, across(): lax.ppermute(data, 'mlp', [(i, (i + mlp_count // 2) % mlp_count) for i in...  11 us
    ppermute x2, waiting for transfers between devices, from_line(): lax.ppermute(part, 'mlp', [(z * width + y, z * width + (y + turn) % width...  10 us
    all_to_all x1, waiting for transfers between devices, shards(): by_head = lax.all_to_all(tokens, 'mlp', 0, 0, tiled=True)  9.7 us
    all_to_all x1, starting transfers between devices, shards(): by_head = lax.all_to_all(tokens, 'mlp', 0, 0, tiled=True)  7.29 us
    pallas_call x1, Pallas kernels, attention(): pl.pallas_call(functools.partial(attention_kernel, heads, fd, hd, turns),...  6.29 us
  transfers between devices with their start and end apart: 23, of which 15 were waited for; matrix products, arithmetic and copies ran while one was open for 0% of the time, Pallas kernels for 18%

profile of v3, /device:TPU:0, one launch (start us, length us, event | category | flops | bytes accessed | tf_op | source)
XLA Modules:
  0.0 134.3 jit_solution(7142118933650590081)
XLA Ops:
  0.6 0.7 convert_bitcast_fusion
  1.3 0.2 copy.21
  1.5 1.0 copy.25
  2.5 0.1 fusion.13
  2.6 0.1 slice_maximum_fusion
  2.7 0.7 stack.9
  3.4 0.7 stack.10
  4.1 0.1 fusion.7.refs_4_
  4.2 2.2 %pack_heads.1 = bf16[8,288,128]{2,1,0:T(8,128)(2,1)} custom-call(bf16[128,256]{1,0:T(8,128)(2,1)} %q_hbm, bf16[128,256]{1,0:T(8,128)(2,1)} %k_hbm, bf16[128,1792]{1,0:T(8,128)(2,1)} %v_hbm), custom_call_target="tpu_custom_call" | custom-call | flops 1 | bytes 1 | tf_op jit(solution)/shard_map/pack_heads/pallas_call | solution.py:66
  6.4 7.3 %all-to-all-start = ((bf16[8,288,128]{2,1,0:T(8,128)(2,1)}), bf16[8,288,128]{2,1,0:T(8,128)(2,1)S(1)}, u32[]{:S(2)}, u32[]{:S(2)}) async-start(bf16[8,288,128]{2,1,0:T(8,128)(2,1)} %pack_heads.1), calls=%async_computation | async-start | bytes 1179648 | tf_op jit(solution)/shard_map/all_to_all | solution.py:439
  13.7 1.4 %weight_share.1 = (bf16[3,96,1792]{2,1,0:T(8,128)(2,1)S(1)}, bf16[3,64,1792]{2,1,0:T(8,128)(2,1)S(1)}) custom-call(bf16[608,1792]{1,0:T(8,128)(2,1)} %bitcast.8, bf16[608,1792]{1,0:T(8,128)(2,1)} %bitcast.12, bf16[608,1792]{1,0:T(8,128)(2,1)} %refs_4_.5), custom_call_target="tpu_custom_call" | custom-call | flops 1 | bytes 1 | tf_op jit(solution)/shard_map/weight_share/pallas_call | solution.py:360
  15.1 0.8 copy-done.3
  16.0 2.0 %collective-permute-start.3 = (bf16[3,96,1792]{2,1,0:T(8,128)(2,1)S(1)}, bf16[3,96,1792]{2,1,0:T(8,128)(2,1)S(1)}, u32[]{:S(2)}, u32[]{:S(2)}) collective-permute-start(bf16[3,96,1792]{2,1,0:T(8,128)(2,1)S(1)} %get-tuple-element.47), channel_id=1, source_target_pairs={{0,1},{1,0},{2,3},{3,2},{4,5},{5,4},{6,7},{7,6},{8,9},{9,8},{10,11... | collective-permute-start | bytes 3096584 | tf_op jit(solution)/shard_map/ppermute | solution.py:374
  18.0 0.1 collective-permute-start.2
  18.1 1.4 %collective-permute-start.1 = (bf16[2,288,128]{2,1,0:T(8,128)(2,1)S(1)}, bf16[2,288,128]{2,1,0:T(8,128)(2,1)S(1)}, u32[]{:S(2)}, u32[]{:S(2)}) collective-permute-start(bf16[2,288,128]{2,1,0:T(8,128)(2,1)S(1)} %fusion.7.refs_4_), channel_id=1, source_target_pairs={{0,16},{8,24},{16,0},{24,8},{1,17},{9,25},{17,1},{25,9},{2,18},{10... | collective-permute-start | bytes 442376 | tf_op jit(solution)/shard_map/ppermute | solution.py:390
  19.5 0.3 collective-permute-start
  19.9 9.7 %all-to-all-done.refs_8_ = bf16[8,288,128]{2,1,0:T(8,128)(2,1)S(1)} async-done(((bf16[8,288,128]{2,1,0:T(8,128)(2,1)}), bf16[8,288,128]{2,1,0:T(8,128)(2,1)S(1)}, u32[]{:S(2)}, u32[]{:S(2)}) %all-to-all-start) | async-done | bytes 589856 | tf_op jit(solution)/shard_map/all_to_all | solution.py:439
  29.6 0.0 collective-permute-done.2.refs_7_
  29.6 0.0 collective-permute-done.1.refs_6_
  29.6 0.0 collective-permute-done.refs_5_
  29.6 0.8 copy-done.4
  30.4 0.0 copy-done.6
  30.4 0.0 copy-done.7
  30.5 0.7 copy-done.8
  31.1 6.3 %attention.1 = bf16[8,224,128]{2,1,0:T(8,128)(2,1)} custom-call(s32[1,4]{1,0:T(1,128)} %refs_0_.1, s32[1,4]{1,0:T(1,128)} %refs_1_.1, s32[4]{0:T(128)} %refs_2_.1, f32[3,1792]{1,0:T(4,128)} %refs_3_.1, bf16[2,288,128]{2,1,0:T(8,128)(2,1)} %copy-done.5, bf16[2,288,128]{2,1,0:T(8,128)(2,1)} %copy-done.8, bf16[2,288,128]{2,1,0:T(8,128)(2,1)} %copy-done.7, ...), custom_call_target="tpu_custom_call" | custom-call | flops 1 | bytes 1 | tf_op jit(solution)/shard_map/attention/pallas_call | solution.py:168
  37.4 3.7 %all-to-all-start.1 = ((bf16[8,224,128]{2,1,0:T(8,128)(2,1)}), bf16[8,224,128]{2,1,0:T(8,128)(2,1)S(1)}, u32[]{:S(2)}, u32[]{:S(2)}) async-start(bf16[8,224,128]{2,1,0:T(8,128)(2,1)} %attention.1), calls=%async_computation.1 | async-start | bytes 917504 | tf_op jit(solution)/shard_map/all_to_all | solution.py:447
  41.1 5.7 %collective-permute-done.3.refs_5_ = bf16[3,96,1792]{2,1,0:T(8,128)(2,1)S(1)} collective-permute-done((bf16[3,96,1792]{2,1,0:T(8,128)(2,1)S(1)}, bf16[3,96,1792]{2,1,0:T(8,128)(2,1)S(1)}, u32[]{:S(2)}, u32[]{:S(2)}) %collective-permute-start.3) | collective-permute-done | bytes 1032224 | tf_op jit(solution)/shard_map/ppermute | solution.py:374
  46.8 1.5 %collective-permute-start.4 = (bf16[3,96,1792]{2,1,0:T(8,128)(2,1)S(1)}, bf16[3,96,1792]{2,1,0:T(8,128)(2,1)S(1)}, u32[]{:S(2)}, u32[]{:S(2)}) collective-permute-start(bf16[3,96,1792]{2,1,0:T(8,128)(2,1)S(1)} %collective-permute-done.3.refs_5_), channel_id=1, source_target_pairs={{0,16},{8,24},{16,0},{24,8},{1,17},{9,25},{17,1},{25,9},{2,18},{10... | collective-permute-start | bytes 3096584 | tf_op jit(solution)/shard_map/ppermute | solution.py:384
  48.3 0.0 collective-permute-start.9
  48.3 6.1 %all-to-all-done.1 = bf16[8,224,128]{2,1,0:T(8,128)(2,1)S(1)} async-done(((bf16[8,224,128]{2,1,0:T(8,128)(2,1)}), bf16[8,224,128]{2,1,0:T(8,128)(2,1)S(1)}, u32[]{:S(2)}, u32[]{:S(2)}) %all-to-all-start.1) | async-done | bytes 458784 | tf_op jit(solution)/shard_map/all_to_all | solution.py:447
  54.4 4.5 %out_projection.1 = (bf16[128,1792]{1,0:T(8,128)(2,1)S(1)}, bf16[128,1792]{1,0:T(8,128)(2,1)S(1)}, bf16[64,1792]{1,0:T(8,128)(2,1)S(1)}, bf16[64,1792]{1,0:T(8,128)(2,1)S(1)}) custom-call(bf16[1792,128]{1,0:T(8,128)(2,1)S(1)} %bitcast.18, bf16[1792,1792]{1,0:T(8,128)(2,1)} %w_hbm.1, bf16[128,1792]{1,0:T(8,128)(2,1)} %res_hbm.1, ...), custom_call_target="tpu_custom_call" | custom-call | flops 1 | bytes 1 | tf_op jit(solution)/shard_map/out_projection/pallas_call | solution.py:220
  58.9 1.0 collective-permute-start.5
  59.9 0.8 collective-permute-start.6
  60.7 4.4 %collective-permute-done.9.refs_7_ = bf16[3,64,1792]{2,1,0:T(8,128)(2,1)S(1)} collective-permute-done((bf16[3,64,1792]{2,1,0:T(8,128)(2,1)}, bf16[3,64,1792]{2,1,0:T(8,128)(2,1)S(1)}, u32[]{:S(2)}, u32[]{:S(2)}) %collective-permute-start.9) | collective-permute-done | bytes 688160 | tf_op jit(solution)/shard_map/ppermute | solution.py:374
  65.1 1.2 collective-permute-start.10
  66.3 6.3 %collective-permute-done.4.refs_6_ = bf16[3,96,1792]{2,1,0:T(8,128)(2,1)S(1)} collective-permute-done((bf16[3,96,1792]{2,1,0:T(8,128)(2,1)S(1)}, bf16[3,96,1792]{2,1,0:T(8,128)(2,1)S(1)}, u32[]{:S(2)}, u32[]{:S(2)}) %collective-permute-start.4) | collective-permute-done | bytes 1032224 | tf_op jit(solution)/shard_map/ppermute | solution.py:384
  72.5 0.4 collective-permute-done.6.refs_0_
  72.9 2.2 %collective-permute-done.5.refs_1_ = bf16[128,1792]{1,0:T(8,128)(2,1)S(1)} collective-permute-done((bf16[128,1792]{1,0:T(8,128)(2,1)S(1)}, bf16[128,1792]{1,0:T(8,128)(2,1)S(1)}, u32[]{:S(2)}, u32[]{:S(2)}) %collective-permute-start.5) | collective-permute-done | bytes 458784 | tf_op jit(solution)/shard_map/ppermute | solution.py:466
  75.1 1.6 %collective-permute-start.7 = (bf16[64,1792]{1,0:T(8,128)(2,1)S(1)}, bf16[64,1792]{1,0:T(8,128)(2,1)S(1)}, u32[]{:S(2)}, u32[]{:S(2)}) collective-permute-start(bf16[64,1792]{1,0:T(8,128)(2,1)S(1)} %collective-permute-done.6.refs_0_), channel_id=1, source_target_pairs={{0,2},{1,3},{2,0},{3,1},{4,6},{5,7},{6,4},{7,5},{8,10},{9,11},{10,... | collective-permute-start | bytes 688136 | tf_op jit(solution)/shard_map/ppermute | solution.py:466
  76.7 0.5 collective-permute-start.8
  77.2 6.9 %collective-permute-done.7.refs_1_ = bf16[64,1792]{1,0:T(8,128)(2,1)S(1)} collective-permute-done((bf16[64,1792]{1,0:T(8,128)(2,1)S(1)}, bf16[64,1792]{1,0:T(8,128)(2,1)S(1)}, u32[]{:S(2)}, u32[]{:S(2)}) %collective-permute-start.7) | collective-permute-done | bytes 229408 | tf_op jit(solution)/shard_map/ppermute | solution.py:466
  84.2 4.4 %collective-permute-done.8.refs_0_ = bf16[64,1792]{1,0:T(8,128)(2,1)S(1)} collective-permute-done((bf16[64,1792]{1,0:T(8,128)(2,1)S(1)}, bf16[64,1792]{1,0:T(8,128)(2,1)S(1)}, u32[]{:S(2)}, u32[]{:S(2)}) %collective-permute-start.8) | collective-permute-done | bytes 229408 | tf_op jit(solution)/shard_map/ppermute | solution.py:463
  88.6 0.0 collective-permute-start.11
  88.6 0.5 collective-permute-start.12
  89.1 0.0 collective-permute-start.13
  89.1 0.5 collective-permute-start.14
  89.6 4.1 %collective-permute-done.13.refs_11_ = bf16[3,64,1792]{2,1,0:T(8,128)(2,1)S(1)} collective-permute-done((bf16[3,64,1792]{2,1,0:T(8,128)(2,1)S(1)}, bf16[3,64,1792]{2,1,0:T(8,128)(2,1)S(1)}, u32[]{:S(2)}, u32[]{:S(2)}) %collective-permute-start.13) | collective-permute-done | bytes 688160 | tf_op jit(solution)/shard_map/ppermute | solution.py:384
  93.7 1.0 collective-permute-done.14.refs_12_
  94.7 0.0 collective-permute-done.12.refs_10_
  94.7 3.7 %feed_forward.3 = (bf16[64,1792]{1,0:T(8,128)(2,1)S(1)}, bf16[64,1792]{1,0:T(8,128)(2,1)S(1)}) custom-call(bf16[64,1792]{1,0:T(8,128)(2,1)S(1)} %collective-permute-done.6.refs_0_, bf16[64,1792]{1,0:T(8,128)(2,1)S(1)} %collective-permute-done.7.refs_1_, bf16[608,1792]{1,0:T(8,128)(2,1)S(1)} %bitcast.9, bf16[608,1792]{1,0:T(8,128)(2,1)S(1)} %bitcast.13, ...), custom_call_target="tpu_custom_call" | custom-call | flops 1 | bytes 1 | tf_op jit(solution)/shard_map/feed_forward/pallas_call | solution.py:270
  98.4 0.1 collective-permute-start.15
  98.5 3.7 %feed_forward.5 = (bf16[64,1792]{1,0:T(8,128)(2,1)S(1)}, bf16[64,1792]{1,0:T(8,128)(2,1)S(1)}) custom-call(bf16[64,1792]{1,0:T(8,128)(2,1)S(1)} %collective-permute-done.8.refs_0_, bf16[64,1792]{1,0:T(8,128)(2,1)S(1)} %collective-permute-done.18.refs_1_, bf16[608,1792]{1,0:T(8,128)(2,1)S(1)} %bitcast.10, bf16[608,1792]{1,0:T(8,128)(2,1)S(1)} %bitcast.14, ...), custom_call_target="tpu_custom_call" | custom-call | flops 1 | bytes 1 | tf_op jit(solution)/shard_map/feed_forward/pallas_call | solution.py:270
  102.1 2.1 %collective-permute-start.19 = (bf16[64,1792]{1,0:T(8,128)(2,1)S(1)}, bf16[64,1792]{1,0:T(8,128)(2,1)S(1)}, u32[]{:S(2)}, u32[]{:S(2)}) collective-permute-start(bf16[64,1792]{1,0:T(8,128)(2,1)S(1)} %get-tuple-element.78), channel_id=1, source_target_pairs={{0,2},{1,3},{2,0},{3,1},{4,6},{5,7},{6,4},{7,5},{8,10},{9,11},{10,... | collective-permute-start | bytes 688136 | tf_op jit(solution)/shard_map/ppermute | solution.py:466
  104.2 2.7 %collective-permute-done.15.refs_1_ = bf16[64,1792]{1,0:T(8,128)(2,1)S(1)} collective-permute-done((bf16[64,1792]{1,0:T(8,128)(2,1)S(1)}, bf16[64,1792]{1,0:T(8,128)(2,1)S(1)}, u32[]{:S(2)}, u32[]{:S(2)}) %collective-permute-start.15) | collective-permute-done | bytes 229408 | tf_op jit(solution)/shard_map/ppermute | solution.py:466
  106.9 0.1 add_parts.2
  107.0 0.0 slice-start.1
  107.0 0.4 collective-permute-start.17
  107.4 4.8 %feed_forward.4 = (bf16[128,1792]{1,0:T(8,128)(2,1)S(1)}, bf16[128,1792]{1,0:T(8,128)(2,1)S(1)}) custom-call(bf16[128,1792]{1,0:T(8,128)(2,1)S(1)} %get-tuple-element.70.refs_0_, bf16[128,1792]{1,0:T(8,128)(2,1)S(1)} %collective-permute-done.5.refs_1_, bf16[608,1792]{1,0:T(8,128)(2,1)S(1)} %bitcast.11, bf16[608,1792]{1,0:T(8,128)(2,1)S(1)} %bitcast.15, ...), custom_call_target="tpu_custom_call" | custom-call | flops 1 | bytes 1 | tf_op jit(solution)/shard_map/feed_forward/pallas_call | solution.py:270
  112.2 0.1 collective-permute-start.16
  112.3 0.5 collective-permute-done.19.refs_1_
  112.7 0.1 add_parts.3
  112.8 6.2 %collective-permute-done.17.refs_3_ = bf16[64,1792]{1,0:T(8,128)(2,1)S(1)} collective-permute-done((bf16[64,1792]{1,0:T(8,128)(2,1)S(1)}, bf16[64,1792]{1,0:T(8,128)(2,1)S(1)}, u32[]{:S(2)}, u32[]{:S(2)}) %collective-permute-start.17) | collective-permute-done | bytes 229408 | tf_op jit(solution)/shard_map/ppermute | solution.py:463
  119.0 12.0 %collective-permute-done.16.refs_2_ = bf16[128,1792]{1,0:T(8,128)(2,1)S(1)} collective-permute-done((bf16[128,1792]{1,0:T(8,128)(2,1)S(1)}, bf16[128,1792]{1,0:T(8,128)(2,1)S(1)}, u32[]{:S(2)}, u32[]{:S(2)}) %collective-permute-start.16) | collective-permute-done | bytes 458784 | tf_op jit(solution)/shard_map/ppermute | solution.py:466
  131.0 3.2 %next_projection.1 = (bf16[128,1792]{1,0:T(8,128)(2,1)}, bf16[128,2304]{1,0:T(8,128)(2,1)}) custom-call(bf16[128,1792]{1,0:T(8,128)(2,1)S(1)} %get-tuple-element.51.refs_0_, bf16[128,1792]{1,0:T(8,128)(2,1)S(1)} %get-tuple-element.72.refs_1_, bf16[128,1792]{1,0:T(8,128)(2,1)S(1)} %collective-permute-done.16.refs_2_, ...), custom_call_target="tpu_custom_call" | custom-call | flops 1 | bytes 1 | tf_op jit(solution)/shard_map/next_projection/pallas_call | solution.py:314
  (24 shorter events, 0.1 us)
Async XLA Ops:
  4.2 15.3 %copy-start.5 = (bf16[2,288,128]{2,1,0:T(8,128)(2,1)}, bf16[2,288,128]{2,1,0:T(8,128)(2,1)S(1)}, u32[]{:S(2)}) copy-start(bf16[2,288,128]{2,1,0:T(8,128)(2,1)S(1)} %fusion.7.refs_4_) | copy-start | bytes 442372
  6.4 23.2 %all-to-all-start = ((bf16[8,288,128]{2,1,0:T(8,128)(2,1)}), bf16[8,288,128]{2,1,0:T(8,128)(2,1)S(1)}, u32[]{:S(2)}, u32[]{:S(2)}) async-start(bf16[8,288,128]{2,1,0:T(8,128)(2,1)} %pack_heads.1), calls=%async_computation | async-start | bytes 1179648 | tf_op jit(solution)/shard_map/all_to_all | solution.py:439
  15.1 0.9 copy-start.3
  16.0 30.8 %collective-permute-start.3 = (bf16[3,96,1792]{2,1,0:T(8,128)(2,1)S(1)}, bf16[3,96,1792]{2,1,0:T(8,128)(2,1)S(1)}, u32[]{:S(2)}, u32[]{:S(2)}) collective-permute-start(bf16[3,96,1792]{2,1,0:T(8,128)(2,1)S(1)} %get-tuple-element.47), channel_id=1, source_target_pairs={{0,1},{1,0},{2,3},{3,2},{4,5},{5,4},{6,7},{7,6},{8,9},{9,8},{10,11... | collective-permute-start | bytes 3096584 | tf_op jit(solution)/shard_map/ppermute | solution.py:374
  18.0 11.6 %collective-permute-start.2 = (bf16[2,288,128]{2,1,0:T(8,128)(2,1)S(1)}, bf16[2,288,128]{2,1,0:T(8,128)(2,1)S(1)}, u32[]{:S(2)}, u32[]{:S(2)}) collective-permute-start(bf16[2,288,128]{2,1,0:T(8,128)(2,1)S(1)} %fusion.7.refs_4_), channel_id=1, source_target_pairs={{0,24},{8,16},{16,8},{24,0},{1,25},{9,17},{17,9},{25,1},{2,26},{10... | collective-permute-start | bytes 442376 | tf_op jit(solution)/shard_map/ppermute | solution.py:390
  18.1 11.5 %collective-permute-start.1 = (bf16[2,288,128]{2,1,0:T(8,128)(2,1)S(1)}, bf16[2,288,128]{2,1,0:T(8,128)(2,1)S(1)}, u32[]{:S(2)}, u32[]{:S(2)}) collective-permute-start(bf16[2,288,128]{2,1,0:T(8,128)(2,1)S(1)} %fusion.7.refs_4_), channel_id=1, source_target_pairs={{0,16},{8,24},{16,0},{24,8},{1,17},{9,25},{17,1},{25,9},{2,18},{10... | collective-permute-start | bytes 442376 | tf_op jit(solution)/shard_map/ppermute | solution.py:390
  19.5 10.1 %collective-permute-start = (bf16[2,288,128]{2,1,0:T(8,128)(2,1)S(1)}, bf16[2,288,128]{2,1,0:T(8,128)(2,1)S(1)}, u32[]{:S(2)}, u32[]{:S(2)}) collective-permute-start(bf16[2,288,128]{2,1,0:T(8,128)(2,1)S(1)} %fusion.7.refs_4_), channel_id=1, source_target_pairs={{0,8},{8,0},{16,24},{24,16},{1,9},{9,1},{17,25},{25,17},{2,10},{10... | collective-permute-start | bytes 442376 | tf_op jit(solution)/shard_map/ppermute | solution.py:390
  29.6 0.8 copy-start.4
  29.6 0.8 copy-start.6
  29.6 0.9 copy-start.7
  30.5 0.7 copy-start.8
  37.4 16.9 %all-to-all-start.1 = ((bf16[8,224,128]{2,1,0:T(8,128)(2,1)}), bf16[8,224,128]{2,1,0:T(8,128)(2,1)S(1)}, u32[]{:S(2)}, u32[]{:S(2)}) async-start(bf16[8,224,128]{2,1,0:T(8,128)(2,1)} %attention.1), calls=%async_computation.1 | async-start | bytes 917504 | tf_op jit(solution)/shard_map/all_to_all | solution.py:447
  46.8 25.7 %collective-permute-start.4 = (bf16[3,96,1792]{2,1,0:T(8,128)(2,1)S(1)}, bf16[3,96,1792]{2,1,0:T(8,128)(2,1)S(1)}, u32[]{:S(2)}, u32[]{:S(2)}) collective-permute-start(bf16[3,96,1792]{2,1,0:T(8,128)(2,1)S(1)} %collective-permute-done.3.refs_5_), channel_id=1, source_target_pairs={{0,16},{8,24},{16,0},{24,8},{1,17},{9,25},{17,1},{25,9},{2,18},{10... | collective-permute-start | bytes 3096584 | tf_op jit(solution)/shard_map/ppermute | solution.py:384
  48.3 16.8 %collective-permute-start.9 = (bf16[3,64,1792]{2,1,0:T(8,128)(2,1)}, bf16[3,64,1792]{2,1,0:T(8,128)(2,1)S(1)}, u32[]{:S(2)}, u32[]{:S(2)}) collective-permute-start(bf16[3,64,1792]{2,1,0:T(8,128)(2,1)} %copy-done.3), channel_id=1, source_target_pairs={{0,1},{1,0},{2,3},{3,2},{4,5},{5,4},{6,7},{7,6},{8,9},{9,8},{10,11... | collective-permute-start | bytes 2064392 | tf_op jit(solution)/shard_map/ppermute | solution.py:374
  54.4 40.3 %copy-start = (bf16[1792,608]{0,1:T(8,128)(2,1)S(1)}, bf16[1792,608]{0,1:T(8,128)(2,1)}, u32[]{:S(2)}) copy-start(bf16[1792,608]{0,1:T(8,128)(2,1)} %param.29) | copy-start | bytes 6537220
  54.4 40.3 %copy-start.1 = (bf16[1792,608]{0,1:T(8,128)(2,1)S(1)}, bf16[1792,608]{0,1:T(8,128)(2,1)}, u32[]{:S(2)}) copy-start(bf16[1792,608]{0,1:T(8,128)(2,1)} %param.30) | copy-start | bytes 6537220
  54.4 40.3 %copy-start.2 = (bf16[608,1792]{1,0:T(8,128)(2,1)S(1)}, bf16[608,1792]{1,0:T(8,128)(2,1)}, u32[]{:S(2)}) copy-start(bf16[608,1792]{1,0:T(8,128)(2,1)} %refs_4_.5) | copy-start | bytes 6537220
  58.9 16.2 %collective-permute-start.5 = (bf16[128,1792]{1,0:T(8,128)(2,1)S(1)}, bf16[128,1792]{1,0:T(8,128)(2,1)S(1)}, u32[]{:S(2)}, u32[]{:S(2)}) collective-permute-start(bf16[128,1792]{1,0:T(8,128)(2,1)S(1)} %get-tuple-element.70.refs_0_), channel_id=1, source_target_pairs={{0,2},{1,3},{2,0},{3,1},{4,6},{5,7},{6,4},{7,5},{8,10},{9,11},{10,... | collective-permute-start | bytes 1376264 | tf_op jit(solution)/shard_map/ppermute | solution.py:466
  59.9 13.0 %collective-permute-start.6 = (bf16[64,1792]{1,0:T(8,128)(2,1)S(1)}, bf16[64,1792]{1,0:T(8,128)(2,1)S(1)}, u32[]{:S(2)}, u32[]{:S(2)}) collective-permute-start(bf16[64,1792]{1,0:T(8,128)(2,1)S(1)} %get-tuple-element.54), channel_id=1, source_target_pairs={{0,4},{1,5},{2,6},{3,7},{4,0},{5,1},{6,2},{7,3},{8,12},{9,13},{10,... | collective-permute-start | bytes 688136 | tf_op jit(solution)/shard_map/ppermute | solution.py:463
  65.1 24.1 %collective-permute-start.10 = (bf16[3,64,1792]{2,1,0:T(8,128)(2,1)S(1)}, bf16[3,64,1792]{2,1,0:T(8,128)(2,1)S(1)}, u32[]{:S(2)}, u32[]{:S(2)}) collective-permute-start(bf16[3,64,1792]{2,1,0:T(8,128)(2,1)S(1)} %collective-permute-done.9.refs_7_), channel_id=1, source_target_pairs={{0,16},{8,24},{16,0},{24,8},{1,17},{9,25},{17,1},{25,9},{2,18},{10... | collective-permute-start | bytes 2064392 | tf_op jit(solution)/shard_map/ppermute | solution.py:384
  75.1 9.0 %collective-permute-start.7 = (bf16[64,1792]{1,0:T(8,128)(2,1)S(1)}, bf16[64,1792]{1,0:T(8,128)(2,1)S(1)}, u32[]{:S(2)}, u32[]{:S(2)}) collective-permute-start(bf16[64,1792]{1,0:T(8,128)(2,1)S(1)} %collective-permute-done.6.refs_0_), channel_id=1, source_target_pairs={{0,2},{1,3},{2,0},{3,1},{4,6},{5,7},{6,4},{7,5},{8,10},{9,11},{10,... | collective-permute-start | bytes 688136 | tf_op jit(solution)/shard_map/ppermute | solution.py:466
  76.7 11.9 %collective-permute-start.8 = (bf16[64,1792]{1,0:T(8,128)(2,1)S(1)}, bf16[64,1792]{1,0:T(8,128)(2,1)S(1)}, u32[]{:S(2)}, u32[]{:S(2)}) collective-permute-start(bf16[64,1792]{1,0:T(8,128)(2,1)S(1)} %get-tuple-element.61), channel_id=1, source_target_pairs={{0,4},{1,5},{2,6},{3,7},{4,0},{5,1},{6,2},{7,3},{8,12},{9,13},{10,... | collective-permute-start | bytes 688136 | tf_op jit(solution)/shard_map/ppermute | solution.py:463
  88.6 6.1 %collective-permute-start.11 = (bf16[3,96,1792]{2,1,0:T(8,128)(2,1)S(1)}, bf16[3,96,1792]{2,1,0:T(8,128)(2,1)S(1)}, u32[]{:S(2)}, u32[]{:S(2)}) collective-permute-start(bf16[3,96,1792]{2,1,0:T(8,128)(2,1)S(1)} %collective-permute-done.3.refs_5_), channel_id=1, source_target_pairs={{0,8},{8,0},{16,24},{24,16},{1,9},{9,1},{17,25},{25,17},{2,10},{10... | collective-permute-start | bytes 3096584 | tf_op jit(solution)/shard_map/ppermute | solution.py:384
  88.6 6.1 %collective-permute-start.12 = (bf16[3,96,1792]{2,1,0:T(8,128)(2,1)S(1)}, bf16[3,96,1792]{2,1,0:T(8,128)(2,1)S(1)}, u32[]{:S(2)}, u32[]{:S(2)}) collective-permute-start(bf16[3,96,1792]{2,1,0:T(8,128)(2,1)S(1)} %collective-permute-done.4.refs_6_), channel_id=1, source_target_pairs={{0,8},{8,0},{16,24},{24,16},{1,9},{9,1},{17,25},{25,17},{2,10},{10... | collective-permute-start | bytes 3096584 | tf_op jit(solution)/shard_map/ppermute | solution.py:384
  89.1 4.6 %collective-permute-start.13 = (bf16[3,64,1792]{2,1,0:T(8,128)(2,1)S(1)}, bf16[3,64,1792]{2,1,0:T(8,128)(2,1)S(1)}, u32[]{:S(2)}, u32[]{:S(2)}) collective-permute-start(bf16[3,64,1792]{2,1,0:T(8,128)(2,1)S(1)} %collective-permute-done.9.refs_7_), channel_id=1, source_target_pairs={{0,8},{8,0},{16,24},{24,16},{1,9},{9,1},{17,25},{25,17},{2,10},{10... | collective-permute-start | bytes 2064392 | tf_op jit(solution)/shard_map/ppermute | solution.py:384
  89.1 5.6 %collective-permute-start.14 = (bf16[3,64,1792]{2,1,0:T(8,128)(2,1)S(1)}, bf16[3,64,1792]{2,1,0:T(8,128)(2,1)S(1)}, u32[]{:S(2)}, u32[]{:S(2)}) collective-permute-start(bf16[3,64,1792]{2,1,0:T(8,128)(2,1)S(1)} %collective-permute-done.10.refs_8_), channel_id=1, source_target_pairs={{0,8},{8,0},{16,24},{24,16},{1,9},{9,1},{17,25},{25,17},{2,10},{10... | collective-permute-start | bytes 2064392 | tf_op jit(solution)/shard_map/ppermute | solution.py:384
  89.6 8.8 %collective-permute-start.18 = (bf16[64,1792]{1,0:T(8,128)(2,1)S(1)}, bf16[64,1792]{1,0:T(8,128)(2,1)S(1)}, u32[]{:S(2)}, u32[]{:S(2)}) collective-permute-start(bf16[64,1792]{1,0:T(8,128)(2,1)S(1)} %collective-permute-done.8.refs_0_), channel_id=1, source_target_pairs={{0,2},{1,3},{2,0},{3,1},{4,6},{5,7},{6,4},{7,5},{8,10},{9,11},{10,... | collective-permute-start | bytes 688136 | tf_op jit(solution)/shard_map/ppermute | solution.py:466
  98.4 8.5 %collective-permute-start.15 = (bf16[64,1792]{1,0:T(8,128)(2,1)S(1)}, bf16[64,1792]{1,0:T(8,128)(2,1)S(1)}, u32[]{:S(2)}, u32[]{:S(2)}) collective-permute-start(bf16[64,1792]{1,0:T(8,128)(2,1)S(1)} %get-tuple-element.69), channel_id=1, source_target_pairs={{0,2},{1,3},{2,0},{3,1},{4,6},{5,7},{6,4},{7,5},{8,10},{9,11},{10,... | collective-permute-start | bytes 688136 | tf_op jit(solution)/shard_map/ppermute | solution.py:466
  102.1 10.6 %collective-permute-start.19 = (bf16[64,1792]{1,0:T(8,128)(2,1)S(1)}, bf16[64,1792]{1,0:T(8,128)(2,1)S(1)}, u32[]{:S(2)}, u32[]{:S(2)}) collective-permute-start(bf16[64,1792]{1,0:T(8,128)(2,1)S(1)} %get-tuple-element.78), channel_id=1, source_target_pairs={{0,2},{1,3},{2,0},{3,1},{4,6},{5,7},{6,4},{7,5},{8,10},{9,11},{10,... | collective-permute-start | bytes 688136 | tf_op jit(solution)/shard_map/ppermute | solution.py:466
  106.9 24.1 %slice-start = ((s8[8257536]{0:T(1024)(128)(4,1)}), s8[4194304]{0:T(1024)(128)(4,1)S(1)}, s32[]{:S(2)}) async-start(s8[8257536]{0:T(1024)(128)(4,1)} %bitcast.16), calls=%async_computation.2 | async-start | bytes 8388608
  107.0 24.0 %slice-start.1 = ((s8[8257536]{0:T(1024)(128)(4,1)}), s8[4063232]{0:T(1024)(128)(4,1)S(1)}, s32[]{:S(2)}) async-start(s8[8257536]{0:T(1024)(128)(4,1)} %bitcast.16), calls=%async_computation.3 | async-start | bytes 8126464
  107.0 12.0 %collective-permute-start.17 = (bf16[64,1792]{1,0:T(8,128)(2,1)S(1)}, bf16[64,1792]{1,0:T(8,128)(2,1)S(1)}, u32[]{:S(2)}, u32[]{:S(2)}) collective-permute-start(bf16[64,1792]{1,0:T(8,128)(2,1)S(1)} %add_parts.2), channel_id=1, source_target_pairs={{0,4},{1,5},{2,6},{3,7},{4,0},{5,1},{6,2},{7,3},{8,12},{9,13},{10,... | collective-permute-start | bytes 688136 | tf_op jit(solution)/shard_map/ppermute | solution.py:463
  112.2 18.8 %collective-permute-start.16 = (bf16[128,1792]{1,0:T(8,128)(2,1)S(1)}, bf16[128,1792]{1,0:T(8,128)(2,1)S(1)}, u32[]{:S(2)}, u32[]{:S(2)}) collective-permute-start(bf16[128,1792]{1,0:T(8,128)(2,1)S(1)} %get-tuple-element.73), channel_id=1, source_target_pairs={{0,2},{1,3},{2,0},{3,1},{4,6},{5,7},{6,4},{7,5},{8,10},{9,11},{10,... | collective-permute-start | bytes 1376264 | tf_op jit(solution)/shard_map/ppermute | solution.py:466
  119.0 12.0 %collective-permute-start.20 = (bf16[64,1792]{1,0:T(8,128)(2,1)S(1)}, bf16[64,1792]{1,0:T(8,128)(2,1)S(1)}, u32[]{:S(2)}, u32[]{:S(2)}) collective-permute-start(bf16[64,1792]{1,0:T(8,128)(2,1)S(1)} %add_parts.3), channel_id=1, source_target_pairs={{0,4},{1,5},{2,6},{3,7},{4,0},{5,1},{6,2},{7,3},{8,12},{9,13},{10,... | collective-permute-start | bytes 688136 | tf_op jit(solution)/shard_map/ppermute | solution.py:463

commit v4 on v3

--- a/solution.py
+++ b/solution.py
@@ -195,17 +195,30 @@
 
 def project_kernel(att_hbm, w_hbm, res_hbm, gain_ref, sum_ref, normed_ref, *refs):
     halves, (att, res, w, sems) = refs[:-4], refs[-4:]
+    half = w.shape[0] // 2
     loads = [
         pltpu.make_async_copy(src, dst, sems.at[i])
-        for i, (src, dst) in enumerate(((att_hbm, att), (w_hbm, w), (res_hbm, res)))
+        for i, (src, dst) in enumerate(
+            (
+                (att_hbm, att),
+                (w_hbm.at[pl.ds(0, half)], w.at[pl.ds(0, half)]),
+                (w_hbm.at[pl.ds(half, half)], w.at[pl.ds(half, half)]),
+                (res_hbm, res),
+            )
+        )
     ]
     for load in loads:
         load.start()
-    for load in loads:
-        load.wait()
-    summed = (res[...].astype(F32) + dot(att[...].T, w[...])).astype(BF16)
+    loads[0].wait()
+    rows = att[...].T
+    loads[1].wait()
+    projected = dot(rows[:, :half], w[:half, :])
+    loads[2].wait()
+    projected = projected + dot(rows[:, half:], w[half:, :])
+    loads[3].wait()
+    summed = (res[...].astype(F32) + projected).astype(BF16)
     sum_ref[...] = summed
-    normed = rms(summed.astype(F32), gain_ref[0:1, :]).astype(BF16)
+    normed = rms(summed.astype(F32), gain_ref[...]).astype(BF16)
     normed_ref[...] = normed
     step = halves[0].shape[0]
     for i, half in enumerate(halves):
@@ -226,7 +239,7 @@
             VMEM(att.shape, BF16),
             VMEM(residual.shape, BF16),
             VMEM(w.shape, BF16),
-            pltpu.SemaphoreType.DMA((3,)),
+            pltpu.SemaphoreType.DMA((4,)),
         ],
         compiler_params=pltpu.CompilerParams(vmem_limit_bytes=40 * MIB),
         cost_estimate=LIGHT,
@@ -295,17 +308,14 @@
 
 
 def next_kernel(whole, *refs):
-    first_ref, wholes, halves = refs[0], refs[1 : 1 + whole], refs[1 + whole : -6]
-    gain_ref, w_hbm, sum_ref, out_ref, w, w_sem = refs[-6:]
-    load = pltpu.make_async_copy(w_hbm, w, w_sem)
-    load.start()
+    first_ref, wholes, halves = refs[0], refs[1 : 1 + whole], refs[1 + whole : -4]
+    gain_ref, w_ref, sum_ref, out_ref = refs[-4:]
     extra = sum(ref[...].astype(F32) for ref in wholes)
     extra = extra + jnp.concatenate([ref[...].astype(F32) for ref in halves], axis=0)
     second = (first_ref[...].astype(F32) + extra).astype(BF16)
     sum_ref[...] = second
-    normed = rms(second.astype(F32), gain_ref[1:2, :]).astype(BF16)
-    load.wait()
-    out_ref[...] = dot(normed, w[...]).astype(BF16)
+    normed = rms(second.astype(F32), gain_ref[...]).astype(BF16)
+    out_ref[...] = dot(normed, w_ref[...]).astype(BF16)
 
 
 def next_projection(first, wholes, halves, gains, w):
@@ -317,9 +327,8 @@
             jax.ShapeDtypeStruct((rows, deep), BF16),
             jax.ShapeDtypeStruct((rows, width), BF16),
         ],
-        in_specs=[vmem()] * (2 + len(wholes) + len(halves)) + [hbm()],
+        in_specs=[vmem()] * (3 + len(wholes) + len(halves)),
         out_specs=[vmem()] * 2,
-        scratch_shapes=[VMEM(w.shape, BF16), pltpu.SemaphoreType.DMA],
         compiler_params=pltpu.CompilerParams(vmem_limit_bytes=40 * MIB),
         cost_estimate=LIGHT,
         name="next_projection",
@@ -339,45 +348,49 @@
 
 
 def portion_kernel(gate, up, down, *refs):
-    outs, sems = refs[:-1], refs[-1]
-    tall = sum(out.shape[1] for out in outs)
+    outs, (held, sems, out_sems) = refs[:-3], refs[-3:]
+    tall = held.shape[1]
     at = first_unit(lax.axis_index("req"), tall, gate.shape[0])
-    copies = []
-    for out in outs:
-        rows = pl.ds(pl.multiple_of(at, 16), out.shape[1])
-        for i, ref in enumerate((gate, up, down)):
-            copies.append(pltpu.make_async_copy(ref.at[rows], out.at[i], sems.at[len(copies)]))
-        at = at + out.shape[1]
-    for copy in copies:
-        copy.start()
-    for copy in copies:
-        copy.wait()
+    rows = pl.ds(pl.multiple_of(at, 16), tall)
+    loads = [
+        pltpu.make_async_copy(ref.at[rows], held.at[i], sems.at[i])
+        for i, ref in enumerate((gate, up, down))
+    ]
+    for load in loads:
+        load.start()
+    for load in loads:
+        load.wait()
+    stores, at = [], 0
+    for i, out in enumerate(outs):
+        size = out.shape[1]
+        stores.append(pltpu.make_async_copy(held.at[:, pl.ds(at, size)], out, out_sems.at[i]))
+        stores[-1].start()
+        at += size
+    for store in stores:
+        store.wait()
 
 
 def portion(weights, sharers):
     units, deep = weights[0].shape
-    sizes = share_of(units, sharers)[1]
+    tall, sizes = share_of(units, sharers)
     return pl.pallas_call(
         portion_kernel,
         out_shape=[jax.ShapeDtypeStruct((3, size, deep), BF16) for size in sizes],
         in_specs=[hbm()] * 3,
         out_specs=[hbm()] * len(sizes),
-        scratch_shapes=[pltpu.SemaphoreType.DMA((3 * len(sizes),))],
+        scratch_shapes=[
+            VMEM((3, tall, deep), BF16),
+            pltpu.SemaphoreType.DMA((3,)),
+            pltpu.SemaphoreType.DMA((len(sizes),)),
+        ],
         compiler_params=pltpu.CompilerParams(vmem_limit_bytes=16 * MIB),
         cost_estimate=LIGHT,
         name="weight_share",
     )(*(stay(w) for w in weights))
 
 
-def from_line(part, width):
-    return [
-        lax.ppermute(
-            part,
-            "mlp",
-            [(z * width + y, z * width + (y + turn) % width) for z in range(DEPTH) for y in range(width)],
-        )
-        for turn in range(1, width)
-    ]
+def from_pair(part, width):
+    return [lax.ppermute(part, "mlp", [(i, i ^ width) for i in range(DEPTH * width)])]
 
 
 def swapped(part, bit):
@@ -433,13 +446,12 @@
 
     sharers = lax.axis_size("req")
     packed = cached_state(prefix_state, prefix_norm, fd)
-    gains = jnp.stack([mlp_gain, next_gain])
     states = list(enumerate(by_xor([packed] * sharers, "req")))
-    tokens = pack(*after((query_in, key_in, values_in), packed, gains), mlp_count)
+    tokens = pack(*(query_in, key_in, values_in), mlp_count)
     by_head = lax.all_to_all(tokens, "mlp", 0, 0, tiled=True)
     share = portion(after(own, tokens), sharers)
     count = len(share)
-    lines = [from_line(share[0], width)]
+    lines = [from_pair(share[0], width)]
     by_head = after(by_head, share)
     attended = attention(
         lengths, old_flags, prefix_owner, by_head, conv_weight, states, heads, fd, hd
@@ -456,43 +468,45 @@
     for bit in bits[:-1]:
         held = pass_on(held, bit)
     for part in range(1, count):
-        lines.append(from_line(after(share[part], lines[-1], attended), width))
-    first_sum, normed, parts = project(after(by_row, lines[0]), out_weight, residual_in, gains)
+        lines.append(from_pair(after(share[part], lines[-1], attended), width))
+    first_sum, normed, parts = project(after(by_row, lines[0]), out_weight, residual_in, mlp_gain[None])
 
     def across(data):
         return lax.ppermute(data, "mlp", [(i, (i + mlp_count // 2) % mlp_count) for i in range(mlp_count)])
 
-    def beside(data):
-        return lax.ppermute(data, "mlp", [(i, i ^ width) for i in range(mlp_count)])
-
-    near = beside(normed)
+    def beside(data, turn):
+        return lax.ppermute(
+            data, "mlp", [(i, i - i % width + (i + turn) % width) for i in range(mlp_count)]
+        )
+
+    turns = range(1, width)
+    near = [beside(normed, turn) for turn in turns]
     far = [across(parts[0])]
-    pieces, near = after(([piece for _, piece in held], near), far[0])
-    held = list(zip([key for key, _ in held], pieces))
-    far_near = []
+    arrived, near = after(([piece for _, piece in held], near), far[0])
+    held = list(zip([key for key, _ in held], arrived))
     for part, piece in enumerate(lines[1:], 1):
         rest = [((part, 0), one) for one in piece]
         for bit in bits[:-1]:
             rest = pass_on(rest, bit)
         held = held + rest
+    far_near = []
     for part in parts[1:]:
         sent = after(far[-1], near, *far_near)
         far.append(across(after(part, near, far)))
-        far_near.append(beside(sent))
-    far_near.append(beside(after(far[-1], far_near)))
+        far_near.append([beside(sent, turn) for turn in turns])
+    sent = after(far[-1], far_near)
+    far_near.append([beside(sent, turn) for turn in turns])
     pieces = [(key, after(piece, far_near[0], far[-1])) for key, piece in held]
     pieces = pass_on(pieces, bits[-1])
-    back, sums = [], []
-    fed = []
-    for pair in zip(far, far_near):
-        fed.append(mlp(after(list(pair), fed), own, pieces))
-    for kept, sent in fed:
-        total = add([kept, beside(sent)])
-        back.append(across(after(total, back)))
-        sums.append(total)
-    part_own, part_near = mlp(after([normed, near], sums[0]), own, pieces)
-    near_back = beside(part_near)
-    return next_projection(first_sum, [part_own, near_back], back, gains, qkv_weight)
+    back, sums, fed = [], [], []
+    for mine, others in zip(far, far_near):
+        fed.append(mlp(after([mine, *others], fed), own, pieces))
+    for kept, *sent in fed:
+        sums.append(add([kept] + [beside(part, -turn) for turn, part in zip(turns, sent)]))
+        back.append(across(after(sums[-1], back)))
+    part_own, *part_near = mlp(after([normed, *near], sums[0]), own, pieces)
+    near_back = [beside(part, -turn) for turn, part in zip(turns, part_near)]
+    return next_projection(first_sum, [part_own, *near_back], back, next_gain[None], qkv_weight)
 
 
 def solution(mesh):

time: 135 us -> 129 us (0.956)
  waiting for transfers between devices: 72.5 us -> 68.7 us
  local copies, waits for them, and re-layouts: 4.97 us -> 2.65 us
  starting transfers between devices: 25.1 us -> 26.9 us
    ppermute x4, waiting for transfers between devices: 11 us -> 23.1 us  [across(): lax.ppermute(data, 'mlp', [(i, (i + mlp_count // 2) % mlp_count) for i in...]
    ppermute x6, waiting for transfers between devices: 11.3 us -> 4.31 us  [swapped(): lax.ppermute(part, 'req', [(i, i ^ bit) for i in range(lax.axis_size('req...]
    ppermute x8, waiting for transfers between devices: 34.3 us -> 27.4 us  [the longest x2 20.4 us: from_pair(): lax.ppermute(part, 'mlp', [(i, i ^ width) for i in range(DEPTH * width)])]
    another operation x2 -> x0, local copies, waits for them, and re-layouts: 1.41 us -> none  [shards(): gains = jnp.stack([mlp_gain, next_gain])]
    unnamed x23 -> x31, local copies, waits for them, and re-layouts: 3.38 us -> 2.46 us
  transfers between devices with their start and end apart: 23 -> 23, of which waited for: 15 -> 12; matrix products, arithmetic and copies ran while one was open for 0% -> 0% of each run, Pallas kernels for 18% -> 19%
where the time goes in v4:
time: 129 us
  waiting for transfers between devices  68.7 us (53%)
  Pallas kernels  29.6 us (23%)
  starting transfers between devices  26.9 us (21%)
  local copies, waits for them, and re-layouts  2.65 us (2%)
    ppermute x4, waiting for transfers between devices, across(): lax.ppermute(data, 'mlp', [(i, (i + mlp_count // 2) % mlp_count) for i in...  23.1 us
    ppermute x2, waiting for transfers between devices, from_pair(): lax.ppermute(part, 'mlp', [(i, i ^ width) for i in range(DEPTH * width)])  20.4 us
    pallas_call x3, Pallas kernels, mlp(): pl.pallas_call(functools.partial(mlp_kernel, len(xs), flips, lax.axis_siz...  12.1 us
    all_to_all x1, waiting for transfers between devices, shards(): by_head = lax.all_to_all(tokens, 'mlp', 0, 0, tiled=True)  8.88 us
    all_to_all x1, starting transfers between devices, shards(): by_head = lax.all_to_all(tokens, 'mlp', 0, 0, tiled=True)  7.29 us
    ppermute x6, waiting for transfers between devices, beside(): lax.ppermute(data, 'mlp', [(i, i - i % width + (i + turn) % width) for i...  6.97 us
    pallas_call x1, Pallas kernels, attention(): pl.pallas_call(functools.partial(attention_kernel, heads, fd, hd, turns),...  6.28 us
    ppermute x6, starting transfers between devices, beside(): lax.ppermute(data, 'mlp', [(i, i - i % width + (i + turn) % width) for i...  5.23 us
  transfers between devices with their start and end apart: 23, of which 12 were waited for; matrix products, arithmetic and copies ran while one was open for 0% of the time, Pallas kernels for 19%

profile of v4, /device:TPU:0, one launch (start us, length us, event | category | flops | bytes accessed | tf_op | source)
XLA Modules:
  0.0 129.1 jit_solution(14130755626999001666)
XLA Ops:
  0.6 2.1 %pack_heads.1 = bf16[8,288,128]{2,1,0:T(8,128)(2,1)} custom-call(bf16[128,256]{1,0:T(8,128)(2,1)} %q_hbm.1, bf16[128,256]{1,0:T(8,128)(2,1)} %k_hbm.1, bf16[128,1792]{1,0:T(8,128)(2,1)} %v_hbm.1), custom_call_target="tpu_custom_call" | custom-call | flops 1 | bytes 1 | tf_op jit(solution)/shard_map/pack_heads/pallas_call | solution.py:66
  2.8 7.3 %all-to-all-start = ((bf16[8,288,128]{2,1,0:T(8,128)(2,1)}), bf16[8,288,128]{2,1,0:T(8,128)(2,1)S(1)}, u32[]{:S(2)}, u32[]{:S(2)}) async-start(bf16[8,288,128]{2,1,0:T(8,128)(2,1)} %pack_heads.1), calls=%async_computation | async-start | bytes 1179648 | tf_op jit(solution)/shard_map/all_to_all | solution.py:451
  10.1 0.0 copy-start.6
  10.1 1.7 %weight_share.1 = (bf16[3,96,1792]{2,1,0:T(8,128)(2,1)S(1)}, bf16[3,64,1792]{2,1,0:T(8,128)(2,1)S(1)}) custom-call(bf16[608,1792]{1,0:T(8,128)(2,1)} %bitcast.8, bf16[608,1792]{1,0:T(8,128)(2,1)} %bitcast.12, bf16[608,1792]{1,0:T(8,128)(2,1)} %refs_4_.5), custom_call_target="tpu_custom_call" | custom-call | flops 1 | bytes 1 | tf_op jit(solution)/shard_map/weight_share/pallas_call | solution.py:376
  11.8 0.8 copy-done.3
  12.6 2.0 %collective-permute-start.3 = (bf16[3,96,1792]{2,1,0:T(8,128)(2,1)S(1)}, bf16[3,96,1792]{2,1,0:T(8,128)(2,1)S(1)}, u32[]{:S(2)}, u32[]{:S(2)}) collective-permute-start(bf16[3,96,1792]{2,1,0:T(8,128)(2,1)S(1)} %get-tuple-element.41), channel_id=1, source_target_pairs={{0,2},{1,3},{2,0},{3,1},{4,6},{5,7},{6,4},{7,5},{8,10},{9,11},{10,... | collective-permute-start | bytes 3096584 | tf_op jit(solution)/shard_map/ppermute | solution.py:393
  14.6 0.2 copy.21
  14.8 0.0 copy-start.10
  14.9 0.1 fusion.13
  15.0 0.1 slice_maximum_fusion
  15.1 0.1 fusion.7.refs_4_
  15.2 0.1 collective-permute-start
  15.3 1.6 %collective-permute-start.1 = (bf16[2,288,128]{2,1,0:T(8,128)(2,1)S(1)}, bf16[2,288,128]{2,1,0:T(8,128)(2,1)S(1)}, u32[]{:S(2)}, u32[]{:S(2)}) collective-permute-start(bf16[2,288,128]{2,1,0:T(8,128)(2,1)S(1)} %fusion.7.refs_4_), channel_id=1, source_target_pairs={{0,16},{8,24},{16,0},{24,8},{1,17},{9,25},{17,1},{25,9},{2,18},{10... | collective-permute-start | bytes 442376 | tf_op jit(solution)/shard_map/ppermute | solution.py:403
  16.8 0.3 collective-permute-start.2
  17.1 8.9 %all-to-all-done.refs_8_ = bf16[8,288,128]{2,1,0:T(8,128)(2,1)S(1)} async-done(((bf16[8,288,128]{2,1,0:T(8,128)(2,1)}), bf16[8,288,128]{2,1,0:T(8,128)(2,1)S(1)}, u32[]{:S(2)}, u32[]{:S(2)}) %all-to-all-start) | async-done | bytes 589856 | tf_op jit(solution)/shard_map/all_to_all | solution.py:451
  26.0 0.0 collective-permute-done.refs_5_
  26.0 0.0 collective-permute-done.1.refs_6_
  26.0 0.0 collective-permute-done.2.refs_7_
  26.0 0.8 copy-done.4
  26.8 0.0 copy-done.7
  26.8 0.1 copy-done.8
  26.9 0.7 copy-done.9
  27.6 6.3 %attention.1 = bf16[8,224,128]{2,1,0:T(8,128)(2,1)} custom-call(s32[1,4]{1,0:T(1,128)} %refs_0_.1, s32[1,4]{1,0:T(1,128)} %refs_1_.1, s32[4]{0:T(128)} %refs_2_.1, f32[3,1792]{1,0:T(4,128)} %refs_3_.1, bf16[2,288,128]{2,1,0:T(8,128)(2,1)} %copy-done.5, bf16[2,288,128]{2,1,0:T(8,128)(2,1)} %copy-done.7, bf16[2,288,128]{2,1,0:T(8,128)(2,1)} %copy-done.8, ...), custom_call_target="tpu_custom_call" | custom-call | flops 1 | bytes 1 | tf_op jit(solution)/shard_map/attention/pallas_call | solution.py:168
  33.9 3.7 %all-to-all-start.1 = ((bf16[8,224,128]{2,1,0:T(8,128)(2,1)}), bf16[8,224,128]{2,1,0:T(8,128)(2,1)S(1)}, u32[]{:S(2)}, u32[]{:S(2)}) async-start(bf16[8,224,128]{2,1,0:T(8,128)(2,1)} %attention.1), calls=%async_computation.1 | async-start | bytes 917504 | tf_op jit(solution)/shard_map/all_to_all | solution.py:459
  37.6 10.3 %collective-permute-done.3.refs_5_ = bf16[3,96,1792]{2,1,0:T(8,128)(2,1)S(1)} collective-permute-done((bf16[3,96,1792]{2,1,0:T(8,128)(2,1)S(1)}, bf16[3,96,1792]{2,1,0:T(8,128)(2,1)S(1)}, u32[]{:S(2)}, u32[]{:S(2)}) %collective-permute-start.3) | collective-permute-done | bytes 1032224 | tf_op jit(solution)/shard_map/ppermute | solution.py:393
  47.9 1.5 %collective-permute-start.4 = (bf16[3,96,1792]{2,1,0:T(8,128)(2,1)S(1)}, bf16[3,96,1792]{2,1,0:T(8,128)(2,1)S(1)}, u32[]{:S(2)}, u32[]{:S(2)}) collective-permute-start(bf16[3,96,1792]{2,1,0:T(8,128)(2,1)S(1)} %collective-permute-done.3.refs_5_), channel_id=1, source_target_pairs={{0,16},{8,24},{16,0},{24,8},{1,17},{9,25},{17,1},{25,9},{2,18},{10... | collective-permute-start | bytes 3096584 | tf_op jit(solution)/shard_map/ppermute | solution.py:397
  49.3 0.0 collective-permute-start.9
  49.4 5.0 %all-to-all-done.1 = bf16[8,224,128]{2,1,0:T(8,128)(2,1)S(1)} async-done(((bf16[8,224,128]{2,1,0:T(8,128)(2,1)}), bf16[8,224,128]{2,1,0:T(8,128)(2,1)S(1)}, u32[]{:S(2)}, u32[]{:S(2)}) %all-to-all-start.1) | async-done | bytes 458784 | tf_op jit(solution)/shard_map/all_to_all | solution.py:459
  54.4 5.0 %out_projection.1 = (bf16[128,1792]{1,0:T(8,128)(2,1)S(1)}, bf16[128,1792]{1,0:T(8,128)(2,1)S(1)}, bf16[64,1792]{1,0:T(8,128)(2,1)S(1)}, bf16[64,1792]{1,0:T(8,128)(2,1)S(1)}) custom-call(bf16[1792,128]{1,0:T(8,128)(2,1)S(1)} %bitcast.18, bf16[1792,1792]{1,0:T(8,128)(2,1)} %w_hbm.1, bf16[128,1792]{1,0:T(8,128)(2,1)} %res_hbm.1, ...), custom_call_target="tpu_custom_call" | custom-call | flops 1 | bytes 1 | tf_op jit(solution)/shard_map/out_projection/pallas_call | solution.py:233
  59.4 0.1 collective-permute-start.5
  59.5 1.5 %collective-permute-start.6 = (bf16[64,1792]{1,0:T(8,128)(2,1)S(1)}, bf16[64,1792]{1,0:T(8,128)(2,1)S(1)}, u32[]{:S(2)}, u32[]{:S(2)}) collective-permute-start(bf16[64,1792]{1,0:T(8,128)(2,1)S(1)} %get-tuple-element.48), channel_id=1, source_target_pairs={{0,4},{1,5},{2,6},{3,7},{4,0},{5,1},{6,2},{7,3},{8,12},{9,13},{10,... | collective-permute-start | bytes 688136 | tf_op jit(solution)/shard_map/ppermute | solution.py:475
  60.9 10.1 %collective-permute-done.9.refs_7_ = bf16[3,64,1792]{2,1,0:T(8,128)(2,1)S(1)} collective-permute-done((bf16[3,64,1792]{2,1,0:T(8,128)(2,1)}, bf16[3,64,1792]{2,1,0:T(8,128)(2,1)S(1)}, u32[]{:S(2)}, u32[]{:S(2)}) %collective-permute-start.9) | collective-permute-done | bytes 688160 | tf_op jit(solution)/shard_map/ppermute | solution.py:393
  71.0 1.5 %collective-permute-start.10 = (bf16[3,64,1792]{2,1,0:T(8,128)(2,1)S(1)}, bf16[3,64,1792]{2,1,0:T(8,128)(2,1)S(1)}, u32[]{:S(2)}, u32[]{:S(2)}) collective-permute-start(bf16[3,64,1792]{2,1,0:T(8,128)(2,1)S(1)} %collective-permute-done.9.refs_7_), channel_id=1, source_target_pairs={{0,16},{8,24},{16,0},{24,8},{1,17},{9,25},{17,1},{25,9},{2,18},{10... | collective-permute-start | bytes 2064392 | tf_op jit(solution)/shard_map/ppermute | solution.py:397
  72.5 0.0 collective-permute-done.4.refs_6_
  72.5 0.0 collective-permute-done.5.refs_1_
  72.5 1.2 collective-permute-start.8
  73.7 0.9 collective-permute-start.7
  74.6 9.9 %collective-permute-done.8.refs_0_ = bf16[64,1792]{1,0:T(8,128)(2,1)S(1)} collective-permute-done((bf16[64,1792]{1,0:T(8,128)(2,1)S(1)}, bf16[64,1792]{1,0:T(8,128)(2,1)S(1)}, u32[]{:S(2)}, u32[]{:S(2)}) %collective-permute-start.8) | collective-permute-done | bytes 229408 | tf_op jit(solution)/shard_map/ppermute | solution.py:475
  84.5 0.0 collective-permute-done.7.refs_1_
  84.5 0.0 collective-permute-start.12
  84.5 0.5 collective-permute-start.11
  85.0 2.3 %collective-permute-done.10.refs_8_ = bf16[3,64,1792]{2,1,0:T(8,128)(2,1)S(1)} collective-permute-done((bf16[3,64,1792]{2,1,0:T(8,128)(2,1)S(1)}, bf16[3,64,1792]{2,1,0:T(8,128)(2,1)S(1)}, u32[]{:S(2)}, u32[]{:S(2)}) %collective-permute-start.10) | collective-permute-done | bytes 688160 | tf_op jit(solution)/shard_map/ppermute | solution.py:397
  87.3 0.0 collective-permute-start.14
  87.4 0.5 collective-permute-start.13
  87.9 0.8 collective-permute-start.18
  88.6 1.0 collective-permute-done.14.refs_12_
  89.6 1.0 collective-permute-done.13.refs_11_
  90.6 3.7 %feed_forward.3 = (bf16[64,1792]{1,0:T(8,128)(2,1)S(1)}, bf16[64,1792]{1,0:T(8,128)(2,1)S(1)}) custom-call(bf16[64,1792]{1,0:T(8,128)(2,1)S(1)} %collective-permute-done.6.refs_0_, bf16[64,1792]{1,0:T(8,128)(2,1)S(1)} %collective-permute-done.7.refs_1_, bf16[608,1792]{1,0:T(8,128)(2,1)S(1)} %bitcast.9, bf16[608,1792]{1,0:T(8,128)(2,1)S(1)} %bitcast.13, ...), custom_call_target="tpu_custom_call" | custom-call | flops 1 | bytes 1 | tf_op jit(solution)/shard_map/feed_forward/pallas_call | solution.py:283
  94.3 1.2 collective-permute-start.15
  95.5 3.6 %feed_forward.5 = (bf16[64,1792]{1,0:T(8,128)(2,1)S(1)}, bf16[64,1792]{1,0:T(8,128)(2,1)S(1)}) custom-call(bf16[64,1792]{1,0:T(8,128)(2,1)S(1)} %collective-permute-done.8.refs_0_, bf16[64,1792]{1,0:T(8,128)(2,1)S(1)} %collective-permute-done.18.refs_1_, bf16[608,1792]{1,0:T(8,128)(2,1)S(1)} %bitcast.10, bf16[608,1792]{1,0:T(8,128)(2,1)S(1)} %bitcast.14, ...), custom_call_target="tpu_custom_call" | custom-call | flops 1 | bytes 1 | tf_op jit(solution)/shard_map/feed_forward/pallas_call | solution.py:283
  99.1 1.0 collective-permute-start.19
  100.1 2.2 %collective-permute-done.15.refs_1_ = bf16[64,1792]{1,0:T(8,128)(2,1)S(1)} collective-permute-done((bf16[64,1792]{1,0:T(8,128)(2,1)S(1)}, bf16[64,1792]{1,0:T(8,128)(2,1)S(1)}, u32[]{:S(2)}, u32[]{:S(2)}) %collective-permute-start.15) | collective-permute-done | bytes 229408 | tf_op jit(solution)/shard_map/ppermute | solution.py:478
  102.3 0.1 add_parts.2
  102.4 0.0 copy-start.11
  102.4 0.0 slice-start.1
  102.4 0.1 collective-permute-start.17
  102.5 4.8 %feed_forward.4 = (bf16[128,1792]{1,0:T(8,128)(2,1)S(1)}, bf16[128,1792]{1,0:T(8,128)(2,1)S(1)}) custom-call(bf16[128,1792]{1,0:T(8,128)(2,1)S(1)} %get-tuple-element.64.refs_0_, bf16[128,1792]{1,0:T(8,128)(2,1)S(1)} %collective-permute-done.5.refs_1_, bf16[608,1792]{1,0:T(8,128)(2,1)S(1)} %bitcast.11, bf16[608,1792]{1,0:T(8,128)(2,1)S(1)} %bitcast.15, ...), custom_call_target="tpu_custom_call" | custom-call | flops 1 | bytes 1 | tf_op jit(solution)/shard_map/feed_forward/pallas_call | solution.py:283
  107.3 1.4 %collective-permute-start.16 = (bf16[128,1792]{1,0:T(8,128)(2,1)S(1)}, bf16[128,1792]{1,0:T(8,128)(2,1)S(1)}, u32[]{:S(2)}, u32[]{:S(2)}) collective-permute-start(bf16[128,1792]{1,0:T(8,128)(2,1)S(1)} %get-tuple-element.67), channel_id=1, source_target_pairs={{0,1},{1,0},{2,3},{3,2},{4,5},{5,4},{6,7},{7,6},{8,9},{9,8},{10,11... | collective-permute-start | bytes 1376264 | tf_op jit(solution)/shard_map/ppermute | solution.py:478
  108.6 0.0 collective-permute-done.19.refs_1_
  108.6 0.1 add_parts.3
  108.7 5.3 %collective-permute-done.17.refs_3_ = bf16[64,1792]{1,0:T(8,128)(2,1)S(1)} collective-permute-done((bf16[64,1792]{1,0:T(8,128)(2,1)S(1)}, bf16[64,1792]{1,0:T(8,128)(2,1)S(1)}, u32[]{:S(2)}, u32[]{:S(2)}) %collective-permute-start.17) | collective-permute-done | bytes 229408 | tf_op jit(solution)/shard_map/ppermute | solution.py:475
  114.0 4.8 %collective-permute-done.16.refs_2_ = bf16[128,1792]{1,0:T(8,128)(2,1)S(1)} collective-permute-done((bf16[128,1792]{1,0:T(8,128)(2,1)S(1)}, bf16[128,1792]{1,0:T(8,128)(2,1)S(1)}, u32[]{:S(2)}, u32[]{:S(2)}) %collective-permute-start.16) | collective-permute-done | bytes 458784 | tf_op jit(solution)/shard_map/ppermute | solution.py:478
  118.8 7.9 %collective-permute-done.20.refs_4_ = bf16[64,1792]{1,0:T(8,128)(2,1)S(1)} collective-permute-done((bf16[64,1792]{1,0:T(8,128)(2,1)S(1)}, bf16[64,1792]{1,0:T(8,128)(2,1)S(1)}, u32[]{:S(2)}, u32[]{:S(2)}) %collective-permute-start.20) | collective-permute-done | bytes 229408 | tf_op jit(solution)/shard_map/ppermute | solution.py:475
  126.7 2.4 %next_projection.1 = (bf16[128,1792]{1,0:T(8,128)(2,1)}, bf16[128,2304]{1,0:T(8,128)(2,1)}) custom-call(bf16[128,1792]{1,0:T(8,128)(2,1)S(1)} %get-tuple-element.45.refs_0_, bf16[128,1792]{1,0:T(8,128)(2,1)S(1)} %get-tuple-element.66.refs_1_, bf16[128,1792]{1,0:T(8,128)(2,1)S(1)} %collective-permute-done.16.refs_2_, ...), custom_call_target="tpu_custom_call" | custom-call | flops 1 | bytes 1 | tf_op jit(solution)/shard_map/next_projection/pallas_call | solution.py:324
  (31 shorter events, 0.1 us)
Async XLA Ops:
  2.8 23.2 %all-to-all-start = ((bf16[8,288,128]{2,1,0:T(8,128)(2,1)}), bf16[8,288,128]{2,1,0:T(8,128)(2,1)S(1)}, u32[]{:S(2)}, u32[]{:S(2)}) async-start(bf16[8,288,128]{2,1,0:T(8,128)(2,1)} %pack_heads.1), calls=%async_computation | async-start | bytes 1179648 | tf_op jit(solution)/shard_map/all_to_all | solution.py:451
  10.0 4.6 %copy-start.12 = (f32[1,2,273]{2,1,0:T(2,128)S(1)}, f32[1,2,273]{2,1,0:T(2,128)}, u32[]{:S(2)}) copy-start(f32[1,2,273]{2,1,0:T(2,128)} %param.23) | copy-start | bytes 6556
  10.1 4.8 %copy-start.6 = (f32[1,2,273,112]{3,1,2,0:T(2,128)S(1)}, f32[1,2,273,112]{3,1,2,0:T(2,128)}, u32[]{:S(2)}) copy-start(f32[1,2,273,112]{3,1,2,0:T(2,128)} %param.22) | copy-start | bytes 733828
  11.8 0.9 copy-start.3
  12.6 35.2 %collective-permute-start.3 = (bf16[3,96,1792]{2,1,0:T(8,128)(2,1)S(1)}, bf16[3,96,1792]{2,1,0:T(8,128)(2,1)S(1)}, u32[]{:S(2)}, u32[]{:S(2)}) collective-permute-start(bf16[3,96,1792]{2,1,0:T(8,128)(2,1)S(1)} %get-tuple-element.41), channel_id=1, source_target_pairs={{0,2},{1,3},{2,0},{3,1},{4,6},{5,7},{6,4},{7,5},{8,10},{9,11},{10,... | collective-permute-start | bytes 3096584 | tf_op jit(solution)/shard_map/ppermute | solution.py:393
  14.8 34.5 %copy-start.10 = (f32[1792]{0:T(1024)S(1)}, f32[1792]{0:T(1024)}, u32[]{:S(2)}) copy-start(f32[1792]{0:T(1024)} %param.28) | copy-start | bytes 21508
  15.2 10.9 %copy-start.5 = (bf16[2,288,128]{2,1,0:T(8,128)(2,1)}, bf16[2,288,128]{2,1,0:T(8,128)(2,1)S(1)}, u32[]{:S(2)}) copy-start(bf16[2,288,128]{2,1,0:T(8,128)(2,1)S(1)} %fusion.7.refs_4_) | copy-start | bytes 442372
  15.2 10.8 %collective-permute-start = (bf16[2,288,128]{2,1,0:T(8,128)(2,1)S(1)}, bf16[2,288,128]{2,1,0:T(8,128)(2,1)S(1)}, u32[]{:S(2)}, u32[]{:S(2)}) collective-permute-start(bf16[2,288,128]{2,1,0:T(8,128)(2,1)S(1)} %fusion.7.refs_4_), channel_id=1, source_target_pairs={{0,8},{8,0},{16,24},{24,16},{1,9},{9,1},{17,25},{25,17},{2,10},{10... | collective-permute-start | bytes 442376 | tf_op jit(solution)/shard_map/ppermute | solution.py:403
  15.3 10.7 %collective-permute-start.1 = (bf16[2,288,128]{2,1,0:T(8,128)(2,1)S(1)}, bf16[2,288,128]{2,1,0:T(8,128)(2,1)S(1)}, u32[]{:S(2)}, u32[]{:S(2)}) collective-permute-start(bf16[2,288,128]{2,1,0:T(8,128)(2,1)S(1)} %fusion.7.refs_4_), channel_id=1, source_target_pairs={{0,16},{8,24},{16,0},{24,8},{1,17},{9,25},{17,1},{25,9},{2,18},{10... | collective-permute-start | bytes 442376 | tf_op jit(solution)/shard_map/ppermute | solution.py:403
  16.8 9.2 %collective-permute-start.2 = (bf16[2,288,128]{2,1,0:T(8,128)(2,1)S(1)}, bf16[2,288,128]{2,1,0:T(8,128)(2,1)S(1)}, u32[]{:S(2)}, u32[]{:S(2)}) collective-permute-start(bf16[2,288,128]{2,1,0:T(8,128)(2,1)S(1)} %fusion.7.refs_4_), channel_id=1, source_target_pairs={{0,24},{8,16},{16,8},{24,0},{1,25},{9,17},{17,9},{25,1},{2,26},{10... | collective-permute-start | bytes 442376 | tf_op jit(solution)/shard_map/ppermute | solution.py:403
  26.0 0.8 copy-start.4
  26.0 0.8 copy-start.7
  26.0 0.9 copy-start.8
  26.9 0.7 copy-start.9
  33.9 20.5 %all-to-all-start.1 = ((bf16[8,224,128]{2,1,0:T(8,128)(2,1)}), bf16[8,224,128]{2,1,0:T(8,128)(2,1)S(1)}, u32[]{:S(2)}, u32[]{:S(2)}) async-start(bf16[8,224,128]{2,1,0:T(8,128)(2,1)} %attention.1), calls=%async_computation.1 | async-start | bytes 917504 | tf_op jit(solution)/shard_map/all_to_all | solution.py:459
  47.9 24.7 %collective-permute-start.4 = (bf16[3,96,1792]{2,1,0:T(8,128)(2,1)S(1)}, bf16[3,96,1792]{2,1,0:T(8,128)(2,1)S(1)}, u32[]{:S(2)}, u32[]{:S(2)}) collective-permute-start(bf16[3,96,1792]{2,1,0:T(8,128)(2,1)S(1)} %collective-permute-done.3.refs_5_), channel_id=1, source_target_pairs={{0,16},{8,24},{16,0},{24,8},{1,17},{9,25},{17,1},{25,9},{2,18},{10... | collective-permute-start | bytes 3096584 | tf_op jit(solution)/shard_map/ppermute | solution.py:397
  49.3 21.7 %collective-permute-start.9 = (bf16[3,64,1792]{2,1,0:T(8,128)(2,1)}, bf16[3,64,1792]{2,1,0:T(8,128)(2,1)S(1)}, u32[]{:S(2)}, u32[]{:S(2)}) collective-permute-start(bf16[3,64,1792]{2,1,0:T(8,128)(2,1)} %copy-done.3), channel_id=1, source_target_pairs={{0,2},{1,3},{2,0},{3,1},{4,6},{5,7},{6,4},{7,5},{8,10},{9,11},{10,... | collective-permute-start | bytes 2064392 | tf_op jit(solution)/shard_map/ppermute | solution.py:393
  54.4 36.2 %copy-start = (bf16[1792,608]{0,1:T(8,128)(2,1)S(1)}, bf16[1792,608]{0,1:T(8,128)(2,1)}, u32[]{:S(2)}) copy-start(bf16[1792,608]{0,1:T(8,128)(2,1)} %param.29) | copy-start | bytes 6537220
  54.4 36.2 %copy-start.1 = (bf16[1792,608]{0,1:T(8,128)(2,1)S(1)}, bf16[1792,608]{0,1:T(8,128)(2,1)}, u32[]{:S(2)}) copy-start(bf16[1792,608]{0,1:T(8,128)(2,1)} %param.30) | copy-start | bytes 6537220
  54.4 36.2 %copy-start.2 = (bf16[608,1792]{1,0:T(8,128)(2,1)S(1)}, bf16[608,1792]{1,0:T(8,128)(2,1)}, u32[]{:S(2)}) copy-start(bf16[608,1792]{1,0:T(8,128)(2,1)} %refs_4_.5) | copy-start | bytes 6537220
  59.4 13.1 %collective-permute-start.5 = (bf16[128,1792]{1,0:T(8,128)(2,1)S(1)}, bf16[128,1792]{1,0:T(8,128)(2,1)S(1)}, u32[]{:S(2)}, u32[]{:S(2)}) collective-permute-start(bf16[128,1792]{1,0:T(8,128)(2,1)S(1)} %get-tuple-element.64.refs_0_), channel_id=1, source_target_pairs={{0,1},{1,0},{2,3},{3,2},{4,5},{5,4},{6,7},{7,6},{8,9},{9,8},{10,11... | collective-permute-start | bytes 1376264 | tf_op jit(solution)/shard_map/ppermute | solution.py:478
  59.5 13.1 %collective-permute-start.6 = (bf16[64,1792]{1,0:T(8,128)(2,1)S(1)}, bf16[64,1792]{1,0:T(8,128)(2,1)S(1)}, u32[]{:S(2)}, u32[]{:S(2)}) collective-permute-start(bf16[64,1792]{1,0:T(8,128)(2,1)S(1)} %get-tuple-element.48), channel_id=1, source_target_pairs={{0,4},{1,5},{2,6},{3,7},{4,0},{5,1},{6,2},{7,3},{8,12},{9,13},{10,... | collective-permute-start | bytes 688136 | tf_op jit(solution)/shard_map/ppermute | solution.py:475
  71.0 16.3 %collective-permute-start.10 = (bf16[3,64,1792]{2,1,0:T(8,128)(2,1)S(1)}, bf16[3,64,1792]{2,1,0:T(8,128)(2,1)S(1)}, u32[]{:S(2)}, u32[]{:S(2)}) collective-permute-start(bf16[3,64,1792]{2,1,0:T(8,128)(2,1)S(1)} %collective-permute-done.9.refs_7_), channel_id=1, source_target_pairs={{0,16},{8,24},{16,0},{24,8},{1,17},{9,25},{17,1},{25,9},{2,18},{10... | collective-permute-start | bytes 2064392 | tf_op jit(solution)/shard_map/ppermute | solution.py:397
  72.5 12.0 %collective-permute-start.8 = (bf16[64,1792]{1,0:T(8,128)(2,1)S(1)}, bf16[64,1792]{1,0:T(8,128)(2,1)S(1)}, u32[]{:S(2)}, u32[]{:S(2)}) collective-permute-start(bf16[64,1792]{1,0:T(8,128)(2,1)S(1)} %get-tuple-element.55), channel_id=1, source_target_pairs={{0,4},{1,5},{2,6},{3,7},{4,0},{5,1},{6,2},{7,3},{8,12},{9,13},{10,... | collective-permute-start | bytes 688136 | tf_op jit(solution)/shard_map/ppermute | solution.py:475
  73.7 10.8 %collective-permute-start.7 = (bf16[64,1792]{1,0:T(8,128)(2,1)S(1)}, bf16[64,1792]{1,0:T(8,128)(2,1)S(1)}, u32[]{:S(2)}, u32[]{:S(2)}) collective-permute-start(bf16[64,1792]{1,0:T(8,128)(2,1)S(1)} %collective-permute-done.6.refs_0_), channel_id=1, source_target_pairs={{0,1},{1,0},{2,3},{3,2},{4,5},{5,4},{6,7},{7,6},{8,9},{9,8},{10,11... | collective-permute-start | bytes 688136 | tf_op jit(solution)/shard_map/ppermute | solution.py:478
  84.5 6.1 %collective-permute-start.12 = (bf16[3,96,1792]{2,1,0:T(8,128)(2,1)S(1)}, bf16[3,96,1792]{2,1,0:T(8,128)(2,1)S(1)}, u32[]{:S(2)}, u32[]{:S(2)}) collective-permute-start(bf16[3,96,1792]{2,1,0:T(8,128)(2,1)S(1)} %collective-permute-done.4.refs_6_), channel_id=1, source_target_pairs={{0,8},{8,0},{16,24},{24,16},{1,9},{9,1},{17,25},{25,17},{2,10},{10... | collective-permute-start | bytes 3096584 | tf_op jit(solution)/shard_map/ppermute | solution.py:397
  84.5 6.1 %collective-permute-start.11 = (bf16[3,96,1792]{2,1,0:T(8,128)(2,1)S(1)}, bf16[3,96,1792]{2,1,0:T(8,128)(2,1)S(1)}, u32[]{:S(2)}, u32[]{:S(2)}) collective-permute-start(bf16[3,96,1792]{2,1,0:T(8,128)(2,1)S(1)} %collective-permute-done.3.refs_5_), channel_id=1, source_target_pairs={{0,8},{8,0},{16,24},{24,16},{1,9},{9,1},{17,25},{25,17},{2,10},{10... | collective-permute-start | bytes 3096584 | tf_op jit(solution)/shard_map/ppermute | solution.py:397
  87.3 2.3 %collective-permute-start.14 = (bf16[3,64,1792]{2,1,0:T(8,128)(2,1)S(1)}, bf16[3,64,1792]{2,1,0:T(8,128)(2,1)S(1)}, u32[]{:S(2)}, u32[]{:S(2)}) collective-permute-start(bf16[3,64,1792]{2,1,0:T(8,128)(2,1)S(1)} %collective-permute-done.10.refs_8_), channel_id=1, source_target_pairs={{0,8},{8,0},{16,24},{24,16},{1,9},{9,1},{17,25},{25,17},{2,10},{10... | collective-permute-start | bytes 2064392 | tf_op jit(solution)/shard_map/ppermute | solution.py:397
  87.4 3.3 %collective-permute-start.13 = (bf16[3,64,1792]{2,1,0:T(8,128)(2,1)S(1)}, bf16[3,64,1792]{2,1,0:T(8,128)(2,1)S(1)}, u32[]{:S(2)}, u32[]{:S(2)}) collective-permute-start(bf16[3,64,1792]{2,1,0:T(8,128)(2,1)S(1)} %collective-permute-done.9.refs_7_), channel_id=1, source_target_pairs={{0,8},{8,0},{16,24},{24,16},{1,9},{9,1},{17,25},{25,17},{2,10},{10... | collective-permute-start | bytes 2064392 | tf_op jit(solution)/shard_map/ppermute | solution.py:397
  87.9 7.6 %collective-permute-start.18 = (bf16[64,1792]{1,0:T(8,128)(2,1)S(1)}, bf16[64,1792]{1,0:T(8,128)(2,1)S(1)}, u32[]{:S(2)}, u32[]{:S(2)}) collective-permute-start(bf16[64,1792]{1,0:T(8,128)(2,1)S(1)} %collective-permute-done.8.refs_0_), channel_id=1, source_target_pairs={{0,1},{1,0},{2,3},{3,2},{4,5},{5,4},{6,7},{7,6},{8,9},{9,8},{10,11... | collective-permute-start | bytes 688136 | tf_op jit(solution)/shard_map/ppermute | solution.py:478
  94.3 8.0 %collective-permute-start.15 = (bf16[64,1792]{1,0:T(8,128)(2,1)S(1)}, bf16[64,1792]{1,0:T(8,128)(2,1)S(1)}, u32[]{:S(2)}, u32[]{:S(2)}) collective-permute-start(bf16[64,1792]{1,0:T(8,128)(2,1)S(1)} %get-tuple-element.63), channel_id=1, source_target_pairs={{0,1},{1,0},{2,3},{3,2},{4,5},{5,4},{6,7},{7,6},{8,9},{9,8},{10,11... | collective-permute-start | bytes 688136 | tf_op jit(solution)/shard_map/ppermute | solution.py:478
  99.1 9.5 %collective-permute-start.19 = (bf16[64,1792]{1,0:T(8,128)(2,1)S(1)}, bf16[64,1792]{1,0:T(8,128)(2,1)S(1)}, u32[]{:S(2)}, u32[]{:S(2)}) collective-permute-start(bf16[64,1792]{1,0:T(8,128)(2,1)S(1)} %get-tuple-element.72), channel_id=1, source_target_pairs={{0,1},{1,0},{2,3},{3,2},{4,5},{5,4},{6,7},{7,6},{8,9},{9,8},{10,11... | collective-permute-start | bytes 688136 | tf_op jit(solution)/shard_map/ppermute | solution.py:478
  102.3 24.4 %slice-start = ((s8[8257536]{0:T(1024)(128)(4,1)}), s8[4194304]{0:T(1024)(128)(4,1)S(1)}, s32[]{:S(2)}) async-start(s8[8257536]{0:T(1024)(128)(4,1)} %bitcast.16), calls=%async_computation.2 | async-start | bytes 8388608
  102.4 11.6 %copy-start.11 = (f32[1792]{0:T(1024)S(1)}, f32[1792]{0:T(1024)}, u32[]{:S(2)}) copy-start(f32[1792]{0:T(1024)} %param.32) | copy-start | bytes 21508
  102.4 24.3 %slice-start.1 = ((s8[8257536]{0:T(1024)(128)(4,1)}), s8[4063232]{0:T(1024)(128)(4,1)S(1)}, s32[]{:S(2)}) async-start(s8[8257536]{0:T(1024)(128)(4,1)} %bitcast.16), calls=%async_computation.3 | async-start | bytes 8126464
  102.4 11.6 %collective-permute-start.17 = (bf16[64,1792]{1,0:T(8,128)(2,1)S(1)}, bf16[64,1792]{1,0:T(8,128)(2,1)S(1)}, u32[]{:S(2)}, u32[]{:S(2)}) collective-permute-start(bf16[64,1792]{1,0:T(8,128)(2,1)S(1)} %add_parts.2), channel_id=1, source_target_pairs={{0,4},{1,5},{2,6},{3,7},{4,0},{5,1},{6,2},{7,3},{8,12},{9,13},{10,... | collective-permute-start | bytes 688136 | tf_op jit(solution)/shard_map/ppermute | solution.py:475
  107.3 11.5 %collective-permute-start.16 = (bf16[128,1792]{1,0:T(8,128)(2,1)S(1)}, bf16[128,1792]{1,0:T(8,128)(2,1)S(1)}, u32[]{:S(2)}, u32[]{:S(2)}) collective-permute-start(bf16[128,1792]{1,0:T(8,128)(2,1)S(1)} %get-tuple-element.67), channel_id=1, source_target_pairs={{0,1},{1,0},{2,3},{3,2},{4,5},{5,4},{6,7},{7,6},{8,9},{9,8},{10,11... | collective-permute-start | bytes 1376264 | tf_op jit(solution)/shard_map/ppermute | solution.py:478
  114.0 12.7 %collective-permute-start.20 = (bf16[64,1792]{1,0:T(8,128)(2,1)S(1)}, bf16[64,1792]{1,0:T(8,128)(2,1)S(1)}, u32[]{:S(2)}, u32[]{:S(2)}) collective-permute-start(bf16[64,1792]{1,0:T(8,128)(2,1)S(1)} %add_parts.3), channel_id=1, source_target_pairs={{0,4},{1,5},{2,6},{3,7},{4,0},{5,1},{6,2},{7,3},{8,12},{9,13},{10,... | collective-permute-start | bytes 688136 | tf_op jit(solution)/shard_map/ppermute | solution.py:475

commit v5 on v4

--- a/solution.py
+++ b/solution.py
@@ -18,7 +18,7 @@
 BF16 = jnp.bfloat16
 VMEM = pltpu.VMEM
 GRANT = 60 * MIB
-FRONT = 60
+FRONT = (30, 40)
 PARTS = 2
 LIGHT = pl.CostEstimate(flops=1, bytes_accessed=1, transcendentals=0)
 
@@ -83,7 +83,7 @@
 
 def attention_kernel(heads, fd, hd, turns, *refs):
     lengths_ref, flags_ref, owner_ref, conv_ref = refs[:4]
-    states, refs = refs[4 : 4 + len(turns)], refs[4 + len(turns) :]
+    states, refs = refs[4 : 5 + len(turns)], refs[5 + len(turns) :]
     x_hbm, out_hbm, turned, vconv, feats, taps, cached, out_ref, in_sems, state_sem, out_sems = refs
     blocks, rows, local = x_hbm.shape
     tokens = blocks * local
@@ -98,9 +98,10 @@
         load.start()
     slot = lax.axis_index("req")
     owner = owner_ref[slot]
-    for turn, state in zip(turns, states):
-
-        @pl.when((slot ^ turn) == owner)
+    here = [(slot ^ turn) == owner for turn in turns]
+    for chosen, state in zip(here + [((slot ^ owner) & 1) == 1], states):
+
+        @pl.when(chosen)
         def _():
             pltpu.make_async_copy(state, cached, state_sem).start()
 
@@ -163,7 +164,7 @@
 def attention(lengths, flags, owner, x, conv, states, heads, fd, hd):
     blocks, rows, local = x.shape
     tokens = blocks * local
-    turns = tuple(turn for turn, _ in states)
+    turns = tuple(turn for turn, _ in states[:-1])
     arrays = [state for _, state in states]
     return pl.pallas_call(
         functools.partial(attention_kernel, heads, fd, hd, turns),
@@ -337,10 +338,10 @@
 
 def share_of(units, sharers):
     tall = -(-units // (16 * sharers)) * 16
-    if tall < 64:
+    if tall < 96:
         return tall, [tall]
-    front = -(-tall * FRONT // 1600) * 16
-    return tall, [front, tall - front]
+    front, middle = (tall * part // 1600 * 16 for part in FRONT)
+    return tall, [front, middle, tall - front - middle]
 
 
 def first_unit(sharer, tall, units):
@@ -395,6 +396,21 @@
 
 def swapped(part, bit):
     return lax.ppermute(part, "req", [(i, i ^ bit) for i in range(lax.axis_size("req"))])
+
+
+def spread_state(packed, owners):
+    slots = lax.axis_size("req")
+    me = lax.axis_index("req")
+    held = [(0, packed)]
+    bit = slots // 2
+    while bit > 1:
+        held += [(turn ^ bit, swapped(state, bit)) for turn, state in held]
+        bit //= 2
+    wanted = owners[me ^ 1]
+    chosen = packed
+    for turn, state in held[1:]:
+        chosen = jnp.where((me ^ turn) == wanted, state, chosen)
+    return held + [(1, swapped(chosen, 1))]
 
 
 def by_xor(blocks, axis):
@@ -446,30 +462,42 @@
 
     sharers = lax.axis_size("req")
     packed = cached_state(prefix_state, prefix_norm, fd)
-    states = list(enumerate(by_xor([packed] * sharers, "req")))
-    tokens = pack(*(query_in, key_in, values_in), mlp_count)
+    states = spread_state(packed, prefix_owner)
+    share = portion(own, sharers)
+    count = len(share)
+    tokens = pack(*after((query_in, key_in, values_in), share), mlp_count)
     by_head = lax.all_to_all(tokens, "mlp", 0, 0, tiled=True)
-    share = portion(after(own, tokens), sharers)
-    count = len(share)
+
+    bits = [1 << i for i in reversed(range(sharers.bit_length() - 1))]
+
+    def pass_on(held, bit):
+        return held + [((part, flip ^ bit), swapped(piece, bit)) for (part, flip), piece in held]
+
+    def keep(held, *earlier):
+        pieces = after([piece for _, piece in held], *earlier)
+        return list(zip([key for key, _ in held], pieces))
+
     lines = [from_pair(share[0], width)]
-    by_head = after(by_head, share)
+    front = [((0, 0), piece) for piece in after(lines[0], [state for _, state in states[:-1]])]
+    for bit in bits[:-1]:
+        front = pass_on(front, bit)
+    by_head = after(by_head, [piece for _, piece in front])
+    for part in range(1, count - 1):
+        lines.append(from_pair(after(share[part], lines[-1]), width))
     attended = attention(
         lengths, old_flags, prefix_owner, by_head, conv_weight, states, heads, fd, hd
     )
     by_row = lax.all_to_all(attended, "mlp", 0, 0, tiled=True)
     by_row = by_row.reshape(mlp_count * heads * hd, by_row.shape[2])
 
-    bits = [1 << i for i in reversed(range(sharers.bit_length() - 1))]
-
-    def pass_on(held, bit):
-        return held + [((part, flip ^ bit), swapped(piece, bit)) for (part, flip), piece in held]
-
-    held = [((0, 0), piece) for piece in after(lines[0], attended)]
+    held = [
+        ((part, 0), piece) for part, line in enumerate(lines[1:], 1) for piece in after(line, attended)
+    ]
     for bit in bits[:-1]:
         held = pass_on(held, bit)
-    for part in range(1, count):
-        lines.append(from_pair(after(share[part], lines[-1], attended), width))
-    first_sum, normed, parts = project(after(by_row, lines[0]), out_weight, residual_in, mlp_gain[None])
+    if count > 1:
+        lines.append(from_pair(after(share[-1], lines[-1], attended), width))
+    first_sum, normed, parts = project(after(by_row, lines[:-1]), out_weight, residual_in, mlp_gain[None])
 
     def across(data):
         return lax.ppermute(data, "mlp", [(i, (i + mlp_count // 2) % mlp_count) for i in range(mlp_count)])
@@ -484,11 +512,11 @@
     far = [across(parts[0])]
     arrived, near = after(([piece for _, piece in held], near), far[0])
     held = list(zip([key for key, _ in held], arrived))
-    for part, piece in enumerate(lines[1:], 1):
-        rest = [((part, 0), one) for one in piece]
+    front, held = front + held, []
+    if count > 1:
+        held = [((count - 1, 0), piece) for piece in lines[-1]]
         for bit in bits[:-1]:
-            rest = pass_on(rest, bit)
-        held = held + rest
+            held = pass_on(held, bit)
     far_near = []
     for part in parts[1:]:
         sent = after(far[-1], near, *far_near)
@@ -496,8 +524,8 @@
         far_near.append([beside(sent, turn) for turn in turns])
     sent = after(far[-1], far_near)
     far_near.append([beside(sent, turn) for turn in turns])
-    pieces = [(key, after(piece, far_near[0], far[-1])) for key, piece in held]
-    pieces = pass_on(pieces, bits[-1])
+    front = pass_on(keep(front, far[0]), bits[-1])
+    pieces = front + pass_on(keep(held, far_near[0], far[-1]), bits[-1])
     back, sums, fed = [], [], []
     for mine, others in zip(far, far_near):
         fed.append(mlp(after([mine, *others], fed), own, pieces))

time: 129 us -> 129 us (level)
  waiting for transfers between devices: 68.7 us -> 60 us
  starting transfers between devices: 26.9 us -> 35.2 us
    ppermute x2 -> x3, waiting for transfers between devices: 20.4 us -> 1.36 us  [from_pair(): lax.ppermute(part, 'mlp', [(i, i ^ width) for i in range(DEPTH * width)])]
    ppermute x4, waiting for transfers between devices: 23.1 us -> 30 us  [across(): lax.ppermute(data, 'mlp', [(i, (i + mlp_count // 2) % mlp_count) for i in...]
    all_to_all x1, starting transfers between devices: 3.7 us -> 9.44 us  [shards(): by_row = lax.all_to_all(attended, 'mlp', 0, 0, tiled=True)]
    all_to_all x1, waiting for transfers between devices: 5.05 us -> 8.78 us  [shards(): by_row = lax.all_to_all(attended, 'mlp', 0, 0, tiled=True)]
    all_to_all x1, waiting for transfers between devices: 8.88 us -> 5.37 us  [shards(): by_head = lax.all_to_all(tokens, 'mlp', 0, 0, tiled=True)]
    ppermute x6 -> x11, waiting for transfers between devices: 4.31 us -> 7.78 us  [swapped(): lax.ppermute(part, 'req', [(i, i ^ bit) for i in range(lax.axis_size('req...]
    ppermute x2 -> x3, starting transfers between devices: 2 us -> 5.05 us  [from_pair(): lax.ppermute(part, 'mlp', [(i, i ^ width) for i in range(DEPTH * width)])]
    ppermute x6 -> x11, starting transfers between devices: 4 us -> 7.03 us  [swapped(): lax.ppermute(part, 'req', [(i, i ^ bit) for i in range(lax.axis_size('req...]
  transfers between devices with their start and end apart: 23 -> 26, of which waited for: 12 -> 16; matrix products, arithmetic and copies ran while one was open for 0% -> 1% of each run, Pallas kernels for 19% -> 20%
where the time goes in v5:
time: 129 us
  waiting for transfers between devices  60 us (47%)
  starting transfers between devices  35.2 us (27%)
  Pallas kernels  29.7 us (23%)
  local copies, waits for them, and re-layouts  1.54 us (1%)
  between operations  1.53 us (1%)
    ppermute x4, waiting for transfers between devices, across(): lax.ppermute(data, 'mlp', [(i, (i + mlp_count // 2) % mlp_count) for i in...  30 us
    pallas_call x3, Pallas kernels, mlp(): pl.pallas_call(functools.partial(mlp_kernel, len(xs), flips, lax.axis_siz...  12.1 us
    all_to_all x1, starting transfers between devices, shards(): by_row = lax.all_to_all(attended, 'mlp', 0, 0, tiled=True)  9.44 us
    all_to_all x1, waiting for transfers between devices, shards(): by_row = lax.all_to_all(attended, 'mlp', 0, 0, tiled=True)  8.78 us
    ppermute x11, waiting for transfers between devices, swapped(): lax.ppermute(part, 'req', [(i, i ^ bit) for i in range(lax.axis_size('req...  7.78 us
    ppermute x11, starting transfers between devices, swapped(): lax.ppermute(part, 'req', [(i, i ^ bit) for i in range(lax.axis_size('req...  7.03 us
    ppermute x6, starting transfers between devices, beside(): lax.ppermute(data, 'mlp', [(i, i - i % width + (i + turn) % width) for i...  6.94 us
    ppermute x6, waiting for transfers between devices, beside(): lax.ppermute(data, 'mlp', [(i, i - i % width + (i + turn) % width) for i...  6.67 us
  transfers between devices with their start and end apart: 26, of which 16 were waited for; matrix products, arithmetic and copies ran while one was open for 1% of the time, Pallas kernels for 20%

profile of v5, /device:TPU:0, one launch (start us, length us, event | category | flops | bytes accessed | tf_op | source)
XLA Modules:
  0.0 128.9 jit_solution(687767156826885247)
XLA Ops:
  0.6 1.8 %weight_share.1 = (bf16[3,48,1792]{2,1,0:T(8,128)(2,1)S(1)}, bf16[3,64,1792]{2,1,0:T(8,128)(2,1)S(1)}, bf16[3,48,1792]{2,1,0:T(8,128)(2,1)S(1)}) custom-call(bf16[608,1792]{1,0:T(8,128)(2,1)} %bitcast.9, bf16[608,1792]{1,0:T(8,128)(2,1)} %bitcast.13, bf16[608,1792]{1,0:T(8,128)(2,1)} %refs_4_.5), custom_call_target="tpu_custom_call" | custom-call | flops 1 | bytes 1 | tf_op jit(solution)/shard_map/weight_share/pallas_call | solution.py:377
  2.4 0.0 copy-start.11
  2.4 0.0 copy-start.7
  2.5 0.0 copy-start.12
  2.5 3.1 %collective-permute-start.2 = (bf16[3,48,1792]{2,1,0:T(8,128)(2,1)S(1)}, bf16[3,48,1792]{2,1,0:T(8,128)(2,1)S(1)}, u32[]{:S(2)}, u32[]{:S(2)}) collective-permute-start(bf16[3,48,1792]{2,1,0:T(8,128)(2,1)S(1)} %get-tuple-element.43), channel_id=1, source_target_pairs={{0,2},{1,3},{2,0},{3,1},{4,6},{5,7},{6,4},{7,5},{8,10},{9,11},{10,... | collective-permute-start | bytes 1548296 | tf_op jit(solution)/shard_map/ppermute | solution.py:394
  5.6 2.1 %pack_heads.1 = bf16[8,288,128]{2,1,0:T(8,128)(2,1)} custom-call(bf16[128,256]{1,0:T(8,128)(2,1)} %q_hbm, bf16[128,256]{1,0:T(8,128)(2,1)} %k_hbm, bf16[128,1792]{1,0:T(8,128)(2,1)} %v_hbm), custom_call_target="tpu_custom_call" | custom-call | flops 1 | bytes 1 | tf_op jit(solution)/shard_map/pack_heads/pallas_call | solution.py:66
  7.7 4.8 %all-to-all-start = ((bf16[8,288,128]{2,1,0:T(8,128)(2,1)}), bf16[8,288,128]{2,1,0:T(8,128)(2,1)S(1)}, u32[]{:S(2)}, u32[]{:S(2)}) async-start(bf16[8,288,128]{2,1,0:T(8,128)(2,1)} %pack_heads.1), calls=%async_computation | async-start | bytes 1179648 | tf_op jit(solution)/shard_map/all_to_all | solution.py:469
  12.5 0.2 copy.21
  12.8 0.0 copy-start.9
  12.8 0.1 fusion.13
  12.9 0.1 slice_maximum_fusion
  13.0 0.1 fusion.7.refs_4_
  13.1 1.6 %collective-permute-start = (bf16[2,288,128]{2,1,0:T(8,128)(2,1)S(1)}, bf16[2,288,128]{2,1,0:T(8,128)(2,1)S(1)}, u32[]{:S(2)}, u32[]{:S(2)}) collective-permute-start(bf16[2,288,128]{2,1,0:T(8,128)(2,1)S(1)} %fusion.7.refs_4_), channel_id=1, source_target_pairs={{0,16},{8,24},{16,0},{24,8},{1,17},{9,25},{17,1},{25,9},{2,18},{10... | collective-permute-start | bytes 442376 | tf_op jit(solution)/shard_map/ppermute | solution.py:398
  14.6 3.7 %collective-permute-done.refs_5_ = bf16[2,288,128]{2,1,0:T(8,128)(2,1)S(1)} collective-permute-done((bf16[2,288,128]{2,1,0:T(8,128)(2,1)S(1)}, bf16[2,288,128]{2,1,0:T(8,128)(2,1)S(1)}, u32[]{:S(2)}, u32[]{:S(2)}) %collective-permute-start) | collective-permute-done | bytes 147488 | tf_op jit(solution)/shard_map/ppermute | solution.py:398
  18.3 1.1 collective-permute-done.2.refs_5_
  19.4 2.6 %collective-permute-start.3 = (bf16[3,48,1792]{2,1,0:T(8,128)(2,1)S(1)}, bf16[3,48,1792]{2,1,0:T(8,128)(2,1)S(1)}, u32[]{:S(2)}, u32[]{:S(2)}) collective-permute-start(bf16[3,48,1792]{2,1,0:T(8,128)(2,1)S(1)} %collective-permute-done.2.refs_5_), channel_id=1, source_target_pairs={{0,16},{8,24},{16,0},{24,8},{1,17},{9,25},{17,1},{25,9},{2,18},{10... | collective-permute-start | bytes 1548296 | tf_op jit(solution)/shard_map/ppermute | solution.py:398
  22.0 0.6 dynamic_slice.3
  23.2 0.7 broadcast_select_fusion
  23.9 0.0 collective-permute-start.1
  23.9 0.0 collective-permute-start.4
  23.9 5.4 %all-to-all-done.refs_7_ = bf16[8,288,128]{2,1,0:T(8,128)(2,1)S(1)} async-done(((bf16[8,288,128]{2,1,0:T(8,128)(2,1)}), bf16[8,288,128]{2,1,0:T(8,128)(2,1)S(1)}, u32[]{:S(2)}, u32[]{:S(2)}) %all-to-all-start) | async-done | bytes 589856 | tf_op jit(solution)/shard_map/all_to_all | solution.py:469
  29.2 1.2 collective-permute-done.3.refs_6_
  30.4 0.0 collective-permute-done.1.refs_6_
  30.5 0.7 copy-done.8
  31.1 6.2 %attention.1 = bf16[8,224,128]{2,1,0:T(8,128)(2,1)} custom-call(s32[1,4]{1,0:T(1,128)} %refs_0_.1, s32[1,4]{1,0:T(1,128)} %refs_1_.1, s32[4]{0:T(128)} %refs_2_.1, f32[3,1792]{1,0:T(4,128)} %refs_3_.1, bf16[2,288,128]{2,1,0:T(8,128)(2,1)} %copy-done.5, bf16[2,288,128]{2,1,0:T(8,128)(2,1)} %copy-done.6, bf16[2,288,128]{2,1,0:T(8,128)(2,1)} %copy-done.8, ...), custom_call_target="tpu_custom_call" | custom-call | flops 1 | bytes 1 | tf_op jit(solution)/shard_map/attention/pallas_call | solution.py:169
  37.3 9.4 %all-to-all-start.1 = ((bf16[8,224,128]{2,1,0:T(8,128)(2,1)}), bf16[8,224,128]{2,1,0:T(8,128)(2,1)S(1)}, u32[]{:S(2)}, u32[]{:S(2)}) async-start(bf16[8,224,128]{2,1,0:T(8,128)(2,1)} %attention.1), calls=%async_computation.1 | async-start | bytes 917504 | tf_op jit(solution)/shard_map/all_to_all | solution.py:490
  46.8 1.6 %collective-permute-start.5 = (bf16[3,64,1792]{2,1,0:T(8,128)(2,1)S(1)}, bf16[3,64,1792]{2,1,0:T(8,128)(2,1)S(1)}, u32[]{:S(2)}, u32[]{:S(2)}) collective-permute-start(bf16[3,64,1792]{2,1,0:T(8,128)(2,1)S(1)} %collective-permute-done.4.refs_7_), channel_id=1, source_target_pairs={{0,16},{8,24},{16,0},{24,8},{1,17},{9,25},{17,1},{25,9},{2,18},{10... | collective-permute-start | bytes 2064392 | tf_op jit(solution)/shard_map/ppermute | solution.py:398
  48.3 2.0 %collective-permute-start.13 = (bf16[3,48,1792]{2,1,0:T(8,128)(2,1)}, bf16[3,48,1792]{2,1,0:T(8,128)(2,1)S(1)}, u32[]{:S(2)}, u32[]{:S(2)}) collective-permute-start(bf16[3,48,1792]{2,1,0:T(8,128)(2,1)} %copy-done.3), channel_id=1, source_target_pairs={{0,2},{1,3},{2,0},{3,1},{4,6},{5,7},{6,4},{7,5},{8,10},{9,11},{10,... | collective-permute-start | bytes 1548296 | tf_op jit(solution)/shard_map/ppermute | solution.py:394
  50.3 8.8 %all-to-all-done.1 = bf16[8,224,128]{2,1,0:T(8,128)(2,1)S(1)} async-done(((bf16[8,224,128]{2,1,0:T(8,128)(2,1)}), bf16[8,224,128]{2,1,0:T(8,128)(2,1)S(1)}, u32[]{:S(2)}, u32[]{:S(2)}) %all-to-all-start.1) | async-done | bytes 458784 | tf_op jit(solution)/shard_map/all_to_all | solution.py:490
  59.1 5.0 %out_projection.1 = (bf16[128,1792]{1,0:T(8,128)(2,1)S(1)}, bf16[128,1792]{1,0:T(8,128)(2,1)S(1)}, bf16[64,1792]{1,0:T(8,128)(2,1)S(1)}, bf16[64,1792]{1,0:T(8,128)(2,1)S(1)}) custom-call(bf16[1792,128]{1,0:T(8,128)(2,1)S(1)} %bitcast.19, bf16[1792,1792]{1,0:T(8,128)(2,1)} %w_hbm.1, bf16[128,1792]{1,0:T(8,128)(2,1)} %res_hbm.1, ...), custom_call_target="tpu_custom_call" | custom-call | flops 1 | bytes 1 | tf_op jit(solution)/shard_map/out_projection/pallas_call | solution.py:234
  64.1 0.1 collective-permute-start.6
  64.2 1.8 %collective-permute-start.7 = (bf16[64,1792]{1,0:T(8,128)(2,1)S(1)}, bf16[64,1792]{1,0:T(8,128)(2,1)S(1)}, u32[]{:S(2)}, u32[]{:S(2)}) collective-permute-start(bf16[64,1792]{1,0:T(8,128)(2,1)S(1)} %get-tuple-element.56), channel_id=1, source_target_pairs={{0,4},{1,5},{2,6},{3,7},{4,0},{5,1},{6,2},{7,3},{8,12},{9,13},{10,... | collective-permute-start | bytes 688136 | tf_op jit(solution)/shard_map/ppermute | solution.py:503
  66.0 0.3 collective-permute-done.13.refs_13_
  66.2 0.6 collective-permute-start.14
  66.8 6.8 %collective-permute-done.7.refs_0_ = bf16[64,1792]{1,0:T(8,128)(2,1)S(1)} collective-permute-done((bf16[64,1792]{1,0:T(8,128)(2,1)S(1)}, bf16[64,1792]{1,0:T(8,128)(2,1)S(1)}, u32[]{:S(2)}, u32[]{:S(2)}) %collective-permute-start.7) | collective-permute-done | bytes 229408 | tf_op jit(solution)/shard_map/ppermute | solution.py:503
  73.6 2.0 %collective-permute-start.8 = (bf16[64,1792]{1,0:T(8,128)(2,1)S(1)}, bf16[64,1792]{1,0:T(8,128)(2,1)S(1)}, u32[]{:S(2)}, u32[]{:S(2)}) collective-permute-start(bf16[64,1792]{1,0:T(8,128)(2,1)S(1)} %collective-permute-done.7.refs_0_), channel_id=1, source_target_pairs={{0,1},{1,0},{2,3},{3,2},{4,5},{5,4},{6,7},{7,6},{8,9},{9,8},{10,11... | collective-permute-start | bytes 688136 | tf_op jit(solution)/shard_map/ppermute | solution.py:506
  75.6 0.2 collective-permute-start.11
  75.8 1.3 %collective-permute-done.14.refs_14_ = bf16[3,48,1792]{2,1,0:T(8,128)(2,1)S(1)} collective-permute-done((bf16[3,48,1792]{2,1,0:T(8,128)(2,1)S(1)}, bf16[3,48,1792]{2,1,0:T(8,128)(2,1)S(1)}, u32[]{:S(2)}, u32[]{:S(2)}) %collective-permute-start.14) | collective-permute-done | bytes 516128 | tf_op jit(solution)/shard_map/ppermute | solution.py:398
  77.1 0.0 collective-permute-start.12
  77.1 10.0 %collective-permute-done.15.refs_0_ = bf16[64,1792]{1,0:T(8,128)(2,1)S(1)} collective-permute-done((bf16[64,1792]{1,0:T(8,128)(2,1)S(1)}, bf16[64,1792]{1,0:T(8,128)(2,1)S(1)}, u32[]{:S(2)}, u32[]{:S(2)}) %collective-permute-start.15) | collective-permute-done | bytes 229408 | tf_op jit(solution)/shard_map/ppermute | solution.py:503
  87.1 0.1 collective-permute-start.9
  87.2 0.4 collective-permute-start.16
  87.6 0.0 collective-permute-done.10.refs_10_
  87.6 0.1 collective-permute-start.17
  87.7 1.3 %collective-permute-done.9.refs_9_ = bf16[3,48,1792]{2,1,0:T(8,128)(2,1)S(1)} collective-permute-done((bf16[3,48,1792]{2,1,0:T(8,128)(2,1)S(1)}, bf16[3,48,1792]{2,1,0:T(8,128)(2,1)S(1)}, u32[]{:S(2)}, u32[]{:S(2)}) %collective-permute-start.9) | collective-permute-done | bytes 516128 | tf_op jit(solution)/shard_map/ppermute | solution.py:398
  89.0 1.2 collective-permute-start.21
  90.2 0.3 collective-permute-done.17.refs_16_
  90.5 3.7 %feed_forward.3 = (bf16[64,1792]{1,0:T(8,128)(2,1)S(1)}, bf16[64,1792]{1,0:T(8,128)(2,1)S(1)}) custom-call(bf16[64,1792]{1,0:T(8,128)(2,1)S(1)} %collective-permute-done.7.refs_0_, bf16[64,1792]{1,0:T(8,128)(2,1)S(1)} %collective-permute-done.8.refs_1_, bf16[608,1792]{1,0:T(8,128)(2,1)S(1)} %bitcast.10, bf16[608,1792]{1,0:T(8,128)(2,1)S(1)} %bitcast.14, ...), custom_call_target="tpu_custom_call" | custom-call | flops 1 | bytes 1 | tf_op jit(solution)/shard_map/feed_forward/pallas_call | solution.py:284
  94.1 1.2 collective-permute-start.18
  95.4 1.3 collective-permute-done.21.refs_1_
  96.6 3.7 %feed_forward.5 = (bf16[64,1792]{1,0:T(8,128)(2,1)S(1)}, bf16[64,1792]{1,0:T(8,128)(2,1)S(1)}) custom-call(bf16[64,1792]{1,0:T(8,128)(2,1)S(1)} %collective-permute-done.15.refs_0_, bf16[64,1792]{1,0:T(8,128)(2,1)S(1)} %collective-permute-done.21.refs_1_, bf16[608,1792]{1,0:T(8,128)(2,1)S(1)} %bitcast.11, bf16[608,1792]{1,0:T(8,128)(2,1)S(1)} %bitcast.15, ...), custom_call_target="tpu_custom_call" | custom-call | flops 1 | bytes 1 | tf_op jit(solution)/shard_map/feed_forward/pallas_call | solution.py:284
  100.3 1.2 collective-permute-start.22
  101.5 0.3 collective-permute-done.18.refs_1_
  101.8 0.1 add_parts.2
  101.9 0.0 copy-start.10
  101.9 0.0 slice-start.1
  101.9 0.1 collective-permute-start.20
  102.0 4.8 %feed_forward.4 = (bf16[128,1792]{1,0:T(8,128)(2,1)S(1)}, bf16[128,1792]{1,0:T(8,128)(2,1)S(1)}) custom-call(bf16[128,1792]{1,0:T(8,128)(2,1)S(1)} %get-tuple-element.74.refs_0_, bf16[128,1792]{1,0:T(8,128)(2,1)S(1)} %collective-permute-done.6.refs_1_, bf16[608,1792]{1,0:T(8,128)(2,1)S(1)} %bitcast.12, bf16[608,1792]{1,0:T(8,128)(2,1)S(1)} %bitcast.16, ...), custom_call_target="tpu_custom_call" | custom-call | flops 1 | bytes 1 | tf_op jit(solution)/shard_map/feed_forward/pallas_call | solution.py:284
  106.8 1.2 collective-permute-start.19
  108.1 0.1 add_parts.3
  108.1 5.4 %collective-permute-done.20.refs_3_ = bf16[64,1792]{1,0:T(8,128)(2,1)S(1)} collective-permute-done((bf16[64,1792]{1,0:T(8,128)(2,1)S(1)}, bf16[64,1792]{1,0:T(8,128)(2,1)S(1)}, u32[]{:S(2)}, u32[]{:S(2)}) %collective-permute-start.20) | collective-permute-done | bytes 229408 | tf_op jit(solution)/shard_map/ppermute | solution.py:503
  113.5 5.1 %collective-permute-done.19.refs_2_ = bf16[128,1792]{1,0:T(8,128)(2,1)S(1)} collective-permute-done((bf16[128,1792]{1,0:T(8,128)(2,1)S(1)}, bf16[128,1792]{1,0:T(8,128)(2,1)S(1)}, u32[]{:S(2)}, u32[]{:S(2)}) %collective-permute-start.19) | collective-permute-done | bytes 458784 | tf_op jit(solution)/shard_map/ppermute | solution.py:506
  118.6 7.9 %collective-permute-done.23.refs_4_ = bf16[64,1792]{1,0:T(8,128)(2,1)S(1)} collective-permute-done((bf16[64,1792]{1,0:T(8,128)(2,1)S(1)}, bf16[64,1792]{1,0:T(8,128)(2,1)S(1)}, u32[]{:S(2)}, u32[]{:S(2)}) %collective-permute-start.23) | collective-permute-done | bytes 229408 | tf_op jit(solution)/shard_map/ppermute | solution.py:503
  126.5 2.4 %next_projection.1 = (bf16[128,1792]{1,0:T(8,128)(2,1)}, bf16[128,2304]{1,0:T(8,128)(2,1)}) custom-call(bf16[128,1792]{1,0:T(8,128)(2,1)S(1)} %get-tuple-element.53.refs_0_, bf16[128,1792]{1,0:T(8,128)(2,1)S(1)} %get-tuple-element.76.refs_1_, bf16[128,1792]{1,0:T(8,128)(2,1)S(1)} %collective-permute-done.19.refs_2_, ...), custom_call_target="tpu_custom_call" | custom-call | flops 1 | bytes 1 | tf_op jit(solution)/shard_map/next_projection/pallas_call | solution.py:325
  (39 shorter events, 0.1 us)
Async XLA Ops:
  2.4 15.9 %copy-start.3 = (bf16[3,48,1792]{2,1,0:T(8,128)(2,1)}, bf16[3,48,1792]{2,1,0:T(8,128)(2,1)S(1)}, u32[]{:S(2)}) copy-start(bf16[3,48,1792]{2,1,0:T(8,128)(2,1)S(1)} %get-tuple-element.67) | copy-start | bytes 1548292
  2.4 10.1 %copy-start.11 = (f32[1,2,273]{2,1,0:T(2,128)S(1)}, f32[1,2,273]{2,1,0:T(2,128)}, u32[]{:S(2)}) copy-start(f32[1,2,273]{2,1,0:T(2,128)} %param.23) | copy-start | bytes 6556
  2.4 10.3 %copy-start.7 = (f32[1,2,273,112]{3,1,2,0:T(2,128)S(1)}, f32[1,2,273,112]{3,1,2,0:T(2,128)}, u32[]{:S(2)}) copy-start(f32[1,2,273,112]{3,1,2,0:T(2,128)} %param.22) | copy-start | bytes 733828
  2.5 19.5 %copy-start.12 = (s32[4]{0:T(128)S(1)}, s32[4]{0:T(128)}, u32[]{:S(2)}) copy-start(s32[4]{0:T(128)} %refs_2_.1) | copy-start | bytes 52
  2.5 16.9 %collective-permute-start.2 = (bf16[3,48,1792]{2,1,0:T(8,128)(2,1)S(1)}, bf16[3,48,1792]{2,1,0:T(8,128)(2,1)S(1)}, u32[]{:S(2)}, u32[]{:S(2)}) collective-permute-start(bf16[3,48,1792]{2,1,0:T(8,128)(2,1)S(1)} %get-tuple-element.43), channel_id=1, source_target_pairs={{0,2},{1,3},{2,0},{3,1},{4,6},{5,7},{6,4},{7,5},{8,10},{9,11},{10,... | collective-permute-start | bytes 1548296 | tf_op jit(solution)/shard_map/ppermute | solution.py:394
  7.7 21.6 %all-to-all-start = ((bf16[8,288,128]{2,1,0:T(8,128)(2,1)}), bf16[8,288,128]{2,1,0:T(8,128)(2,1)S(1)}, u32[]{:S(2)}, u32[]{:S(2)}) async-start(bf16[8,288,128]{2,1,0:T(8,128)(2,1)} %pack_heads.1), calls=%async_computation | async-start | bytes 1179648 | tf_op jit(solution)/shard_map/all_to_all | solution.py:469
  12.8 37.5 %copy-start.9 = (f32[1792]{0:T(1024)S(1)}, f32[1792]{0:T(1024)}, u32[]{:S(2)}) copy-start(f32[1792]{0:T(1024)} %param.28) | copy-start | bytes 21508
  13.1 17.4 %copy-start.5 = (bf16[2,288,128]{2,1,0:T(8,128)(2,1)}, bf16[2,288,128]{2,1,0:T(8,128)(2,1)S(1)}, u32[]{:S(2)}) copy-start(bf16[2,288,128]{2,1,0:T(8,128)(2,1)S(1)} %fusion.7.refs_4_) | copy-start | bytes 442372
  13.1 5.2 %collective-permute-start = (bf16[2,288,128]{2,1,0:T(8,128)(2,1)S(1)}, bf16[2,288,128]{2,1,0:T(8,128)(2,1)S(1)}, u32[]{:S(2)}, u32[]{:S(2)}) collective-permute-start(bf16[2,288,128]{2,1,0:T(8,128)(2,1)S(1)} %fusion.7.refs_4_), channel_id=1, source_target_pairs={{0,16},{8,24},{16,0},{24,8},{1,17},{9,25},{17,1},{25,9},{2,18},{10... | collective-permute-start | bytes 442376 | tf_op jit(solution)/shard_map/ppermute | solution.py:398
  18.3 12.2 %copy-start.6 = (bf16[2,288,128]{2,1,0:T(8,128)(2,1)}, bf16[2,288,128]{2,1,0:T(8,128)(2,1)S(1)}, u32[]{:S(2)}) copy-start(bf16[2,288,128]{2,1,0:T(8,128)(2,1)S(1)} %collective-permute-done.refs_5_) | copy-start | bytes 442372
  19.4 11.1 %collective-permute-start.3 = (bf16[3,48,1792]{2,1,0:T(8,128)(2,1)S(1)}, bf16[3,48,1792]{2,1,0:T(8,128)(2,1)S(1)}, u32[]{:S(2)}, u32[]{:S(2)}) collective-permute-start(bf16[3,48,1792]{2,1,0:T(8,128)(2,1)S(1)} %collective-permute-done.2.refs_5_), channel_id=1, source_target_pairs={{0,16},{8,24},{16,0},{24,8},{1,17},{9,25},{17,1},{25,9},{2,18},{10... | collective-permute-start | bytes 1548296 | tf_op jit(solution)/shard_map/ppermute | solution.py:398
  23.9 6.6 %collective-permute-start.1 = (bf16[2,288,128]{2,1,0:T(8,128)(2,1)}, bf16[2,288,128]{2,1,0:T(8,128)(2,1)S(1)}, u32[]{:S(2)}, u32[]{:S(2)}) collective-permute-start(bf16[2,288,128]{2,1,0:T(8,128)(2,1)} %broadcast_select_fusion), channel_id=1, source_target_pairs={{0,8},{8,0},{16,24},{24,16},{1,9},{9,1},{17,25},{25,17},{2,10},{10... | collective-permute-start | bytes 442376 | tf_op jit(solution)/shard_map/ppermute | solution.py:398
  23.9 22.9 %collective-permute-start.4 = (bf16[3,64,1792]{2,1,0:T(8,128)(2,1)S(1)}, bf16[3,64,1792]{2,1,0:T(8,128)(2,1)S(1)}, u32[]{:S(2)}, u32[]{:S(2)}) collective-permute-start(bf16[3,64,1792]{2,1,0:T(8,128)(2,1)S(1)} %get-tuple-element.51), channel_id=1, source_target_pairs={{0,2},{1,3},{2,0},{3,1},{4,6},{5,7},{6,4},{7,5},{8,10},{9,11},{10,... | collective-permute-start | bytes 2064392 | tf_op jit(solution)/shard_map/ppermute | solution.py:394
  29.2 1.2 copy-start.4
  30.5 0.7 copy-start.8
  37.3 21.8 %all-to-all-start.1 = ((bf16[8,224,128]{2,1,0:T(8,128)(2,1)}), bf16[8,224,128]{2,1,0:T(8,128)(2,1)S(1)}, u32[]{:S(2)}, u32[]{:S(2)}) async-start(bf16[8,224,128]{2,1,0:T(8,128)(2,1)} %attention.1), calls=%async_computation.1 | async-start | bytes 917504 | tf_op jit(solution)/shard_map/all_to_all | solution.py:490
  46.8 20.0 %collective-permute-start.5 = (bf16[3,64,1792]{2,1,0:T(8,128)(2,1)S(1)}, bf16[3,64,1792]{2,1,0:T(8,128)(2,1)S(1)}, u32[]{:S(2)}, u32[]{:S(2)}) collective-permute-start(bf16[3,64,1792]{2,1,0:T(8,128)(2,1)S(1)} %collective-permute-done.4.refs_7_), channel_id=1, source_target_pairs={{0,16},{8,24},{16,0},{24,8},{1,17},{9,25},{17,1},{25,9},{2,18},{10... | collective-permute-start | bytes 2064392 | tf_op jit(solution)/shard_map/ppermute | solution.py:398
  48.3 17.9 %collective-permute-start.13 = (bf16[3,48,1792]{2,1,0:T(8,128)(2,1)}, bf16[3,48,1792]{2,1,0:T(8,128)(2,1)S(1)}, u32[]{:S(2)}, u32[]{:S(2)}) collective-permute-start(bf16[3,48,1792]{2,1,0:T(8,128)(2,1)} %copy-done.3), channel_id=1, source_target_pairs={{0,2},{1,3},{2,0},{3,1},{4,6},{5,7},{6,4},{7,5},{8,10},{9,11},{10,... | collective-permute-start | bytes 1548296 | tf_op jit(solution)/shard_map/ppermute | solution.py:394
  59.1 31.4 %copy-start = (bf16[1792,608]{0,1:T(8,128)(2,1)S(1)}, bf16[1792,608]{0,1:T(8,128)(2,1)}, u32[]{:S(2)}) copy-start(bf16[1792,608]{0,1:T(8,128)(2,1)} %param.29) | copy-start | bytes 6537220
  59.1 31.4 %copy-start.1 = (bf16[1792,608]{0,1:T(8,128)(2,1)S(1)}, bf16[1792,608]{0,1:T(8,128)(2,1)}, u32[]{:S(2)}) copy-start(bf16[1792,608]{0,1:T(8,128)(2,1)} %param.30) | copy-start | bytes 6537220
  59.1 31.4 %copy-start.2 = (bf16[608,1792]{1,0:T(8,128)(2,1)S(1)}, bf16[608,1792]{1,0:T(8,128)(2,1)}, u32[]{:S(2)}) copy-start(bf16[608,1792]{1,0:T(8,128)(2,1)} %refs_4_.5) | copy-start | bytes 6537220
  64.1 9.5 %collective-permute-start.6 = (bf16[128,1792]{1,0:T(8,128)(2,1)S(1)}, bf16[128,1792]{1,0:T(8,128)(2,1)S(1)}, u32[]{:S(2)}, u32[]{:S(2)}) collective-permute-start(bf16[128,1792]{1,0:T(8,128)(2,1)S(1)} %get-tuple-element.74.refs_0_), channel_id=1, source_target_pairs={{0,1},{1,0},{2,3},{3,2},{4,5},{5,4},{6,7},{7,6},{8,9},{9,8},{10,11... | collective-permute-start | bytes 1376264 | tf_op jit(solution)/shard_map/ppermute | solution.py:506
  64.2 9.4 %collective-permute-start.7 = (bf16[64,1792]{1,0:T(8,128)(2,1)S(1)}, bf16[64,1792]{1,0:T(8,128)(2,1)S(1)}, u32[]{:S(2)}, u32[]{:S(2)}) collective-permute-start(bf16[64,1792]{1,0:T(8,128)(2,1)S(1)} %get-tuple-element.56), channel_id=1, source_target_pairs={{0,4},{1,5},{2,6},{3,7},{4,0},{5,1},{6,2},{7,3},{8,12},{9,13},{10,... | collective-permute-start | bytes 688136 | tf_op jit(solution)/shard_map/ppermute | solution.py:503
  66.2 10.9 %collective-permute-start.14 = (bf16[3,48,1792]{2,1,0:T(8,128)(2,1)S(1)}, bf16[3,48,1792]{2,1,0:T(8,128)(2,1)S(1)}, u32[]{:S(2)}, u32[]{:S(2)}) collective-permute-start(bf16[3,48,1792]{2,1,0:T(8,128)(2,1)S(1)} %collective-permute-done.13.refs_13_), channel_id=1, source_target_pairs={{0,16},{8,24},{16,0},{24,8},{1,17},{9,25},{17,1},{25,9},{2,18},{10... | collective-permute-start | bytes 1548296 | tf_op jit(solution)/shard_map/ppermute | solution.py:398
  73.6 14.0 %collective-permute-start.10 = (bf16[3,48,1792]{2,1,0:T(8,128)(2,1)S(1)}, bf16[3,48,1792]{2,1,0:T(8,128)(2,1)S(1)}, u32[]{:S(2)}, u32[]{:S(2)}) collective-permute-start(bf16[3,48,1792]{2,1,0:T(8,128)(2,1)S(1)} %collective-permute-done.3.refs_6_), channel_id=1, source_target_pairs={{0,8},{8,0},{16,24},{24,16},{1,9},{9,1},{17,25},{25,17},{2,10},{10... | collective-permute-start | bytes 1548296 | tf_op jit(solution)/shard_map/ppermute | solution.py:398
  73.6 13.5 %collective-permute-start.15 = (bf16[64,1792]{1,0:T(8,128)(2,1)S(1)}, bf16[64,1792]{1,0:T(8,128)(2,1)S(1)}, u32[]{:S(2)}, u32[]{:S(2)}) collective-permute-start(bf16[64,1792]{1,0:T(8,128)(2,1)S(1)} %get-tuple-element.69), channel_id=1, source_target_pairs={{0,4},{1,5},{2,6},{3,7},{4,0},{5,1},{6,2},{7,3},{8,12},{9,13},{10,... | collective-permute-start | bytes 688136 | tf_op jit(solution)/shard_map/ppermute | solution.py:503
  73.6 13.5 %collective-permute-start.8 = (bf16[64,1792]{1,0:T(8,128)(2,1)S(1)}, bf16[64,1792]{1,0:T(8,128)(2,1)S(1)}, u32[]{:S(2)}, u32[]{:S(2)}) collective-permute-start(bf16[64,1792]{1,0:T(8,128)(2,1)S(1)} %collective-permute-done.7.refs_0_), channel_id=1, source_target_pairs={{0,1},{1,0},{2,3},{3,2},{4,5},{5,4},{6,7},{7,6},{8,9},{9,8},{10,11... | collective-permute-start | bytes 688136 | tf_op jit(solution)/shard_map/ppermute | solution.py:506
  75.6 14.5 %collective-permute-start.11 = (bf16[3,64,1792]{2,1,0:T(8,128)(2,1)S(1)}, bf16[3,64,1792]{2,1,0:T(8,128)(2,1)S(1)}, u32[]{:S(2)}, u32[]{:S(2)}) collective-permute-start(bf16[3,64,1792]{2,1,0:T(8,128)(2,1)S(1)} %collective-permute-done.4.refs_7_), channel_id=1, source_target_pairs={{0,8},{8,0},{16,24},{24,16},{1,9},{9,1},{17,25},{25,17},{2,10},{10... | collective-permute-start | bytes 2064392 | tf_op jit(solution)/shard_map/ppermute | solution.py:398
  77.1 13.0 %collective-permute-start.12 = (bf16[3,64,1792]{2,1,0:T(8,128)(2,1)S(1)}, bf16[3,64,1792]{2,1,0:T(8,128)(2,1)S(1)}, u32[]{:S(2)}, u32[]{:S(2)}) collective-permute-start(bf16[3,64,1792]{2,1,0:T(8,128)(2,1)S(1)} %collective-permute-done.5.refs_8_), channel_id=1, source_target_pairs={{0,8},{8,0},{16,24},{24,16},{1,9},{9,1},{17,25},{25,17},{2,10},{10... | collective-permute-start | bytes 2064392 | tf_op jit(solution)/shard_map/ppermute | solution.py:398
  87.1 1.9 %collective-permute-start.9 = (bf16[3,48,1792]{2,1,0:T(8,128)(2,1)S(1)}, bf16[3,48,1792]{2,1,0:T(8,128)(2,1)S(1)}, u32[]{:S(2)}, u32[]{:S(2)}) collective-permute-start(bf16[3,48,1792]{2,1,0:T(8,128)(2,1)S(1)} %collective-permute-done.2.refs_5_), channel_id=1, source_target_pairs={{0,8},{8,0},{16,24},{24,16},{1,9},{9,1},{17,25},{25,17},{2,10},{10... | collective-permute-start | bytes 1548296 | tf_op jit(solution)/shard_map/ppermute | solution.py:398
  87.2 3.0 %collective-permute-start.16 = (bf16[3,48,1792]{2,1,0:T(8,128)(2,1)S(1)}, bf16[3,48,1792]{2,1,0:T(8,128)(2,1)S(1)}, u32[]{:S(2)}, u32[]{:S(2)}) collective-permute-start(bf16[3,48,1792]{2,1,0:T(8,128)(2,1)S(1)} %collective-permute-done.13.refs_13_), channel_id=1, source_target_pairs={{0,8},{8,0},{16,24},{24,16},{1,9},{9,1},{17,25},{25,17},{2,10},{10... | collective-permute-start | bytes 1548296 | tf_op jit(solution)/shard_map/ppermute | solution.py:398
  87.6 2.9 %collective-permute-start.17 = (bf16[3,48,1792]{2,1,0:T(8,128)(2,1)S(1)}, bf16[3,48,1792]{2,1,0:T(8,128)(2,1)S(1)}, u32[]{:S(2)}, u32[]{:S(2)}) collective-permute-start(bf16[3,48,1792]{2,1,0:T(8,128)(2,1)S(1)} %collective-permute-done.14.refs_14_), channel_id=1, source_target_pairs={{0,8},{8,0},{16,24},{24,16},{1,9},{9,1},{17,25},{25,17},{2,10},{10... | collective-permute-start | bytes 1548296 | tf_op jit(solution)/shard_map/ppermute | solution.py:398
  89.0 7.6 %collective-permute-start.21 = (bf16[64,1792]{1,0:T(8,128)(2,1)S(1)}, bf16[64,1792]{1,0:T(8,128)(2,1)S(1)}, u32[]{:S(2)}, u32[]{:S(2)}) collective-permute-start(bf16[64,1792]{1,0:T(8,128)(2,1)S(1)} %collective-permute-done.15.refs_0_), channel_id=1, source_target_pairs={{0,1},{1,0},{2,3},{3,2},{4,5},{5,4},{6,7},{7,6},{8,9},{9,8},{10,11... | collective-permute-start | bytes 688136 | tf_op jit(solution)/shard_map/ppermute | solution.py:506
  94.1 7.7 %collective-permute-start.18 = (bf16[64,1792]{1,0:T(8,128)(2,1)S(1)}, bf16[64,1792]{1,0:T(8,128)(2,1)S(1)}, u32[]{:S(2)}, u32[]{:S(2)}) collective-permute-start(bf16[64,1792]{1,0:T(8,128)(2,1)S(1)} %get-tuple-element.73), channel_id=1, source_target_pairs={{0,1},{1,0},{2,3},{3,2},{4,5},{5,4},{6,7},{7,6},{8,9},{9,8},{10,11... | collective-permute-start | bytes 688136 | tf_op jit(solution)/shard_map/ppermute | solution.py:506
  100.3 7.7 %collective-permute-start.22 = (bf16[64,1792]{1,0:T(8,128)(2,1)S(1)}, bf16[64,1792]{1,0:T(8,128)(2,1)S(1)}, u32[]{:S(2)}, u32[]{:S(2)}) collective-permute-start(bf16[64,1792]{1,0:T(8,128)(2,1)S(1)} %get-tuple-element.82), channel_id=1, source_target_pairs={{0,1},{1,0},{2,3},{3,2},{4,5},{5,4},{6,7},{7,6},{8,9},{9,8},{10,11... | collective-permute-start | bytes 688136 | tf_op jit(solution)/shard_map/ppermute | solution.py:506
  101.8 24.7 %slice-start = ((s8[8257536]{0:T(1024)(128)(4,1)}), s8[4194304]{0:T(1024)(128)(4,1)S(1)}, s32[]{:S(2)}) async-start(s8[8257536]{0:T(1024)(128)(4,1)} %bitcast.17), calls=%async_computation.2 | async-start | bytes 8388608
  101.9 11.6 %copy-start.10 = (f32[1792]{0:T(1024)S(1)}, f32[1792]{0:T(1024)}, u32[]{:S(2)}) copy-start(f32[1792]{0:T(1024)} %param.32) | copy-start | bytes 21508
  101.9 24.6 %slice-start.1 = ((s8[8257536]{0:T(1024)(128)(4,1)}), s8[4063232]{0:T(1024)(128)(4,1)S(1)}, s32[]{:S(2)}) async-start(s8[8257536]{0:T(1024)(128)(4,1)} %bitcast.17), calls=%async_computation.3 | async-start | bytes 8126464
  101.9 11.6 %collective-permute-start.20 = (bf16[64,1792]{1,0:T(8,128)(2,1)S(1)}, bf16[64,1792]{1,0:T(8,128)(2,1)S(1)}, u32[]{:S(2)}, u32[]{:S(2)}) collective-permute-start(bf16[64,1792]{1,0:T(8,128)(2,1)S(1)} %add_parts.2), channel_id=1, source_target_pairs={{0,4},{1,5},{2,6},{3,7},{4,0},{5,1},{6,2},{7,3},{8,12},{9,13},{10,... | collective-permute-start | bytes 688136 | tf_op jit(solution)/shard_map/ppermute | solution.py:503
  106.8 11.8 %collective-permute-start.19 = (bf16[128,1792]{1,0:T(8,128)(2,1)S(1)}, bf16[128,1792]{1,0:T(8,128)(2,1)S(1)}, u32[]{:S(2)}, u32[]{:S(2)}) collective-permute-start(bf16[128,1792]{1,0:T(8,128)(2,1)S(1)} %get-tuple-element.77), channel_id=1, source_target_pairs={{0,1},{1,0},{2,3},{3,2},{4,5},{5,4},{6,7},{7,6},{8,9},{9,8},{10,11... | collective-permute-start | bytes 1376264 | tf_op jit(solution)/shard_map/ppermute | solution.py:506
  113.5 13.0 %collective-permute-start.23 = (bf16[64,1792]{1,0:T(8,128)(2,1)S(1)}, bf16[64,1792]{1,0:T(8,128)(2,1)S(1)}, u32[]{:S(2)}, u32[]{:S(2)}) collective-permute-start(bf16[64,1792]{1,0:T(8,128)(2,1)S(1)} %add_parts.3), channel_id=1, source_target_pairs={{0,4},{1,5},{2,6},{3,7},{4,0},{5,1},{6,2},{7,3},{8,12},{9,13},{10,... | collective-permute-start | bytes 688136 | tf_op jit(solution)/shard_map/ppermute | solution.py:503
